TPU v7x, 256 devices: a whole 4x4x8 slice. The times are simulated.
256 devices in a mesh: img: 2 (over y_lo), slab: 128 (over y_hi, x, z, core).
Axes of the slice: x: 4, y: 4 (y_hi: 2, y_lo: 2; y = y_hi * 2 + y_lo), z: 8, core: 2. Of those that a mesh axis runs over, the one named last changes fastest.
Arguments:
- images: float32 [16384, 128, 128], P(('img', 'slab')), may hold values from 0.05 to 5
- orient: int32 [16384], P(('img', 'slab')), may hold values from 0 to 511, as said below
- sharp: float32 [16384], P(('img', 'slab')), may hold values from 0.05 to 2
- density: bfloat16 [512, 512, 512], P('slab', None, 'img'), may hold values from -6 to 6
- support: int32 [512, 512, 512], P('slab', None, 'img'), may hold values 0 or 1
Outputs:
- updated: float32 [512, 512, 512], P('slab', None, 'img')
Inputs may be any that keep to these rules, and one draw needn't show every extreme that they name: `orient`: snapshot n's centre plane lies among the 4 planes that begin at 4 times ((n // 64) mod the number of slabs); the first snapshot's centre is plane 0 and the last one's plane 512 - 1.
All inputs are finite; a program needn't handle non-finite values. No bound on the sum of `support` on one device may be relied on, other than what follows from the above.
Results may differ from a plain program's by a relative error of at most 0.0075.
The roundings to bfloat16 on the way count: a program that leaves them out, or rounds other values in their place, can miss the bound.
Values may be sent and summed in bfloat16 or wider, within the bound.
A program may use at most 64 MiB of HBM per device.

v0:
```python
import math

import jax
import jax.numpy as jnp
from jax import lax
from jax.sharding import PartitionSpec as P

GZ = 512
GY = 512
GX = 512


least_modulus = 0.5
feedback = 0.9


def with_halo(cells, sides, width):
    for axis, dim in sides:
        count = lax.axis_size(axis)
        ends = count - 1
        head = lax.slice_in_dim(cells, 0, width, axis=dim)
        tail = lax.slice_in_dim(cells, cells.shape[dim] - width, cells.shape[dim], axis=dim)
        cells = jnp.concatenate(
            [
                lax.ppermute(tail, axis, [(i, (i + 1) % count) for i in range(ends)]),
                cells,
                lax.ppermute(head, axis, [((i + 1) % count, i) for i in range(ends)]),
            ],
            axis=dim,
        )
    return cells


def dft_tables(length):
    index = jnp.arange(length, dtype=jnp.int32)
    product = index[:, None] * index[None, :] % length
    angles = product.astype(jnp.float32) * (2.0 * math.pi / length)
    factor = 1.0 / math.sqrt(length)
    return (
        (jnp.cos(angles) * factor).astype(jnp.bfloat16),
        (jnp.sin(angles) * factor).astype(jnp.bfloat16),
    )


def interpolation(cells, pixels):
    grid = jnp.arange(cells, dtype=jnp.float32)
    detector = jnp.arange(pixels, dtype=jnp.float32)
    position = (grid + 0.5) * (pixels / cells) - 0.5
    return jnp.maximum(0.0, 1.0 - jnp.abs(position[:, None] - detector[None, :]))


def band_weights(sharp, reach):
    offsets = jnp.arange(-reach, reach + 1).astype(jnp.float32)
    raw = jnp.exp(-sharp[:, None] * (offsets * offsets)[None, :])
    return raw / jnp.sum(raw, axis=1, keepdims=True)


def section(form, first, second):
    return jnp.einsum(form, first, second, preferred_element_type=jnp.float32)


def rim_add(planes, reach, depth):
    padded = with_halo(planes, (("slab", 0),), reach)
    owned = planes[reach : reach + depth]
    owned = owned.at[:reach].add(padded[:reach])
    owned = owned.at[depth - reach :].add(padded[padded.shape[0] - reach :])
    return owned


def plane_total(planes):
    return lax.psum(planes, "img")


def forward_third(real_part, imag_part, cos_x, sin_x):
    real_x = (
        section("zyx,kx->zyk", real_part, cos_x) + section("zyx,kx->zyk", imag_part, sin_x)
    ).astype(jnp.bfloat16)
    imag_x = (
        section("zyx,kx->zyk", imag_part, cos_x) - section("zyx,kx->zyk", real_part, sin_x)
    ).astype(jnp.bfloat16)
    return (real_x, imag_x)


def body(images, orient, sharp, density, support):
    depth, rows_all, width_own = density.shape
    count = images.shape[0]
    pixels = images.shape[1]
    reach = min(4, depth)
    slab_index = lax.axis_index("slab")
    image_index = lax.axis_index("img")
    scale = depth / (count * lax.axis_size("img"))
    weights = band_weights(sharp, reach)
    local = orient - slab_index * depth
    extended = depth + 2 * reach
    plane_ids = jnp.arange(extended, dtype=jnp.int32)
    offsets = jnp.arange(2 * reach + 1, dtype=jnp.int32)
    hits = plane_ids[:, None, None] == local[None, :, None] + offsets[None, None, :]
    mixing = jnp.sum(jnp.where(hits, weights[None, :, :], 0.0), axis=2)
    flat = images.reshape(count, pixels * pixels)
    planes = jnp.dot(
        mixing, flat, precision=lax.Precision.HIGHEST, preferred_element_type=jnp.float32
    )
    merged = rim_add(plane_total(planes), reach, depth)
    merged = merged.reshape(depth, pixels, pixels)
    across_y = interpolation(GY, pixels)
    across_x = interpolation(GX, pixels)
    cos_y, sin_y = dft_tables(GY)
    cos_x, sin_x = dft_tables(GX)
    cos_z, sin_z = dft_tables(GZ)
    real_y = section("jy,zyx->zjx", cos_y, density).astype(jnp.bfloat16)
    imag_y = (-section("jy,zyx->zjx", sin_y, density)).astype(jnp.bfloat16)
    columns_x = lax.dynamic_slice_in_dim(across_x, image_index * width_own, width_own, 0)
    expanded = jnp.einsum("yp,zpq->zyq", across_y, merged, precision=lax.Precision.HIGHEST)
    amplitude = jnp.sqrt(
        scale * jnp.einsum("zyq,xq->zyx", expanded, columns_x, precision=lax.Precision.HIGHEST)
    ).astype(jnp.bfloat16)
    real_y, imag_y, amplitude = (
        lax.all_to_all(real_y, "img", split_axis=1, concat_axis=2, tiled=True),
        lax.all_to_all(imag_y, "img", split_axis=1, concat_axis=2, tiled=True),
        lax.all_to_all(amplitude, "img", split_axis=1, concat_axis=2, tiled=True),
    )
    real_x, imag_x = forward_third(real_y, imag_y, cos_x, sin_x)
    real_x, imag_x, amplitude = (
        lax.all_to_all(real_x, "slab", split_axis=1, concat_axis=0, tiled=True),
        lax.all_to_all(imag_x, "slab", split_axis=1, concat_axis=0, tiled=True),
        lax.all_to_all(amplitude, "slab", split_axis=1, concat_axis=0, tiled=True),
    )
    real_z = section("kz,zyx->kyx", cos_z, real_x) + section("kz,zyx->kyx", sin_z, imag_x)
    imag_z = section("kz,zyx->kyx", cos_z, imag_x) - section("kz,zyx->kyx", sin_z, real_x)
    modulus = jnp.sqrt(real_z * real_z + imag_z * imag_z)
    factor = amplitude.astype(jnp.float32) / jnp.maximum(modulus, least_modulus)
    proj_real = (real_z * factor).astype(jnp.bfloat16)
    proj_imag = (imag_z * factor).astype(jnp.bfloat16)
    back_real = (
        section("kz,zyx->kyx", cos_z, proj_real) - section("kz,zyx->kyx", sin_z, proj_imag)
    ).astype(jnp.bfloat16)
    back_imag = (
        section("kz,zyx->kyx", cos_z, proj_imag) + section("kz,zyx->kyx", sin_z, proj_real)
    ).astype(jnp.bfloat16)
    back_real, back_imag = (
        lax.all_to_all(back_real, "slab", split_axis=0, concat_axis=1, tiled=True),
        lax.all_to_all(back_imag, "slab", split_axis=0, concat_axis=1, tiled=True),
    )
    out_real = (
        section("zyx,kx->zyk", back_real, cos_x) - section("zyx,kx->zyk", back_imag, sin_x)
    ).astype(jnp.bfloat16)
    out_imag = (
        section("zyx,kx->zyk", back_imag, cos_x) + section("zyx,kx->zyk", back_real, sin_x)
    ).astype(jnp.bfloat16)
    out_real, out_imag = (
        lax.all_to_all(out_real, "img", split_axis=2, concat_axis=1, tiled=True),
        lax.all_to_all(out_imag, "img", split_axis=2, concat_axis=1, tiled=True),
    )
    projected = section("jy,zyx->zjx", cos_y, out_real) - section("jy,zyx->zjx", sin_y, out_imag)
    previous = density.astype(jnp.float32)
    return jnp.where(support == 1, projected, previous - feedback * projected)


def solution(mesh):
    placed = (
        P(("img", "slab"), None, None),
        P(("img", "slab")),
        P(("img", "slab")),
        P("slab", None, "img"),
        P("slab", None, "img"),
    )
    return jax.shard_map(
        body, mesh=mesh, in_specs=placed, out_specs=P("slab", None, "img"), check_vma=False
    )
```

profile of v0, /device:TPU:64, one launch (start us, length us, event | category | flops | bytes accessed | tf_op | source)
XLA Modules:
  0.0 412.9 jit_solution(1750657256558146516)
XLA Ops:
  8.1 7.5 %fusion = f32[12,16384]{1,0:T(8,128)} fusion(f32[12,64]{1,0:T(8,128)S(1)} %select_reduce_fusion, f32[8,8,128,128]{3,2,1,0:T(8,128)} %bitcast.126), kind=kOutput, calls=%fused_computation | convolution fusion | flops 150994944 | bytes 4983808 | tf_op jit(solution)/shard_map/dot_general | solution.py:100
  30.8 48.9 %all-reduce.2.cloned.1.call-done = f32[12,16384]{1,0:T(8,128)} async-done(((f32[12,16384]{1,0:T(8,128)}), f32[12,16384]{1,0:T(8,128)}) %all-reduce.2.cloned.1.call-update) | async-done | bytes 786448 | tf_op jit(solution)/shard_map/psum | solution.py:71
  111.1 6.3 %fusion.40 = f32[4,256,512]{2,1,0:T(8,128)} fusion(bf16[4,256,512]{2,1,0:T(8,128)(2,1)S(1)} %copy-done.3), kind=kOutput, calls=%fused_computation.53 | convolution fusion | flops 541065216 | bytes 3145728 | tf_op jit(solution)/shard_map/zyx,kx->zyk/dot_general | solution.py:59
  119.2 6.3 %add_convert_fusion.2 = bf16[4,256,512]{2,1,0:T(8,128)(2,1)S(1)} fusion(f32[4,256,512]{2,1,0:T(8,128)} %fusion.40, bf16[4,256,512]{2,1,0:T(8,128)(2,1)S(1)} %all_to_all.131), kind=kOutput, calls=%fused_computation.16 | convolution fusion | flops 542113792 | bytes 4194304 | tf_op jit(solution)/shard_map/zyx,kx->zyk/dot_general | solution.py:59
  127.4 12.9 %all-to-all-start.2 = ((bf16[4,256,512]{2,0,1:T(4,128)(2,1)}), bf16[4,256,512]{2,0,1:T(4,128)(2,1)S(1)}, u32[]{:S(2)}, u32[]{:S(2)}) async-start(bf16[4,256,512]{2,0,1:T(4,128)(2,1)} %copy.86), calls=%async_computation.2 | async-start | bytes 2097152 | tf_op jit(solution)/shard_map/all_to_all | solution.py:124
  140.2 5.6 %fusion.36 = f32[4,256,512]{2,1,0:T(8,128)S(1)} fusion(bf16[4,256,512]{2,1,0:T(8,128)(2,1)S(1)} %copy-done.10), kind=kOutput, calls=%fused_computation.51 | convolution fusion | flops 541065216 | bytes 3145728 | tf_op jit(solution)/shard_map/zyx,kx->zyk/dot_general | solution.py:59
  153.2 17.3 %all-to-all-done.2 = bf16[4,256,512]{2,0,1:T(4,128)(2,1)S(1)} async-done(((bf16[4,256,512]{2,0,1:T(4,128)(2,1)}), bf16[4,256,512]{2,0,1:T(4,128)(2,1)S(1)}, u32[]{:S(2)}, u32[]{:S(2)}) %all-to-all-start.2) | async-done | bytes 1048608 | tf_op jit(solution)/shard_map/all_to_all | solution.py:124
  170.5 7.6 %all-to-all-start.3 = ((bf16[4,256,512]{2,0,1:T(4,128)(2,1)}), bf16[4,256,512]{2,0,1:T(4,128)(2,1)S(1)}, u32[]{:S(2)}, u32[]{:S(2)}) async-start(bf16[4,256,512]{2,0,1:T(4,128)(2,1)} %copy.88), calls=%async_computation.3 | async-start | bytes 2097152 | tf_op jit(solution)/shard_map/all_to_all | solution.py:125
  182.5 26.0 %all-to-all-done.3 = bf16[4,256,512]{2,0,1:T(4,128)(2,1)S(1)} async-done(((bf16[4,256,512]{2,0,1:T(4,128)(2,1)}), bf16[4,256,512]{2,0,1:T(4,128)(2,1)S(1)}, u32[]{:S(2)}, u32[]{:S(2)}) %all-to-all-start.3) | async-done | bytes 1048608 | tf_op jit(solution)/shard_map/all_to_all | solution.py:125
  208.6 8.1 %all-to-all-start.5 = ((bf16[4,256,512]{2,0,1:T(4,128)(2,1)}), bf16[4,256,512]{2,0,1:T(4,128)(2,1)S(1)}, u32[]{:S(2)}, u32[]{:S(2)}) async-start(bf16[4,256,512]{2,0,1:T(4,128)(2,1)} %copy.95), calls=%async_computation.5 | async-start | bytes 2097152 | tf_op jit(solution)/shard_map/all_to_all | solution.py:126
  226.5 5.7 %fusion.34 = f32[512,2,512]{2,0,1:T(8,128)} fusion(bf16[512,2,512]{2,0,1:T(8,128)(2,1)S(1)} %copy-done.12), kind=kOutput, calls=%fused_computation.50 | convolution fusion | flops 541065216 | bytes 3145728 | tf_op jit(solution)/shard_map/kz,zyx->kyx/dot_general | solution.py:59
  232.1 5.7 %convolution_add_fusion = f32[512,2,512]{2,0,1:T(8,128)} fusion(f32[512,2,512]{2,0,1:T(8,128)S(1)} %fusion.38, bf16[512,2,512]{2,0,1:T(8,128)(2,1)S(1)} %copy-done.12), kind=kOutput, calls=%fused_computation.19 | convolution fusion | flops 541589504 | bytes 5242880 | tf_op jit(solution)/shard_map/kz,zyx->kyx/dot_general | solution.py:59
  237.8 9.2 %all-to-all-done.5 = bf16[4,256,512]{2,0,1:T(4,128)(2,1)S(1)} async-done(((bf16[4,256,512]{2,0,1:T(4,128)(2,1)}), bf16[4,256,512]{2,0,1:T(4,128)(2,1)S(1)}, u32[]{:S(2)}, u32[]{:S(2)}) %all-to-all-start.5) | async-done | bytes 1048608 | tf_op jit(solution)/shard_map/all_to_all | solution.py:126
  249.7 7.2 %multiply_convert_fusion = (bf16[512,2,512]{2,0,1:T(8,128)(2,1)S(1)}, bf16[512,2,512]{2,0,1:T(8,128)(2,1)S(1)}) fusion(f32[512,2,512]{2,0,1:T(8,128)} %reshape.136, f32[512,2,512]{2,0,1:T(8,128)} %convolution_add_fusion, f32[512,2,512]{2,0,1:T(8,128)} %fusion.34, bf16[512,2,512]{2,0,1:T(8,128)(2,1)S(1)} %copy-done.5), kind=kOutput, calls=%fused_computation.11 | convolution fusion | flops 546308096 | bytes 9437184 | tf_op jit(solution)/shard_map/kz,zyx->kyx/dot_general | solution.py:59
  268.3 7.9 %all-to-all-start.7 = ((bf16[512,2,512]{2,1,0:T(2,128)(2,1)}), bf16[512,2,512]{2,1,0:T(2,128)(2,1)S(1)}, u32[]{:S(2)}, u32[]{:S(2)}) async-start(bf16[512,2,512]{2,1,0:T(2,128)(2,1)} %copy.99), calls=%async_computation.7 | async-start | bytes 2097152 | tf_op jit(solution)/shard_map/all_to_all | solution.py:142
  287.6 19.0 %all-to-all-done.7 = bf16[512,2,512]{2,1,0:T(2,128)(2,1)S(1)} async-done(((bf16[512,2,512]{2,1,0:T(2,128)(2,1)}), bf16[512,2,512]{2,1,0:T(2,128)(2,1)S(1)}, u32[]{:S(2)}, u32[]{:S(2)}) %all-to-all-start.7) | async-done | bytes 1048608 | tf_op jit(solution)/shard_map/all_to_all | solution.py:142
  306.6 8.1 %all-to-all-start.6 = ((bf16[512,2,512]{2,1,0:T(2,128)(2,1)}), bf16[512,2,512]{2,1,0:T(2,128)(2,1)S(1)}, u32[]{:S(2)}, u32[]{:S(2)}) async-start(bf16[512,2,512]{2,1,0:T(2,128)(2,1)} %copy.97), calls=%async_computation.6 | async-start | bytes 2097152 | tf_op jit(solution)/shard_map/all_to_all | solution.py:141
  315.9 6.3 %fusion.24 = f32[4,256,512]{2,1,0:T(8,128)} fusion(bf16[4,256,512]{2,1,0:T(8,128)(2,1)S(1)} %all_to_all.152), kind=kOutput, calls=%fused_computation.45 | convolution fusion | flops 541065216 | bytes 3145728 | tf_op jit(solution)/shard_map/zyx,kx->zyk/dot_general | solution.py:59
  322.2 22.8 %all-to-all-done.6 = bf16[512,2,512]{2,1,0:T(2,128)(2,1)S(1)} async-done(((bf16[512,2,512]{2,1,0:T(2,128)(2,1)}), bf16[512,2,512]{2,1,0:T(2,128)(2,1)S(1)}, u32[]{:S(2)}, u32[]{:S(2)}) %all-to-all-start.6) | async-done | bytes 1048608 | tf_op jit(solution)/shard_map/all_to_all | solution.py:141
  346.2 5.9 %add_convert_fusion = bf16[4,256,512]{2,1,0:T(8,128)(2,1)S(1)} fusion(f32[4,256,512]{2,1,0:T(8,128)} %fusion.24, bf16[4,256,512]{2,1,0:T(8,128)(2,1)S(1)} %all_to_all.148), kind=kOutput, calls=%fused_computation.7 | convolution fusion | flops 542113792 | bytes 4194304 | tf_op jit(solution)/shard_map/zyx,kx->zyk/dot_general | solution.py:59
  357.1 5.6 %fusion.30 = f32[4,256,512]{2,1,0:T(8,128)S(1)} fusion(bf16[4,256,512]{2,1,0:T(8,128)(2,1)S(1)} %all_to_all.148), kind=kOutput, calls=%fused_computation.48 | convolution fusion | flops 541065216 | bytes 3145728 | tf_op jit(solution)/shard_map/zyx,kx->zyk/dot_general | solution.py:59
  382.6 7.0 %all-to-all-done.8 = bf16[4,256,512]{1,0,2:T(4,128)(2,1)S(1)} async-done(((bf16[4,256,512]{1,0,2:T(4,128)(2,1)}), bf16[4,256,512]{1,0,2:T(4,128)(2,1)S(1)}, u32[]{:S(2)}, u32[]{:S(2)}) %all-to-all-start.8) | async-done | bytes 1048608 | tf_op jit(solution)/shard_map/all_to_all | solution.py:151
  391.4 5.6 %fusion.26 = f32[4,256,512]{2,1,0:T(8,128)S(1)} fusion(bf16[4,512,256]{1,2,0:T(8,128)(2,1)S(1)} %all_to_all.156), kind=kOutput, calls=%fused_computation.46 | convolution fusion | flops 541065216 | bytes 3145728 | tf_op jit(solution)/shard_map/jy,zyx->zjx/dot_general | solution.py:59
  397.1 7.0 %bitcast_select_fusion = f32[4,512,256]{1,2,0:T(8,128)S(1)} fusion(bf16[4,512,256]{1,2,0:T(8,128)(2,1)S(1)} %copy-done.8, f32[4,256,512]{2,1,0:T(8,128)S(1)} %fusion.26, s32[4,512,256]{1,2,0:T(8,128)S(1)} %copy-done, bf16[4,512,256]{1,2,0:T(8,128)(2,1)S(1)} %copy-done.11), kind=kOutput, calls=%fused_computation.4 | convolution fusion | flops 544210944 | bytes 8388608 | tf_op jit(solution)/shard_map/jy,zyx->zjx/dot_general | solution.py:59
  (101 shorter events, 129.0 us)
Async XLA Ops:
  6.5 73.2 %all-reduce.2.cloned.1.call-start = ((), (), s32[]{:S(2)}) async-start(), calls=%async_computation.10 | async-start | bytes 2097152 | tf_op jit(solution)/shard_map/psum | solution.py:71
  8.1 7.5 %copy-start.1 = (bf16[4,512,256]{2,1,0:T(8,128)(2,1)S(1)}, bf16[4,512,256]{2,1,0:T(8,128)(2,1)}, u32[]{:S(2)}) copy-start(bf16[4,512,256]{2,1,0:T(8,128)(2,1)} %param.16) | copy-start | bytes 3145732
  22.3 67.0 %all-to-all-start = ((bf16[4,512,256]{2,0,1:T(4,128)(2,1)}), bf16[4,512,256]{2,0,1:T(4,128)(2,1)S(1)}, u32[]{:S(2)}, u32[]{:S(2)}) async-start(bf16[4,512,256]{2,0,1:T(4,128)(2,1)} %copy.82), calls=%async_computation | async-start | bytes 2097152 | tf_op jit(solution)/shard_map/all_to_all | solution.py:118
  81.8 14.2 %collective-permute-start = (f32[4,16384]{1,0:T(4,128)}, f32[4,16384]{1,0:T(4,128)}, u32[]{:S(2)}, u32[]{:S(2)}) collective-permute-start(f32[4,16384]{1,0:T(4,128)} %get-tuple-element.47), channel_id=1, source_target_pairs={{0,1},{1,2},{2,3},{3,4},{4,5},{5,6},{6,7},{7,8},{8,9},{9,10},{10,1... | collective-permute-start | bytes 786440 | tf_op jit(solution)/shard_map/ppermute | solution.py:25
  83.7 12.3 %collective-permute-start.1 = (f32[4,16384]{1,0:T(4,128)}, f32[4,16384]{1,0:T(4,128)}, u32[]{:S(2)}, u32[]{:S(2)}) collective-permute-start(f32[4,16384]{1,0:T(4,128)} %get-tuple-element.48), channel_id=1, source_target_pairs={{1,0},{2,1},{3,2},{4,3},{5,4},{6,5},{7,6},{8,7},{9,8},{10,9},{11,1... | collective-permute-start | bytes 786440 | tf_op jit(solution)/shard_map/ppermute | solution.py:27
  89.3 18.1 %all-to-all-start.1 = ((bf16[4,512,256]{2,0,1:T(4,128)(2,1)}), bf16[4,512,256]{2,0,1:T(4,128)(2,1)S(1)}, u32[]{:S(2)}, u32[]{:S(2)}) async-start(bf16[4,512,256]{2,0,1:T(4,128)(2,1)} %copy.84), calls=%async_computation.1 | async-start | bytes 2097152 | tf_op jit(solution)/shard_map/all_to_all | solution.py:119
  100.9 10.2 %copy-start.3 = (bf16[4,256,512]{2,1,0:T(8,128)(2,1)S(1)}, bf16[4,256,512]{2,1,0:T(8,128)(2,1)}, u32[]{:S(2)}) copy-start(bf16[4,256,512]{2,1,0:T(8,128)(2,1)} %all_to_all.127) | copy-start | bytes 3145732
  107.4 20.0 %all-to-all-start.4 = ((bf16[4,512,256]{2,0,1:T(4,128)(2,1)}), bf16[4,512,256]{2,0,1:T(4,128)(2,1)S(1)}, u32[]{:S(2)}, u32[]{:S(2)}) async-start(bf16[4,512,256]{2,0,1:T(4,128)(2,1)} %copy.92), calls=%async_computation.4 | async-start | bytes 2097152 | tf_op jit(solution)/shard_map/all_to_all | solution.py:120
  119.2 6.3 %copy-start.9 = (bf16[4,256,512]{2,1,0:T(8,128)(2,1)}, bf16[4,256,512]{2,1,0:T(8,128)(2,1)S(1)}, u32[]{:S(2)}) copy-start(bf16[4,256,512]{2,1,0:T(8,128)(2,1)S(1)} %all_to_all.131) | copy-start | bytes 3145732
  127.3 12.9 %copy-start.10 = (bf16[4,256,512]{2,1,0:T(8,128)(2,1)S(1)}, bf16[4,256,512]{2,1,0:T(8,128)(2,1)}, u32[]{:S(2)}) copy-start(bf16[4,256,512]{2,1,0:T(8,128)(2,1)} %copy-done.9) | copy-start | bytes 3145732
  127.4 43.2 %all-to-all-start.2 = ((bf16[4,256,512]{2,0,1:T(4,128)(2,1)}), bf16[4,256,512]{2,0,1:T(4,128)(2,1)S(1)}, u32[]{:S(2)}, u32[]{:S(2)}) async-start(bf16[4,256,512]{2,0,1:T(4,128)(2,1)} %copy.86), calls=%async_computation.2 | async-start | bytes 2097152 | tf_op jit(solution)/shard_map/all_to_all | solution.py:124
  140.2 5.7 %copy-start.4 = (bf16[4,256,512]{2,1,0:T(8,128)(2,1)S(1)}, bf16[4,256,512]{2,1,0:T(8,128)(2,1)}, u32[]{:S(2)}) copy-start(bf16[4,256,512]{2,1,0:T(8,128)(2,1)} %all_to_all.127) | copy-start | bytes 3145732
  170.5 38.1 %all-to-all-start.3 = ((bf16[4,256,512]{2,0,1:T(4,128)(2,1)}), bf16[4,256,512]{2,0,1:T(4,128)(2,1)S(1)}, u32[]{:S(2)}, u32[]{:S(2)}) async-start(bf16[4,256,512]{2,0,1:T(4,128)(2,1)} %copy.88), calls=%async_computation.3 | async-start | bytes 2097152 | tf_op jit(solution)/shard_map/all_to_all | solution.py:125
  208.6 38.4 %all-to-all-start.5 = ((bf16[4,256,512]{2,0,1:T(4,128)(2,1)}), bf16[4,256,512]{2,0,1:T(4,128)(2,1)S(1)}, u32[]{:S(2)}, u32[]{:S(2)}) async-start(bf16[4,256,512]{2,0,1:T(4,128)(2,1)} %copy.95), calls=%async_computation.5 | async-start | bytes 2097152 | tf_op jit(solution)/shard_map/all_to_all | solution.py:126
  266.3 10.0 %copy-start.14 = (bf16[512,2,512]{2,0,1:T(8,128)(2,1)S(1)}, bf16[512,2,512]{2,0,1:T(8,128)(2,1)}, u32[]{:S(2)}) copy-start(bf16[512,2,512]{2,0,1:T(8,128)(2,1)} %copy-done.13) | copy-start | bytes 3145732
  268.3 38.2 %all-to-all-start.7 = ((bf16[512,2,512]{2,1,0:T(2,128)(2,1)}), bf16[512,2,512]{2,1,0:T(2,128)(2,1)S(1)}, u32[]{:S(2)}, u32[]{:S(2)}) async-start(bf16[512,2,512]{2,1,0:T(2,128)(2,1)} %copy.99), calls=%async_computation.7 | async-start | bytes 2097152 | tf_op jit(solution)/shard_map/all_to_all | solution.py:142
  306.6 38.4 %all-to-all-start.6 = ((bf16[512,2,512]{2,1,0:T(2,128)(2,1)}), bf16[512,2,512]{2,1,0:T(2,128)(2,1)S(1)}, u32[]{:S(2)}, u32[]{:S(2)}) async-start(bf16[512,2,512]{2,1,0:T(2,128)(2,1)} %copy.97), calls=%async_computation.6 | async-start | bytes 2097152 | tf_op jit(solution)/shard_map/all_to_all | solution.py:141
  315.9 6.3 %copy-start.6 = (bf16[4,256,512]{2,1,0:T(8,128)(2,1)}, bf16[4,256,512]{2,1,0:T(8,128)(2,1)S(1)}, u32[]{:S(2)}) copy-start(bf16[4,256,512]{2,1,0:T(8,128)(2,1)S(1)} %all_to_all.152) | copy-start | bytes 3145732
  353.5 18.5 %all-to-all-start.9 = ((bf16[4,256,512]{1,0,2:T(4,128)(2,1)}), bf16[4,256,512]{1,0,2:T(4,128)(2,1)S(1)}, u32[]{:S(2)}, u32[]{:S(2)}) async-start(bf16[4,256,512]{1,0,2:T(4,128)(2,1)} %copy.103), calls=%async_computation.9 | async-start | bytes 2097152 | tf_op jit(solution)/shard_map/all_to_all | solution.py:152
  368.4 7.2 %copy-start.2 = (bf16[4,512,256]{2,1,0:T(8,128)(2,1)S(1)}, bf16[4,512,256]{2,1,0:T(8,128)(2,1)}, u32[]{:S(2)}) copy-start(bf16[4,512,256]{2,1,0:T(8,128)(2,1)} %param.16) | copy-start | bytes 3145732
  372.0 17.6 %all-to-all-start.8 = ((bf16[4,256,512]{1,0,2:T(4,128)(2,1)}), bf16[4,256,512]{1,0,2:T(4,128)(2,1)S(1)}, u32[]{:S(2)}, u32[]{:S(2)}) async-start(bf16[4,256,512]{1,0,2:T(4,128)(2,1)} %copy.101), calls=%async_computation.8 | async-start | bytes 2097152 | tf_op jit(solution)/shard_map/all_to_all | solution.py:151
  391.4 5.7 %copy-start = (s32[4,512,256]{1,2,0:T(8,128)S(1)}, s32[4,512,256]{1,2,0:T(8,128)}, u32[]{:S(2)}) copy-start(s32[4,512,256]{1,2,0:T(8,128)} %copy.81) | copy-start | bytes 6291460
  391.4 5.7 %copy-start.8 = (bf16[4,512,256]{1,2,0:T(8,128)(2,1)S(1)}, bf16[4,512,256]{1,2,0:T(8,128)(2,1)}, u32[]{:S(2)}) copy-start(bf16[4,512,256]{1,2,0:T(8,128)(2,1)} %copy.105) | copy-start | bytes 3145732
  391.4 5.7 %copy-start.11 = (bf16[4,512,256]{1,2,0:T(8,128)(2,1)S(1)}, bf16[4,512,256]{1,2,0:T(8,128)(2,1)}, u32[]{:S(2)}) copy-start(bf16[4,512,256]{1,2,0:T(8,128)(2,1)} %all_to_all.160) | copy-start | bytes 3145732
  (4 other events, 15.9 us)
Sparse Core Ops, SparseCore 0:
  15.7 63.9 all-reduce.1
where the time goes:
time: 421 us; the launch traced here: 413 us
  waiting for transfers between devices  157 us (37%)
  matrix products  122 us (29%)
  starting transfers between devices  68.9 us (16%)
  local copies, waits for them, and re-layouts  47.1 us (11%)
  between operations  14.1 us (3%)
    dot_general x20, matrix products, section(): return jnp.einsum(form, first, second, preferred_element_type=jnp.float32)  111 us
    psum x1, waiting for transfers between devices, plane_total(): return lax.psum(planes, 'img')  48.9 us
    all_to_all x1, waiting for transfers between devices, body(): lax.all_to_all(imag_x, 'slab', split_axis=1, concat_axis=0, tiled=True)  26 us
    all_to_all x1, waiting for transfers between devices, body(): lax.all_to_all(back_real, 'slab', split_axis=0, concat_axis=1, tiled=True)  22.8 us
    all_to_all x1, waiting for transfers between devices, body(): lax.all_to_all(back_imag, 'slab', split_axis=0, concat_axis=1, tiled=True)  19 us
    all_to_all x1, waiting for transfers between devices, body(): lax.all_to_all(real_x, 'slab', split_axis=1, concat_axis=0, tiled=True)  17.3 us
    all_to_all x1, starting transfers between devices, body(): lax.all_to_all(real_x, 'slab', split_axis=1, concat_axis=0, tiled=True)  12.9 us
    all_to_all x1, waiting for transfers between devices, body(): lax.all_to_all(amplitude, 'slab', split_axis=1, concat_axis=0, tiled=True)  9.17 us
  transfers between devices with their start and end apart: 13, of which 9 were waited for; matrix products, arithmetic and copies ran while one was open for 27% of the time, Pallas kernels for 0%

commit v1 on v0

v1 whole, which is shorter than its diff:
```python
import math

import jax
import jax.numpy as jnp
import ml_dtypes
import numpy as np
from jax import lax
from jax.sharding import PartitionSpec as P

GZ = 512
GY = 512
GX = 512
PIX = 128
REACH = 4

least_modulus = 0.5
feedback = 0.9


def dft_tables(length):
    index = np.arange(length, dtype=np.int64)
    product = (index[:, None] * index[None, :]) % length
    angles = product.astype(np.float32) * np.float32(2.0 * math.pi / length)
    factor = np.float32(1.0 / math.sqrt(length))
    return (
        (np.cos(angles) * factor).astype(ml_dtypes.bfloat16),
        (np.sin(angles) * factor).astype(ml_dtypes.bfloat16),
    )


def interpolation(cells, pixels):
    grid = np.arange(cells, dtype=np.float32)
    detector = np.arange(pixels, dtype=np.float32)
    position = (grid + np.float32(0.5)) * np.float32(pixels / cells) - np.float32(0.5)
    return np.maximum(
        np.float32(0.0), np.float32(1.0) - np.abs(position[:, None] - detector[None, :])
    )


def bf(table):
    return np.asarray(table).astype(ml_dtypes.bfloat16)


COS, SIN = dft_tables(GY)
HALF = GY // 2
FORWARD_Y = np.stack([COS[:HALF], np.concatenate([COS[HALF : HALF + 1], -SIN[1:HALF]])])
_two = 2.0 * COS[:, :HALF].astype(np.float32)
_two[:, 0] = COS[:, 0]
_sin = -2.0 * SIN[:, :HALF].astype(np.float32)
_sin[:, 0] = COS[:, HALF]
BACK_Y = np.stack([bf(_two), bf(_sin)])
COS_X = np.concatenate([COS, SIN], axis=0)
FORWARD_X = np.concatenate(
    [np.concatenate([COS, -SIN], axis=1), np.concatenate([SIN, COS], axis=1)], axis=0
)
BACK_X = np.concatenate(
    [np.concatenate([COS, SIN], axis=1), np.concatenate([-SIN, COS], axis=1)], axis=0
)
_across = interpolation(GY, PIX)
_mirror = (-np.arange(GY)) % GY
_partner = _mirror[:HALF].copy()
_partner[0] = HALF
ACROSS_Y = bf(np.stack([_across[:HALF], _across[_partner]]))
ACROSS_X = bf(_across)
ACROSS_X_MIRROR = bf(_across[_mirror])
MIRROR = bf(np.eye(GZ, dtype=np.float32)[_mirror])


def band_weights(sharp, reach):
    offsets = jnp.arange(-reach, reach + 1).astype(jnp.float32)
    raw = jnp.exp(-sharp[:, None] * (offsets * offsets)[None, :])
    return raw / jnp.sum(raw, axis=1, keepdims=True)


def dot(first, second):
    return jnp.dot(first, second, preferred_element_type=jnp.float32)


def own_planes(planes, images, slabs, image_index, depth):
    axes = ("img", "slab")
    share = depth // images
    total = lax.dynamic_slice_in_dim(planes, depth + image_index * share, share, 0)
    for shift in (-1, 0, 1):
        for turn in range(images):
            if shift == 0 and turn == 0:
                continue
            target = (image_index + turn) % images
            piece = lax.dynamic_slice_in_dim(
                planes, (1 + shift) * depth + target * share, share, 0
            )
            pairs = [
                (i * slabs + s, (i + turn) % images * slabs + s + shift)
                for i in range(images)
                for s in range(slabs)
                if 0 <= s + shift < slabs
            ]
            total = total + lax.ppermute(piece, axes, pairs)
    return total


def amplitudes(rows, across, scale):
    return jnp.sqrt(scale * dot(rows, across.T)).astype(jnp.bfloat16).astype(jnp.float32)


def project(real_x, imag_x, amplitude):
    real_z = dot(COS, real_x) + dot(SIN, imag_x)
    imag_z = dot(COS, imag_x) - dot(SIN, real_x)
    modulus = jnp.sqrt(real_z * real_z + imag_z * imag_z)
    factor = amplitude / jnp.maximum(modulus, least_modulus)
    proj_real = (real_z * factor).astype(jnp.bfloat16)
    proj_imag = (imag_z * factor).astype(jnp.bfloat16)
    back_real = (dot(COS, proj_real) - dot(SIN, proj_imag)).astype(jnp.bfloat16)
    back_imag = (dot(COS, proj_imag) + dot(SIN, proj_real)).astype(jnp.bfloat16)
    return back_real, back_imag


def body(images, orient, sharp, density, support):
    depth, rows_all, width_own = density.shape
    count = images.shape[0]
    image_count = lax.axis_size("img")
    slabs = lax.axis_size("slab")
    devices = image_count * slabs
    slab_index = lax.axis_index("slab")
    image_index = lax.axis_index("img")
    axes = ("img", "slab")
    scale = depth / (count * image_count)

    weights = band_weights(sharp, REACH)
    local = orient - slab_index * depth
    plane_ids = jnp.arange(depth + 2 * REACH, dtype=jnp.int32)
    offsets = jnp.arange(2 * REACH + 1, dtype=jnp.int32)
    hits = plane_ids[:, None, None] == local[None, :, None] + offsets[None, None, :]
    mixing = jnp.sum(jnp.where(hits, weights[None, :, :], 0.0), axis=2)
    planes = jnp.dot(
        mixing,
        images.reshape(count, PIX * PIX),
        precision=lax.Precision.HIGH,
        preferred_element_type=jnp.float32,
    )
    mine = own_planes(planes, image_count, slabs, image_index, depth)
    share = mine.shape[0]
    mine = mine.reshape(share, PIX, PIX).astype(jnp.bfloat16)
    expanded = jnp.einsum(
        "ejp,zpq->jezq", ACROSS_Y, mine, preferred_element_type=jnp.float32
    ).astype(jnp.bfloat16)
    expanded = lax.all_to_all(
        expanded.reshape(devices, 2 * share, PIX), axes, split_axis=0, concat_axis=0, tiled=True
    )
    expanded = (
        expanded.reshape(image_count, slabs, 2, share, PIX)
        .transpose(2, 1, 0, 3, 4)
        .reshape(2, GZ, PIX)
    )

    spectrum = jnp.einsum(
        "cjy,zyx->jczx", FORWARD_Y, density, preferred_element_type=jnp.float32
    ).astype(jnp.bfloat16)
    lines = lax.all_to_all(
        spectrum.reshape(devices, 2 * depth, width_own), axes, split_axis=0, concat_axis=0, tiled=True
    )
    lines = (
        lines.reshape(image_count, slabs, 2, depth, width_own)
        .transpose(1, 3, 2, 0, 4)
        .reshape(GZ, 2 * GX)
    )
    first, second = expanded[0], expanded[1]
    first_mirror = dot(MIRROR, first).astype(jnp.bfloat16)
    second_mirror = dot(MIRROR, second).astype(jnp.bfloat16)

    def usual(lines, first, second, first_mirror, second_mirror):
        both = dot(lines, FORWARD_X).astype(jnp.bfloat16)
        amplitude = 0.5 * (
            amplitudes(first, ACROSS_X, scale) + amplitudes(second_mirror, ACROSS_X_MIRROR, scale)
        )
        back_real, back_imag = project(both[:, :GX], both[:, GX:], amplitude)
        return dot(jnp.concatenate([back_real, back_imag], axis=1), BACK_X).astype(jnp.bfloat16)

    def real_rows(lines, first, second, first_mirror, second_mirror):
        out = []
        for part, near, far in ((0, first, first_mirror), (1, second, second_mirror)):
            line = lines[:, part * GX : (part + 1) * GX]
            both = dot(line, FORWARD_X[:GX]).astype(jnp.bfloat16)
            amplitude = 0.5 * (
                amplitudes(near, ACROSS_X, scale) + amplitudes(far, ACROSS_X_MIRROR, scale)
            )
            back_real, back_imag = project(both[:, :GX], both[:, GX:], amplitude)
            out.append(
                dot(jnp.concatenate([back_real, back_imag], axis=1), BACK_X[:, :GX]).astype(
                    jnp.bfloat16
                )
            )
        return jnp.concatenate(out, axis=1)

    special = jnp.logical_and(slab_index == 0, image_index == 0)
    out = lax.cond(
        special, real_rows, usual, lines, first, second, first_mirror, second_mirror
    )
    out = (
        out.reshape(slabs, depth, 2, image_count, width_own)
        .transpose(3, 0, 2, 1, 4)
        .reshape(devices, 2 * depth, width_own)
    )
    out = lax.all_to_all(out, axes, split_axis=0, concat_axis=0, tiled=True)
    out = out.reshape(devices, 2, depth, width_own)
    projected = jnp.einsum("cyj,jczx->zyx", BACK_Y, out, preferred_element_type=jnp.float32)
    previous = density.astype(jnp.float32)
    return jnp.where(support == 1, projected, previous - feedback * projected)


def solution(mesh):
    placed = (
        P(("img", "slab"), None, None),
        P(("img", "slab")),
        P(("img", "slab")),
        P("slab", None, "img"),
        P("slab", None, "img"),
    )
    return jax.shard_map(
        body, mesh=mesh, in_specs=placed, out_specs=P("slab", None, "img"), check_vma=False
    )
```

time: 421 us -> 173 us (0.41)
  the two profiles are of different devices: /device:TPU:64 before, /device:TPU:1 now
where the time goes in v1:
time: 173 us
  waiting for transfers between devices  75.2 us (43%)
  starting transfers between devices  49.6 us (29%)
  matrix products  27 us (16%)
  local copies, waits for them, and re-layouts  18.1 us (10%)
    all_to_all x1, waiting for transfers between devices, body(): lax.all_to_all(spectrum.reshape(devices, 2 * depth, width_own), axes, spl...  30 us
    all_to_all x1, waiting for transfers between devices, body(): out = lax.all_to_all(out, axes, split_axis=0, concat_axis=0, tiled=True)  27.8 us
    dot_general x13, matrix products, dot(): return jnp.dot(first, second, preferred_element_type=jnp.float32)  18.4 us
    all_to_all x1, starting transfers between devices, body(): lax.all_to_all(expanded.reshape(devices, 2 * share, PIX), axes, split_axi...  15.4 us
    all_to_all x1, starting transfers between devices, body(): out = lax.all_to_all(out, axes, split_axis=0, concat_axis=0, tiled=True)  14.4 us
    ppermute x5, starting transfers between devices, own_planes(): total = total + lax.ppermute(piece, axes, pairs)  14.3 us
    all_to_all x1, waiting for transfers between devices, body(): lax.all_to_all(expanded.reshape(devices, 2 * share, PIX), axes, split_axi...  13.1 us
    all_to_all x1, starting transfers between devices, body(): lax.all_to_all(spectrum.reshape(devices, 2 * depth, width_own), axes, spl...  5.46 us
  transfers between devices with their start and end apart: 8, of which 5 were waited for; matrix products, arithmetic and copies ran while one was open for 4% of the time, Pallas kernels for 0%

profile of v1, /device:TPU:1, one launch (start us, length us, event | category | flops | bytes accessed | tf_op | source)
XLA Modules:
  0.0 172.5 jit_solution(3335849295288674710)
XLA Ops:
  1.5 5.4 %fusion.67 = f32[12,16384]{1,0:T(8,128)S(1)} fusion(f32[12,64]{1,0:T(8,128)S(1)} %select_reduce_fusion, f32[8,8,128,128]{3,2,1,0:T(8,128)} %bitcast.139), kind=kOutput, calls=%fused_computation.98 | convolution fusion | flops 75497472 | bytes 4983808 | tf_op jit(solution)/shard_map/dot_general | solution.py:134
  7.2 5.3 %collective-permute-start = (f32[2,16384]{1,0:T(2,128)S(1)}, f32[2,16384]{1,0:T(2,128)S(1)}, u32[]{:S(2)}, u32[]{:S(2)}) collective-permute-start(f32[2,16384]{1,0:T(2,128)S(1)} %get-tuple-element.220), channel_id=1, source_target_pairs={{1,0},{2,1},{3,2},{4,3},{5,4},{6,5},{7,6},{8,7},{9,8},{10,9},{11,1... | collective-permute-start | bytes 393224 | tf_op jit(solution)/shard_map/ppermute | solution.py:97
  12.5 1.9 %collective-permute-start.1 = (f32[2,16384]{1,0:T(2,128)S(1)}, f32[2,16384]{1,0:T(2,128)S(1)}, u32[]{:S(2)}, u32[]{:S(2)}) collective-permute-start(f32[2,16384]{1,0:T(2,128)S(1)} %get-tuple-element.224), channel_id=1, source_target_pairs={{1,128},{2,129},{3,130},{4,131},{5,132},{6,133},{7,134},{8,135},{9... | collective-permute-start | bytes 393224 | tf_op jit(solution)/shard_map/ppermute | solution.py:97
  15.3 4.4 %collective-permute-start.3 = (f32[2,16384]{1,0:T(2,128)S(1)}, f32[2,16384]{1,0:T(2,128)S(1)}, u32[]{:S(2)}, u32[]{:S(2)}) collective-permute-start(f32[2,16384]{1,0:T(2,128)S(1)} %get-tuple-element.222), channel_id=1, source_target_pairs={{0,1},{1,2},{2,3},{3,4},{4,5},{5,6},{6,7},{7,8},{8,9},{9,10},{10,1... | collective-permute-start | bytes 393224 | tf_op jit(solution)/shard_map/ppermute | solution.py:97
  19.6 1.9 %collective-permute-start.4 = (f32[2,16384]{1,0:T(2,128)S(1)}, f32[2,16384]{1,0:T(2,128)S(1)}, u32[]{:S(2)}, u32[]{:S(2)}) collective-permute-start(f32[2,16384]{1,0:T(2,128)S(1)} %get-tuple-element.221), channel_id=1, source_target_pairs={{0,129},{1,130},{2,131},{3,132},{4,133},{5,134},{6,135},{7,136},{8... | collective-permute-start | bytes 393224 | tf_op jit(solution)/shard_map/ppermute | solution.py:97
  21.7 4.2 %collective-permute-done.4 = f32[2,16384]{1,0:T(2,128)S(1)} collective-permute-done((f32[2,16384]{1,0:T(2,128)S(1)}, f32[2,16384]{1,0:T(2,128)S(1)}, u32[]{:S(2)}, u32[]{:S(2)}) %collective-permute-start.4) | collective-permute-done | bytes 131104 | tf_op jit(solution)/shard_map/ppermute | solution.py:97
  27.4 15.4 %all-to-all-start.1 = ((bf16[256,4,128]{2,1,0:T(4,128)(2,1)}), bf16[256,4,128]{2,1,0:T(4,128)(2,1)S(1)}, u32[]{:S(2)}, u32[]{:S(2)}) async-start(bf16[256,4,128]{2,1,0:T(4,128)(2,1)} %copy.125), calls=%async_computation.1 | async-start | bytes 524288 | tf_op jit(solution)/shard_map/all_to_all | solution.py:146
  43.6 1.6 copy.121
  45.1 13.1 %all-to-all-done.1 = bf16[256,4,128]{2,1,0:T(4,128)(2,1)S(1)} async-done(((bf16[256,4,128]{2,1,0:T(4,128)(2,1)}), bf16[256,4,128]{2,1,0:T(4,128)(2,1)S(1)}, u32[]{:S(2)}, u32[]{:S(2)}) %all-to-all-start.1) | async-done | bytes 262176 | tf_op jit(solution)/shard_map/all_to_all | solution.py:146
  58.3 5.5 %all-to-all-start = ((bf16[256,8,256]{2,1,0:T(8,128)(2,1)}), bf16[256,8,256]{2,1,0:T(8,128)(2,1)S(1)}, u32[]{:S(2)}, u32[]{:S(2)}) async-start(bf16[256,8,256]{2,1,0:T(8,128)(2,1)} %copy.121), calls=%async_computation | async-start | bytes 2097152 | tf_op jit(solution)/shard_map/all_to_all | solution.py:158
  64.8 30.0 %all-to-all-done = bf16[256,8,256]{2,1,0:T(8,128)(2,1)S(1)} async-done(((bf16[256,8,256]{2,1,0:T(8,128)(2,1)}), bf16[256,8,256]{2,1,0:T(8,128)(2,1)S(1)}, u32[]{:S(2)}, u32[]{:S(2)}) %all-to-all-start) | async-done | bytes 1048608 | tf_op jit(solution)/shard_map/all_to_all | solution.py:158
  95.1 1.6 copy.122
  97.5 19.9 %conditional.1 = (bf16[512,1024]{0,1:T(8,128)(2,1)S(1)}) conditional(s32[]{:T(128)} %convert_element_type.151, (bf16[512,1024]{1,0:T(8,128)(2,1)S(1)}, bf16[512,512]{1,0:T(8,128)(2,1)S(1)}, bf16[512,512]{1,0:T(8,128)(2,1)S(1)}, bf16[512,128]{1,0:T(8,128)(2,1)}, bf16[128,512]{1,0:T(8,128)(2,1)}, /*index=5*/bf16[512,128]{0,1:T(8,128)(2,1)S(1)}, ...), branch_computations={%region_2.3_spmd.clone, %region_3.4_spmd.clone} | conditional | flops 6727139328 | bytes 74449104 | solution.py:195
  97.5 2.9 %fusion = bf16[512,1024]{0,1:T(8,128)(2,1)S(1)} fusion(bf16[1024,1024]{1,0:T(8,128)(2,1)} %constant.94.clone.2, bf16[512,1024]{1,0:T(8,128)(2,1)S(1)} %get-tuple-element.88), kind=kOutput, calls=%fused_computation.2 | convolution fusion | flops 1074266112 | bytes 4194304 | tf_op jit(solution)/shard_map/cond/branch_0_fun/dot_general | solution.py:76
  103.0 1.9 %multiply_convert_fusion = (bf16[512,512]{0,1:T(8,128)(2,1)}, bf16[512,512]{0,1:T(8,128)(2,1)S(1)}) fusion(f32[512,512]{0,1:T(8,128)S(1)} %fusion.1, f32[512,512]{0,1:T(8,128)S(1)} %fusion.4, f32[512,512]{0,1:T(8,128)S(1)} %fusion.11, bf16[512,128]{1,0:T(8,128)(2,1)S(1)} %copy-done.14, bf16[128,512]{1,0:T(8,128)(2,1)S(1)} %copy-done.19), kind=kOutput, calls=%fused_computation.23 | convolution fusion | flops 70778880 | bytes 4456448 | tf_op jit(solution)/shard_map/cond/branch_0_fun/dot_general | solution.py:76
  106.3 2.8 %fusion.14 = f32[512,1024]{1,0:T(8,128)S(1)} fusion(bf16[512,1024]{1,0:T(8,128)(2,1)} %constant.104, f32[512,512]{1,0:T(8,128)} %fusion.80, bf16[512,512]{0,1:T(8,128)(2,1)} %get-tuple-element.214, bf16[512,512]{1,0:T(8,128)(2,1)S(1)} %get-tuple-element.90), kind=kOutput, calls=%fused_computation.22 | convolution fusion | flops 805830656 | bytes 5242880 | tf_op jit(solution)/shard_map/cond/branch_0_fun/dot_general | solution.py:76
  109.1 2.5 %fusion.81 = f32[512,512]{1,0:T(8,128)} fusion(bf16[512,512]{0,1:T(8,128)(2,1)} %get-tuple-element.214, bf16[512,512]{1,0:T(8,128)(2,1)S(1)} %get-tuple-element.89), kind=kOutput, calls=%fused_computation.131 | convolution fusion | flops 268435456 | bytes 2097152 | tf_op jit(solution)/shard_map/cond/branch_0_fun/dot_general | solution.py:76
  111.6 3.8 %add_convert_fusion = bf16[512,1024]{1,0:T(8,128)(2,1)} fusion(f32[512,1024]{1,0:T(8,128)S(1)} %fusion.14, bf16[512,1024]{1,0:T(8,128)(2,1)} %constant.105, f32[512,512]{1,0:T(8,128)} %fusion.81, bf16[512,512]{0,1:T(8,128)(2,1)} %copy-done.4, bf16[512,512]{1,0:T(8,128)(2,1)S(1)} %get-tuple-element.90), kind=kOutput, calls=%fused_computation | convolution fusion | flops 806879232 | bytes 6291456 | tf_op jit(solution)/shard_map/cond/branch_0_fun/dot_general | solution.py:76
  119.1 1.6 copy.134
  120.7 14.4 %all-to-all-start.2 = ((bf16[256,8,256]{2,1,0:T(8,128)(2,1)}), bf16[256,8,256]{2,1,0:T(8,128)(2,1)S(1)}, u32[]{:S(2)}, u32[]{:S(2)}) async-start(bf16[256,8,256]{2,1,0:T(8,128)(2,1)} %copy.134), calls=%async_computation.2 | async-start | bytes 2097152 | tf_op jit(solution)/shard_map/all_to_all | solution.py:203
  136.4 1.9 %copy.120 = s32[4,512,256]{1,2,0:T(8,128)S(1)} copy(s32[4,512,256]{2,1,0:T(8,128)} %param.29) | data formatting | bytes 4194304 | tf_op args[4]
  138.3 27.8 %all-to-all-done.2 = bf16[256,8,256]{2,1,0:T(8,128)(2,1)S(1)} async-done(((bf16[256,8,256]{2,1,0:T(8,128)(2,1)}), bf16[256,8,256]{2,1,0:T(8,128)(2,1)S(1)}, u32[]{:S(2)}, u32[]{:S(2)}) %all-to-all-start.2) | async-done | bytes 1048608 | tf_op jit(solution)/shard_map/all_to_all | solution.py:203
  167.4 2.2 %bitcast_select_fusion = f32[4,512,256]{1,2,0:T(8,128)} fusion(bf16[4,512,256]{1,2,0:T(8,128)(2,1)S(1)} %copy-done.2, s32[4,512,256]{1,2,0:T(8,128)S(1)} %copy.120, bf16[256,2,4,256]{3,0,2,1:T(8,128)(2,1)S(1)} %bitcast.143, bf16[2,512,256,1]{2,1,3,0:T(8,128)(2,1)S(1)} %copy-done.16), kind=kOutput, calls=%fused_computation.101 | convolution fusion | flops 539492352 | bytes 6815744 | tf_op jit(solution)/shard_map/cyj,jczx->zyx/dot_general | solution.py:205
  169.7 2.9 %copy.138 = f32[4,512,256]{2,1,0:T(8,128)} copy(f32[4,512,256]{1,2,0:T(8,128)} %bitcast_select_fusion) | data formatting | bytes 4194304 | tf_op jit(solution)/shard_map/jit(_where)/select_n | solution.py:207
  (68 shorter events, 16.7 us)
Async XLA Ops:
  7.0 19.1 %copy-start.17 = (bf16[2,256,128,1]{2,1,0,3:T(8,128)(2,1)S(1)}, bf16[2,256,128,1]{2,1,0,3:T(8,128)(2,1)}, u32[]{:S(2)}) copy-start(bf16[2,256,128,1]{2,1,0,3:T(8,128)(2,1)} %constant.107) | copy-start | bytes 393220
  7.0 35.9 %copy-start.8 = (bf16[4,512,256]{2,1,0:T(8,128)(2,1)S(1)}, bf16[4,512,256]{2,1,0:T(8,128)(2,1)}, u32[]{:S(2)}) copy-start(bf16[4,512,256]{2,1,0:T(8,128)(2,1)} %param.28) | copy-start | bytes 3145732
  7.2 14.3 %collective-permute-start = (f32[2,16384]{1,0:T(2,128)S(1)}, f32[2,16384]{1,0:T(2,128)S(1)}, u32[]{:S(2)}, u32[]{:S(2)}) collective-permute-start(f32[2,16384]{1,0:T(2,128)S(1)} %get-tuple-element.220), channel_id=1, source_target_pairs={{1,0},{2,1},{3,2},{4,3},{5,4},{6,5},{7,6},{8,7},{9,8},{10,9},{11,1... | collective-permute-start | bytes 393224 | tf_op jit(solution)/shard_map/ppermute | solution.py:97
  12.5 9.1 %collective-permute-start.1 = (f32[2,16384]{1,0:T(2,128)S(1)}, f32[2,16384]{1,0:T(2,128)S(1)}, u32[]{:S(2)}, u32[]{:S(2)}) collective-permute-start(f32[2,16384]{1,0:T(2,128)S(1)} %get-tuple-element.224), channel_id=1, source_target_pairs={{1,128},{2,129},{3,130},{4,131},{5,132},{6,133},{7,134},{8,135},{9... | collective-permute-start | bytes 393224 | tf_op jit(solution)/shard_map/ppermute | solution.py:97
  14.5 7.3 %collective-permute-start.2 = (f32[2,16384]{1,0:T(2,128)S(1)}, f32[2,16384]{1,0:T(2,128)S(1)}, u32[]{:S(2)}, u32[]{:S(2)}) collective-permute-start(f32[2,16384]{1,0:T(2,128)S(1)} %get-tuple-element.223), channel_id=1, source_target_pairs={{0,128},{1,129},{2,130},{3,131},{4,132},{5,133},{6,134},{7,135},{8... | collective-permute-start | bytes 393224 | tf_op jit(solution)/shard_map/ppermute | solution.py:97
  15.3 6.5 %collective-permute-start.3 = (f32[2,16384]{1,0:T(2,128)S(1)}, f32[2,16384]{1,0:T(2,128)S(1)}, u32[]{:S(2)}, u32[]{:S(2)}) collective-permute-start(f32[2,16384]{1,0:T(2,128)S(1)} %get-tuple-element.222), channel_id=1, source_target_pairs={{0,1},{1,2},{2,3},{3,4},{4,5},{5,6},{6,7},{7,8},{8,9},{9,10},{10,1... | collective-permute-start | bytes 393224 | tf_op jit(solution)/shard_map/ppermute | solution.py:97
  19.6 6.3 %collective-permute-start.4 = (f32[2,16384]{1,0:T(2,128)S(1)}, f32[2,16384]{1,0:T(2,128)S(1)}, u32[]{:S(2)}, u32[]{:S(2)}) collective-permute-start(f32[2,16384]{1,0:T(2,128)S(1)} %get-tuple-element.221), channel_id=1, source_target_pairs={{0,129},{1,130},{2,131},{3,132},{4,133},{5,134},{6,135},{7,136},{8... | collective-permute-start | bytes 393224 | tf_op jit(solution)/shard_map/ppermute | solution.py:97
  21.7 21.1 %copy-start.18 = (bf16[2,256,512,1]{2,1,3,0:T(8,128)(2,1)S(1)}, bf16[2,256,512,1]{2,1,3,0:T(8,128)(2,1)}, u32[]{:S(2)}) copy-start(bf16[2,256,512,1]{2,1,3,0:T(8,128)(2,1)} %constant.106) | copy-start | bytes 1572868
  27.4 30.9 %all-to-all-start.1 = ((bf16[256,4,128]{2,1,0:T(4,128)(2,1)}), bf16[256,4,128]{2,1,0:T(4,128)(2,1)S(1)}, u32[]{:S(2)}, u32[]{:S(2)}) async-start(bf16[256,4,128]{2,1,0:T(4,128)(2,1)} %copy.125), calls=%async_computation.1 | async-start | bytes 524288 | tf_op jit(solution)/shard_map/all_to_all | solution.py:146
  45.1 19.0 %copy-start.3 = (bf16[512,512]{1,0:T(8,128)(2,1)S(1)}, bf16[512,512]{1,0:T(8,128)(2,1)}, u32[]{:S(2)}) copy-start(bf16[512,512]{1,0:T(8,128)(2,1)} %constant.87.clone) | copy-start | bytes 1572868
  58.3 36.5 %all-to-all-start = ((bf16[256,8,256]{2,1,0:T(8,128)(2,1)}), bf16[256,8,256]{2,1,0:T(8,128)(2,1)S(1)}, u32[]{:S(2)}, u32[]{:S(2)}) async-start(bf16[256,8,256]{2,1,0:T(8,128)(2,1)} %copy.121), calls=%async_computation | async-start | bytes 2097152 | tf_op jit(solution)/shard_map/all_to_all | solution.py:158
  64.0 0.8 copy-start.11
  64.2 0.7 copy-start.13
  95.1 2.4 %copy-start = (bf16[512,512]{1,0:T(8,128)(2,1)S(1)}, bf16[512,512]{1,0:T(8,128)(2,1)}, u32[]{:S(2)}) copy-start(bf16[512,512]{1,0:T(8,128)(2,1)} %constant.92.clone) | copy-start | bytes 1572868
  95.1 2.4 %copy-start.1 = (bf16[512,512]{1,0:T(8,128)(2,1)S(1)}, bf16[512,512]{1,0:T(8,128)(2,1)}, u32[]{:S(2)}) copy-start(bf16[512,512]{1,0:T(8,128)(2,1)} %constant.91.clone) | copy-start | bytes 1572868
  95.1 2.4 %copy-start.7 = (bf16[128,512]{1,0:T(8,128)(2,1)S(1)}, bf16[128,512]{1,0:T(8,128)(2,1)}, u32[]{:S(2)}) copy-start(bf16[128,512]{1,0:T(8,128)(2,1)} %constant.90.clone) | copy-start | bytes 393220
  101.9 1.1 copy-start.14
  101.9 1.1 copy-start.19
  104.8 1.4 copy-start.4
  119.1 16.0 %copy-start.9 = (bf16[4,512,256]{2,1,0:T(8,128)(2,1)S(1)}, bf16[4,512,256]{2,1,0:T(8,128)(2,1)}, u32[]{:S(2)}) copy-start(bf16[4,512,256]{2,1,0:T(8,128)(2,1)} %param.28) | copy-start | bytes 3145732
  120.7 45.4 %all-to-all-start.2 = ((bf16[256,8,256]{2,1,0:T(8,128)(2,1)}), bf16[256,8,256]{2,1,0:T(8,128)(2,1)S(1)}, u32[]{:S(2)}, u32[]{:S(2)}) async-start(bf16[256,8,256]{2,1,0:T(8,128)(2,1)} %copy.134), calls=%async_computation.2 | async-start | bytes 2097152 | tf_op jit(solution)/shard_map/all_to_all | solution.py:203
  166.1 1.2 copy-start.2
  166.1 1.4 copy-start.16

commit v2 on v1

v2 whole, which is shorter than its diff:
```python
import functools
import math

import jax
import jax.numpy as jnp
import ml_dtypes
import numpy as np
from jax import lax
from jax.experimental import pallas as pl
from jax.experimental.pallas import tpu as pltpu
from jax.sharding import PartitionSpec as P

GZ = 512
GY = 512
GX = 512
PIX = 128

least_modulus = 0.5
feedback = 0.9


def dft_tables(length):
    index = np.arange(length, dtype=np.int64)
    product = (index[:, None] * index[None, :]) % length
    angles = product.astype(np.float32) * np.float32(2.0 * math.pi / length)
    factor = np.float32(1.0 / math.sqrt(length))
    return (
        (np.cos(angles) * factor).astype(ml_dtypes.bfloat16),
        (np.sin(angles) * factor).astype(ml_dtypes.bfloat16),
    )


def interpolation(cells, pixels):
    grid = np.arange(cells, dtype=np.float32)
    detector = np.arange(pixels, dtype=np.float32)
    position = (grid + np.float32(0.5)) * np.float32(pixels / cells) - np.float32(0.5)
    return np.maximum(
        np.float32(0.0), np.float32(1.0) - np.abs(position[:, None] - detector[None, :])
    )


def bf(table):
    return np.asarray(table).astype(ml_dtypes.bfloat16)


COS, SIN = dft_tables(GY)
HALF = GY // 2
_y, _x, _z, _c = np.meshgrid(np.arange(4), np.arange(4), np.arange(8), np.arange(2), indexing="ij")
ROW_OF = 32 * _z + 8 * _y + 2 * _x + _c
_imag = np.concatenate([COS[HALF : HALF + 1], -SIN[1:HALF]])
FORWARD_Y = np.stack(
    [COS[:HALF][ROW_OF.reshape(4, 64)], _imag[ROW_OF.reshape(4, 64)]], axis=1
).reshape(4, 128, GY)
_two = 2.0 * COS[:, :HALF].astype(np.float32)
_two[:, 0] = COS[:, 0]
_sin = -2.0 * SIN[:, :HALF].astype(np.float32)
_sin[:, 0] = COS[:, HALF]
BACK_Y = np.stack(
    [bf(t.reshape(GY, 8, 32).transpose(0, 2, 1).reshape(GY, HALF)) for t in (_two, _sin)]
)
FORWARD_X = np.concatenate(
    [np.concatenate([COS, -SIN], axis=1), np.concatenate([SIN, COS], axis=1)], axis=0
)
BACK_X = np.concatenate(
    [np.concatenate([COS, SIN], axis=1), np.concatenate([-SIN, COS], axis=1)], axis=0
)
_across = interpolation(GY, PIX)
_mirror = (-np.arange(GY)) % GY
ACROSS_X = bf(_across)
ACROSS_X_MIRROR = bf(_across[_mirror])
_yh, _xx, _cc, _zz, _z4 = np.meshgrid(
    np.arange(2), np.arange(4), np.arange(2), np.arange(8), np.arange(4), indexing="ij"
)
Z_ORDER = (4 * (64 * _yh + 16 * _xx + 2 * _zz + _cc) + _z4).reshape(-1)
_yh, _yl, _xx, _cc, _zz, _p2 = np.meshgrid(
    np.arange(2), np.arange(2), np.arange(4), np.arange(2), np.arange(8), np.arange(2), indexing="ij"
)
K_ORDER = (4 * (64 * _yh + 16 * _xx + 2 * _zz + _cc) + 2 * _yl + _p2).reshape(-1)
COS_Z = COS[K_ORDER][:, Z_ORDER]
SIN_Z = SIN[K_ORDER][:, Z_ORDER]
COS_B = COS[:, K_ORDER]
SIN_B = SIN[:, K_ORDER]
MIRROR = bf(K_ORDER[None, :] == _mirror[K_ORDER][:, None])
WINDOWS = np.zeros((2, 32, 2, 2, 16), np.float32)
for _m in range(32):
    for _r in range(16):
        WINDOWS[:, _m, 0, 0, _r] = max(0.0, 1.0 - abs(_m / 4 + 3.625 - _r))
        WINDOWS[:, _m, 1, 1, _r] = max(0.0, 1.0 - abs(11.625 - _m / 4 - _r))
WINDOWS[1, 0, 1, 1, :] = 0.0
WINDOWS[1, 0, 1, 1, 0:2] = (0.375, 0.625)
WINDOWS = bf(WINDOWS.reshape(2, 64, 32))

MESH = pl.DeviceIdType.MESH


def dot(first, second):
    return jnp.dot(first, second, preferred_element_type=jnp.float32)


def place():
    slab = lax.axis_index("slab")
    return (slab // 64) * 2 + lax.axis_index("img"), (slab // 16) % 4, (slab // 2) % 8, slab % 2


def device(y, x, z, c):
    return (y % 2, (y // 2) * 64 + x * 16 + z * 2 + c)


def greet(others):
    barrier = pltpu.get_barrier_semaphore()
    for other in others:
        pl.semaphore_signal(barrier, inc=1, device_id=other, device_id_type=MESH)
    return lambda: pl.semaphore_wait(barrier, len(others))


class Exchange:
    def __init__(self, x_ref, a_ref, r_ref, sems):
        self.x_ref, self.a_ref, self.r_ref = x_ref, a_ref, r_ref
        self.local, self.z_send, self.z_recv, self.p_send, self.p_recv, self.own = sems
        self.y, self.x, self.z, self.c = place()
        self.m = (self.y * 4 + self.x) * 2 + self.c

    def along_z(self, k, step):
        row, depth = (self.y + k) % 4, (self.z + step) % 8
        return pltpu.make_async_remote_copy(
            src_ref=self.x_ref.at[row, :, depth],
            dst_ref=self.a_ref.at[row, :, self.z],
            send_sem=self.z_send.at[k],
            recv_sem=self.z_recv.at[k],
            device_id=device(self.y, self.x, depth, self.c),
            device_id_type=MESH,
        )

    def keep(self, k):
        row = (self.y + k) % 4
        return pltpu.make_async_copy(
            self.x_ref.at[row, :, self.z], self.a_ref.at[row, :, self.z], self.local.at[k]
        )

    def whole(self, k):
        row = (self.y + k) % 4
        return pltpu.make_async_remote_copy(
            src_ref=self.x_ref.at[row, :, pl.ds(0, 7)],
            dst_ref=self.a_ref.at[row, :, pl.ds(0, 7)],
            send_sem=self.z_send.at[k],
            recv_sem=self.z_recv.at[k],
            device_id=device(self.y, self.x, (self.z + 1) % 8, self.c),
            device_id_type=MESH,
        )

    def start(self, k):
        for step in (4, 1, 7, 2, 6, 3, 5):
            self.along_z(k, step).start()
        self.keep(k).start()

    def spread(self, k):
        self.keep(k).wait()
        self.whole(k).wait_recv()
        row = (self.y + k) % 4
        for dx in (2, 1, 3, 0):
            for dc in (0, 1):
                if (k, dx, dc) == (0, 0, 0):
                    self.mine().start()
                    continue
                column, core = (self.x + dx) % 4, (self.c + dc) % 2
                pltpu.make_async_remote_copy(
                    src_ref=self.a_ref.at[row, column, :, core],
                    dst_ref=self.r_ref.at[self.m],
                    send_sem=self.p_send,
                    recv_sem=self.p_recv,
                    device_id=device(row, column, self.z, core),
                    device_id_type=MESH,
                ).start()

    def mine(self):
        return pltpu.make_async_copy(
            self.a_ref.at[self.y, self.x, :, self.c], self.r_ref.at[self.m], self.own
        )

    def finish(self):
        for k in range(4):
            self.whole(k).wait_send()
        self.mine().wait()
        rest = pltpu.make_async_remote_copy(
            src_ref=self.r_ref.at[pl.ds(0, 31)],
            dst_ref=self.r_ref.at[pl.ds(0, 31)],
            send_sem=self.p_send,
            recv_sem=self.p_recv,
            device_id=device(self.y, self.x, (self.z + 1) % 8, self.c),
            device_id_type=MESH,
        )
        rest.wait_send()
        rest.wait_recv()


EXCHANGE_SEMS = [pltpu.SemaphoreType.DMA((4,))] * 3 + [pltpu.SemaphoreType.DMA] * 3
BLOCKS = (4, 4, 8, 2, 16, 128)
ORDER = (1, 2, 3, 0)


def partners():
    y, x, z, c = place()
    return [device(y, x, (z + d) % 8, c) for d in range(1, 8)] + [
        device((y + d // 8) % 4, (x + d // 2 % 4) % 4, z, (c + d) % 2) for d in range(1, 32)
    ]


def back_kernel(x_ref, r_ref, a_ref, *sems):
    entered = greet(partners())
    exchange = Exchange(x_ref, a_ref, r_ref, sems)
    entered()
    for k in ORDER:
        exchange.start(k)
    for k in ORDER:
        exchange.spread(k)
    exchange.finish()


def back_exchange(blocks):
    return pl.pallas_call(
        back_kernel,
        out_shape=jax.ShapeDtypeStruct((32, 8, 16, 128), jnp.bfloat16),
        in_specs=[pl.BlockSpec(memory_space=pltpu.VMEM)],
        out_specs=pl.BlockSpec(memory_space=pltpu.VMEM),
        scratch_shapes=[pltpu.VMEM(BLOCKS, jnp.bfloat16)] + EXCHANGE_SEMS,
        compiler_params=pltpu.CompilerParams(
            collective_id=2, has_side_effects=True, vmem_limit_bytes=16 << 20
        ),
    )(blocks)


def forward_kernel(
    density, table, windows, orient, sharp, images,
    r_ref, e_ref,
    x_ref, a_ref, stage, held, parts, sent, got, padded, g_ref, h_ref, made, whole_rows,
    load, c_send, c_recv, g_send, g_recv, g_own, e_send, e_recv, e_own, *sems,
):
    y, x, z, c = place()
    image = lax.axis_index("img")
    slab = lax.axis_index("slab")
    m = (y * 4 + x) * 2 + c

    def beside(shift, turn):
        return ((image + turn) % 2, (slab + shift + 128) % 128)

    moves = [(shift, turn) for shift in (-1, 0, 1) for turn in (0, 1) if (shift, turn) != (0, 0)]
    entered = greet(partners() + [beside(*move) for move in moves])
    fetch = pltpu.make_async_copy(images, held, load)
    fetch.start()
    exchange = Exchange(x_ref, a_ref, r_ref, sems)

    def transform(k):
        row = (y + k) % 4
        for plane in range(4):
            out = dot(table[row], density[plane])
            for part in range(2):
                for side in range(2):
                    stage[pl.ds(plane * 4 + part * 2 + side, 64, stride=16), :] = out[
                        part * 64 : part * 64 + 64, side * 128 : side * 128 + 128
                    ]
        x_ref[row] = stage[...].astype(jnp.bfloat16).reshape(4, 8, 2, 16, 128)

    transform(1)
    entered()
    exchange.start(1)
    for k in (2, 3):
        transform(k)
        exchange.start(k)
    transform(0)

    near = orient[...] - slab * 4
    steps = lax.broadcasted_iota(jnp.int32, (16, 64), 0) - 4 - near
    squares = (steps * steps).astype(jnp.float32)
    raw = jnp.exp(-sharp[...] * squares)
    total = 1.0 + 2.0 * (
        jnp.exp(-sharp[...])
        + jnp.exp(-4.0 * sharp[...])
        + jnp.exp(-9.0 * sharp[...])
        + jnp.exp(-16.0 * sharp[...])
    )
    mixing = jnp.where(jnp.abs(steps) <= 4, raw / total, 0.0)
    high = mixing.astype(jnp.bfloat16)
    low = (mixing - high.astype(jnp.float32)).astype(jnp.bfloat16)
    factors = jnp.concatenate(
        [
            jnp.concatenate([high, high], axis=1),
            jnp.concatenate([low, jnp.zeros_like(low)], axis=1),
        ],
        axis=0,
    )
    fetch.wait()

    def mix(index, carry):
        at = index * 2
        rows = jnp.concatenate(
            [held[pl.ds(at, 64, stride=128), :], held[pl.ds(at + 1, 64, stride=128), :]], axis=1
        )
        upper = rows.astype(jnp.bfloat16)
        lower = (rows - upper.astype(jnp.float32)).astype(jnp.bfloat16)
        out = dot(factors, jnp.concatenate([upper, lower], axis=0))
        out = out[:16] + out[16:]
        parts[pl.ds(at, 16, stride=128), :] = out[:, :128]
        parts[pl.ds(at + 1, 16, stride=128), :] = out[:, 128:]
        return carry

    lax.fori_loop(0, 64, mix, 0)
    sent[...] = parts[...].astype(jnp.bfloat16).reshape(16, 128, 128)

    def gift(index, shift, turn):
        first = 4 + 4 * shift + 2 * ((image + turn) % 2)
        return pltpu.make_async_remote_copy(
            src_ref=sent.at[pl.ds(first, 2)],
            dst_ref=got.at[index],
            send_sem=c_send.at[index],
            recv_sem=c_recv.at[index],
            device_id=beside(shift, turn),
            device_id_type=MESH,
        )

    gifts = [gift(index, *move) for index, move in enumerate(moves)]
    for copy in gifts:
        copy.start()
    exchange.spread(1)
    for copy in gifts:
        copy.wait()
    padded[...] = jnp.zeros_like(padded)
    for plane in range(2):
        own = sent[4 + 2 * image + plane].astype(jnp.float32)
        for index, (shift, turn) in enumerate(moves):
            piece = got[index, plane].astype(jnp.float32)
            if shift:
                source = slab - shift
                piece = jnp.where(jnp.logical_and(source >= 0, source < 128), piece, 0.0)
            own = own + piece
        padded[plane, pl.ds(16, 128), :] = own
        for depth in range(8):
            g_ref[depth, plane, pl.ds(0, 16), :] = padded[
                plane, pl.ds(16 + 8 * depth - 4, 16), :
            ].astype(jnp.bfloat16)
            mirrored = padded[plane, pl.ds(16 + 116 - 8 * depth, 16), :]
            if depth == 0:
                mirrored = jnp.concatenate([own[63:65], mirrored[2:]], axis=0)
            g_ref[depth, plane, pl.ds(16, 16), :] = mirrored.astype(jnp.bfloat16)

    def window(step):
        depth = (z + step) % 8
        return pltpu.make_async_remote_copy(
            src_ref=g_ref.at[depth],
            dst_ref=h_ref.at[z],
            send_sem=g_send,
            recv_sem=g_recv,
            device_id=device(y, x, depth, c),
            device_id_type=MESH,
        )

    for step in (4, 1, 7, 2, 6, 3, 5):
        window(step).start()
    stay = pltpu.make_async_copy(g_ref.at[z], h_ref.at[z], g_own)
    stay.start()
    exchange.start(0)
    exchange.spread(2)
    stay.wait()
    seven = pltpu.make_async_remote_copy(
        src_ref=g_ref.at[pl.ds(0, 7)],
        dst_ref=h_ref.at[pl.ds(0, 7)],
        send_sem=g_send,
        recv_sem=g_recv,
        device_id=device(y, x, (z + 1) % 8, c),
        device_id_type=MESH,
    )
    seven.wait_send()
    seven.wait_recv()
    weights = windows[jnp.where(z == 0, 1, 0)]
    for source in range(8):
        for plane in range(2):
            made[pl.ds(source * 2 + plane, 64, stride=16), :] = dot(weights, h_ref[source, plane])
    whole_rows[...] = made[...].astype(jnp.bfloat16).reshape(32, 2, 16, 128)
    for d in range(1, 32):
        row, column, core = (y + d // 8) % 4, (x + d // 2 % 4) % 4, (c + d) % 2
        pltpu.make_async_remote_copy(
            src_ref=whole_rows.at[(row * 4 + column) * 2 + core],
            dst_ref=e_ref.at[m],
            send_sem=e_send,
            recv_sem=e_recv,
            device_id=device(row, column, z, core),
            device_id_type=MESH,
        ).start()
    kept = pltpu.make_async_copy(whole_rows.at[m], e_ref.at[m], e_own)
    kept.start()
    exchange.spread(3)
    exchange.spread(0)
    kept.wait()
    others = pltpu.make_async_remote_copy(
        src_ref=whole_rows.at[pl.ds(0, 31)],
        dst_ref=e_ref.at[pl.ds(0, 31)],
        send_sem=e_send,
        recv_sem=e_recv,
        device_id=device(y, x, (z + 1) % 8, c),
        device_id_type=MESH,
    )
    others.wait_send()
    others.wait_recv()
    exchange.finish()


def forward_exchange(density, orient, sharp, images):
    vmem = pl.BlockSpec(memory_space=pltpu.VMEM)
    bfloat, single = jnp.bfloat16, jnp.float32
    one = pltpu.SemaphoreType.DMA
    return pl.pallas_call(
        forward_kernel,
        out_shape=[
            jax.ShapeDtypeStruct((32, 8, 16, 128), bfloat),
            jax.ShapeDtypeStruct((32, 2, 16, 128), bfloat),
        ],
        in_specs=[vmem] * 5 + [pl.BlockSpec(memory_space=pl.ANY)],
        out_specs=[vmem] * 2,
        scratch_shapes=[
            pltpu.VMEM(BLOCKS, bfloat),
            pltpu.VMEM(BLOCKS, bfloat),
            pltpu.VMEM((1024, 128), single),
            pltpu.VMEM((64 * 128, 128), single),
            pltpu.VMEM((16 * 128, 128), single),
            pltpu.VMEM((16, 128, 128), bfloat),
            pltpu.VMEM((5, 2, 128, 128), bfloat),
            pltpu.VMEM((2, 160, 128), single),
            pltpu.VMEM((8, 2, 32, 128), bfloat),
            pltpu.VMEM((8, 2, 32, 128), bfloat),
            pltpu.VMEM((1024, 128), single),
            pltpu.VMEM((32, 2, 16, 128), bfloat),
            one, one((5,)), one((5,)), one, one, one, one, one, one,
        ]
        + EXCHANGE_SEMS,
        compiler_params=pltpu.CompilerParams(
            collective_id=1, has_side_effects=True, vmem_limit_bytes=32 << 20
        ),
    )(
        density,
        FORWARD_Y,
        WINDOWS,
        orient.reshape(1, -1),
        sharp.reshape(1, -1),
        images.reshape(-1, PIX),
    )


def amplitudes(rows, across, scale):
    return jnp.sqrt(scale * dot(rows, across.T)).astype(jnp.bfloat16).astype(jnp.float32)


def project(real_x, imag_x, amplitude):
    real_z = dot(COS_Z, real_x) + dot(SIN_Z, imag_x)
    imag_z = dot(COS_Z, imag_x) - dot(SIN_Z, real_x)
    modulus = jnp.sqrt(real_z * real_z + imag_z * imag_z)
    factor = amplitude / jnp.maximum(modulus, least_modulus)
    proj_real = (real_z * factor).astype(jnp.bfloat16)
    proj_imag = (imag_z * factor).astype(jnp.bfloat16)
    back_real = (dot(COS_B, proj_real) - dot(SIN_B, proj_imag)).astype(jnp.bfloat16)
    back_imag = (dot(COS_B, proj_imag) + dot(SIN_B, proj_real)).astype(jnp.bfloat16)
    return back_real, back_imag


def body(images, orient, sharp, density, support):
    depth, rows_all, width_own = density.shape
    count = images.shape[0]
    image_count = lax.axis_size("img")
    slab_index = lax.axis_index("slab")
    image_index = lax.axis_index("img")
    scale = depth / (count * image_count)

    lines, expanded = forward_exchange(density, orient, sharp, images)
    lines = (
        lines.reshape(2, 2, 4, 2, 8, 4, 2, 2, 128)
        .transpose(0, 2, 3, 4, 5, 6, 1, 7, 8)
        .reshape(GZ, 2 * GX)
    )
    expanded = expanded.reshape(32, 2, 16, PIX).transpose(1, 0, 2, 3).reshape(2, GZ, PIX)
    first, second = expanded[0], expanded[1]
    first_mirror = dot(MIRROR, first).astype(jnp.bfloat16)
    second_mirror = dot(MIRROR, second).astype(jnp.bfloat16)

    def usual(lines, first, second, first_mirror, second_mirror):
        both = dot(lines, FORWARD_X).astype(jnp.bfloat16)
        amplitude = 0.5 * (
            amplitudes(first, ACROSS_X, scale) + amplitudes(second_mirror, ACROSS_X_MIRROR, scale)
        )
        back_real, back_imag = project(both[:, :GX], both[:, GX:], amplitude)
        return dot(jnp.concatenate([back_real, back_imag], axis=1), BACK_X).astype(jnp.bfloat16)

    def real_rows(lines, first, second, first_mirror, second_mirror):
        out = []
        for part, near, far in ((0, first, first_mirror), (1, second, second_mirror)):
            line = lines[:, part * GX : (part + 1) * GX]
            both = dot(line, FORWARD_X[:GX]).astype(jnp.bfloat16)
            amplitude = 0.5 * (
                amplitudes(near, ACROSS_X, scale) + amplitudes(far, ACROSS_X_MIRROR, scale)
            )
            back_real, back_imag = project(both[:, :GX], both[:, GX:], amplitude)
            out.append(
                dot(jnp.concatenate([back_real, back_imag], axis=1), BACK_X[:, :GX]).astype(
                    jnp.bfloat16
                )
            )
        return jnp.concatenate(out, axis=1)

    special = jnp.logical_and(slab_index == 0, image_index == 0)
    out = lax.cond(
        special, real_rows, usual, lines, first, second, first_mirror, second_mirror
    )
    blocks = out.reshape(2, 4, 8, 2, depth, 2, 2, 2, 128).transpose(0, 6, 1, 2, 3, 4, 5, 7, 8)
    out = back_exchange(blocks.reshape(BLOCKS))
    projected = jnp.einsum(
        "cyj,jzchl->zyhl",
        BACK_Y,
        out.reshape(HALF, depth, 2, 2, 128),
        preferred_element_type=jnp.float32,
    ).reshape(depth, GY, width_own)
    previous = density.astype(jnp.float32)
    return jnp.where(support == 1, projected, previous - feedback * projected)


def solution(mesh):
    placed = (
        P(("img", "slab"), None, None),
        P(("img", "slab")),
        P(("img", "slab")),
        P("slab", None, "img"),
        P("slab", None, "img"),
    )
    return jax.shard_map(
        body, mesh=mesh, in_specs=placed, out_specs=P("slab", None, "img"), check_vma=False
    )
```

time: 173 us -> 129 us (0.75)
  the two profiles are of different devices: /device:TPU:1 before, /device:TPU:105 now
where the time goes in v2:
time: 129 us; the launch traced here: 128 us
  Pallas kernels  90.9 us (70%)
  matrix products  17.2 us (13%)
  local copies, waits for them, and re-layouts  15.6 us (12%)
  other arithmetic  3.91 us (3%)
    pallas_call x1, Pallas kernels, forward_exchange(): pl.pallas_call(forward_kernel, out_shape=[jax.ShapeDtypeStruct((32, 8, 16...  46.2 us
    pallas_call x1, Pallas kernels, back_exchange(): pl.pallas_call(back_kernel, out_shape=jax.ShapeDtypeStruct((32, 8, 16, 12...  44.7 us
    dot_general x13, matrix products, dot(): return jnp.dot(first, second, preferred_element_type=jnp.float32)  15.1 us
    unnamed x32, local copies, waits for them, and re-layouts  6.59 us
    select_n x1, other arithmetic, body(): return jnp.where(support == 1, projected, previous - feedback * projected)  3.91 us
    reshape x1, local copies, waits for them, and re-layouts, body(): projected = jnp.einsum('cyj,jzchl->zyhl', BACK_Y, out.reshape(HALF, depth...  3.01 us

profile of v2, /device:TPU:105, one launch (start us, length us, event | category | flops | bytes accessed | tf_op | source)
XLA Modules:
  0.0 128.3 jit_solution(8271958857248576874)
XLA Ops:
  0.0 1.2 copy-done
  1.2 2.2 %copy-done.2 = f32[64,128,128]{2,1,0:T(8,128)S(1)} copy-done((f32[64,128,128]{2,1,0:T(8,128)S(1)}, f32[64,128,128]{2,1,0:T(8,128)}, u32[]{:S(2)}) %copy-start.2) | copy-done | bytes 4194328
  3.4 1.0 copy-done.3
  4.5 0.8 copy-done.4
  5.2 0.7 copy-done.5
  5.9 0.7 copy-done.6
  6.5 46.2 %shard_map.243 = (bf16[32,8,16,128]{3,2,1,0:T(8,128)(2,1)S(1)}, bf16[32,2,16,128]{3,2,1,0:T(8,128)(2,1)S(1)}) custom-call(bf16[4,512,256]{2,1,0:T(8,128)(2,1)S(1)} %copy-done, bf16[4,128,512]{2,1,0:T(8,128)(2,1)S(1)} %copy-done.3, bf16[2,64,32]{2,1,0:T(8,128)(2,1)S(1)} %copy-done.4, s32[1,64]{1,0:T(1,128)S(1)} %bitcast.111, f32[1,64]{1,0:T(1,128)S(1)} %bitcast.112, ...), custom_call_target="tpu_custom_call" | custom-call | tf_op jit(solution)/shard_map/pallas_call | solution.py:410
  53.5 0.8 copy.56
  54.3 1.6 %reshape.36 = bf16[512,1024]{1,0:T(8,128)(2,1)} reshape(bf16[2,4,2,8,4,2,2,2,128]{8,7,6,5,4,3,2,1,0:T(2,128)(2,1)S(1)} %copy.56) | data formatting | bytes 2097152 | tf_op jit(solution)/shard_map/reshape | solution.py:475
  55.9 16.4 %conditional.1 = (bf16[512,1024]{0,1:T(8,128)(2,1)S(1)}) conditional(s32[]{:T(128)} %convert_element_type.126, (bf16[512,1024]{1,0:T(8,128)(2,1)}, bf16[512,512]{1,0:T(8,128)(2,1)S(1)}, bf16[512,512]{1,0:T(8,128)(2,1)S(1)}, bf16[512,128]{1,0:T(8,128)(2,1)}, bf16[128,512]{1,0:T(8,128)(2,1)}, /*index=5*/bf16[512,128]{0,1:T(8,128)(2,1)S(1)}, ...), branch_computations={%region_0.0_spmd.clone, %region_1.0_spmd.clone} | conditional | flops 6727139328 | bytes 74449104 | solution.py:507
  55.9 3.2 %fusion = bf16[512,1024]{0,1:T(8,128)(2,1)S(1)} fusion(bf16[1024,1024]{1,0:T(8,128)(2,1)} %constant.62.clone.2, bf16[512,1024]{1,0:T(8,128)(2,1)} %get-tuple-element.104), kind=kOutput, calls=%fused_computation.2 | convolution fusion | flops 1074266112 | bytes 4194304 | tf_op jit(solution)/shard_map/cond/branch_0_fun/dot_general | solution.py:97
  61.0 0.6 fusion.11
  61.6 1.1 multiply_convert_fusion
  62.7 0.8 copy-done.13
  64.0 3.7 %fusion.14 = f32[512,1024]{1,0:T(8,128)} fusion(bf16[512,1024]{1,0:T(8,128)(2,1)} %constant.72, f32[512,512]{1,0:T(8,128)S(1)} %fusion.72, bf16[512,512]{0,1:T(8,128)(2,1)S(1)} %get-tuple-element.192, bf16[512,512]{1,0:T(8,128)(2,1)S(1)} %get-tuple-element.112), kind=kOutput, calls=%fused_computation.22 | convolution fusion | flops 805830656 | bytes 5242880 | tf_op jit(solution)/shard_map/cond/branch_0_fun/dot_general | solution.py:97
  68.1 3.2 %add_convert_fusion = bf16[512,1024]{1,0:T(8,128)(2,1)S(1)} fusion(f32[512,1024]{1,0:T(8,128)} %fusion.14, bf16[512,1024]{1,0:T(8,128)(2,1)} %constant.73, f32[512,512]{1,0:T(8,128)S(1)} %fusion.73, bf16[512,512]{0,1:T(8,128)(2,1)} %copy-done.13, bf16[512,512]{1,0:T(8,128)(2,1)S(1)} %get-tuple-element.112), kind=kOutput, calls=%fused_computation | convolution fusion | flops 806879232 | bytes 6291456 | tf_op jit(solution)/shard_map/cond/branch_0_fun/dot_general | solution.py:97
  71.4 0.5 copy.51
  72.3 0.5 copy.60
  72.9 0.8 reshape.37
  73.6 1.0 copy.61
  74.6 44.7 %shard_map.244 = bf16[32,8,16,128]{3,2,1,0:T(8,128)(2,1)S(1)} custom-call(bf16[4,4,8,2,16,128]{5,4,3,2,1,0:T(8,128)(2,1)S(1)} %bitcast.108), custom_call_target="tpu_custom_call" | custom-call | tf_op jit(solution)/shard_map/pallas_call | solution.py:220
  119.3 2.1 %fusion.69 = f32[4,2,128,512,1]{3,2,4,1,0:T(8,128)} fusion(bf16[2,512,256,1,1]{2,1,0,4,3:T(8,128)(2,1)S(1)} %copy-done.17, bf16[256,4,2,2,128]{4,3,2,1,0:T(2,128)(2,1)S(1)} %bitcast.106), kind=kOutput, calls=%fused_computation.103 | convolution fusion | flops 536870912 | bytes 3670016 | tf_op jit(solution)/shard_map/cyj,jzchl->zyhl/dot_general | solution.py:512
  121.4 3.0 %copy.64 = f32[4,512,256]{2,1,0:T(8,128)} copy(f32[4,512,256]{1,2,0:T(8,128)} %bitcast.113) | data formatting | bytes 4194304 | tf_op jit(solution)/shard_map/reshape | solution.py:517
  124.4 3.9 %subtract_select_fusion = f32[4,512,256]{2,1,0:T(8,128)} fusion(f32[4,512,256]{2,1,0:T(8,128)} %copy.64, bf16[4,512,256]{2,1,0:T(8,128)(2,1)S(1)} %copy-done.1, s32[4,512,256]{2,1,0:T(8,128)} %param.31), kind=kLoop, calls=%fused_computation.98 | loop fusion | flops 2621440 | bytes 7340032 | tf_op jit(solution)/shard_map/jit(_where)/select_n | solution.py:519
  (40 shorter events, 3.5 us)
Async XLA Ops:
  0.0 1.2 copy-start
  1.2 2.2 %copy-start.2 = (f32[64,128,128]{2,1,0:T(8,128)S(1)}, f32[64,128,128]{2,1,0:T(8,128)}, u32[]{:S(2)}) copy-start(f32[64,128,128]{2,1,0:T(8,128)} %param.27) | copy-start | bytes 12582916
  3.4 1.0 copy-start.3
  4.5 0.8 copy-start.4
  5.2 0.7 copy-start.5
  5.9 0.7 copy-start.6
  6.5 46.3 %copy-start.12 = (bf16[512,512]{1,0:T(8,128)(2,1)S(1)}, bf16[512,512]{1,0:T(8,128)(2,1)}, u32[]{:S(2)}) copy-start(bf16[512,512]{1,0:T(8,128)(2,1)} %constant.53.clone) | copy-start | bytes 1572868
  52.8 0.7 copy-start.18
  52.8 0.7 copy-start.20
  53.5 2.4 %copy-start.7 = (bf16[512,512]{1,0:T(8,128)(2,1)S(1)}, bf16[512,512]{1,0:T(8,128)(2,1)}, u32[]{:S(2)}) copy-start(bf16[512,512]{1,0:T(8,128)(2,1)} %constant.60.clone) | copy-start | bytes 1572868
  53.5 2.4 %copy-start.8 = (bf16[512,512]{1,0:T(8,128)(2,1)S(1)}, bf16[512,512]{1,0:T(8,128)(2,1)}, u32[]{:S(2)}) copy-start(bf16[512,512]{1,0:T(8,128)(2,1)} %constant.57.clone) | copy-start | bytes 1572868
  53.5 2.4 %copy-start.9 = (bf16[512,512]{1,0:T(8,128)(2,1)S(1)}, bf16[512,512]{1,0:T(8,128)(2,1)}, u32[]{:S(2)}) copy-start(bf16[512,512]{1,0:T(8,128)(2,1)} %constant.58.clone) | copy-start | bytes 1572868
  53.5 2.4 %copy-start.10 = (bf16[512,512]{1,0:T(8,128)(2,1)S(1)}, bf16[512,512]{1,0:T(8,128)(2,1)}, u32[]{:S(2)}) copy-start(bf16[512,512]{1,0:T(8,128)(2,1)} %constant.59.clone) | copy-start | bytes 1572868
  53.5 2.4 %copy-start.16 = (bf16[128,512]{1,0:T(8,128)(2,1)S(1)}, bf16[128,512]{1,0:T(8,128)(2,1)}, u32[]{:S(2)}) copy-start(bf16[128,512]{1,0:T(8,128)(2,1)} %constant.56.clone) | copy-start | bytes 393220
  60.5 1.1 copy-start.21
  60.5 1.1 copy-start.23
  62.7 0.8 copy-start.13
  73.6 45.7 %copy-start.17 = (bf16[2,512,256,1,1]{2,1,0,4,3:T(8,128)(2,1)S(1)}, bf16[2,512,256,1,1]{2,1,0,4,3:T(8,128)(2,1)}, u32[]{:S(2)}) copy-start(bf16[2,512,256,1,1]{2,1,0,4,3:T(8,128)(2,1)} %constant.74) | copy-start | bytes 1572868
  121.4 3.0 %copy-start.1 = (bf16[4,512,256]{2,1,0:T(8,128)(2,1)S(1)}, bf16[4,512,256]{2,1,0:T(8,128)(2,1)}, u32[]{:S(2)}) copy-start(bf16[4,512,256]{2,1,0:T(8,128)(2,1)} %density.1) | copy-start | bytes 3145732

commit v3 on v2

--- a/solution.py
+++ b/solution.py
@@ -58,16 +58,22 @@
 BACK_Y = np.stack(
     [bf(t.reshape(GY, 8, 32).transpose(0, 2, 1).reshape(GY, HALF)) for t in (_two, _sin)]
 )
-FORWARD_X = np.concatenate(
-    [np.concatenate([COS, -SIN], axis=1), np.concatenate([SIN, COS], axis=1)], axis=0
-)
-BACK_X = np.concatenate(
-    [np.concatenate([COS, SIN], axis=1), np.concatenate([-SIN, COS], axis=1)], axis=0
-)
+BACK_Y = np.concatenate([BACK_Y[0], BACK_Y[1]], axis=1)
+COS_X, SIN_X = COS.reshape(2, 256, GX), SIN.reshape(2, 256, GX)
+COS_R, SIN_R = (t.reshape(GX, 2, 256).transpose(1, 0, 2) for t in (COS, SIN))
 _across = interpolation(GY, PIX)
 _mirror = (-np.arange(GY)) % GY
-ACROSS_X = bf(_across)
-ACROSS_X_MIRROR = bf(_across[_mirror])
+ACROSS_X = np.stack([bf(_across.T), bf(_across[_mirror].T)])
+EDGE_IN = np.zeros((2, GX, 128), np.float32)
+EDGE_OUT = np.zeros((2, 128, GX), np.float32)
+EDGE_ACROSS = np.zeros((2, PIX, 128), np.float32)
+for _e in range(2):
+    EDGE_IN[_e, :, _e] = COS[:, GX // 2].astype(np.float32)
+    EDGE_OUT[_e, _e, :] = COS[GX // 2].astype(np.float32)
+    EDGE_ACROSS[_e, :, _e] = _across[GX // 2]
+EDGE_IN = bf(EDGE_IN.reshape(2, 2, 256, 128))
+EDGE_OUT = bf(EDGE_OUT.reshape(2, 128, 2, 256).transpose(0, 2, 1, 3))
+EDGE_ACROSS = bf(EDGE_ACROSS)
 _yh, _xx, _cc, _zz, _z4 = np.meshgrid(
     np.arange(2), np.arange(4), np.arange(2), np.arange(8), np.arange(4), indexing="ij"
 )
@@ -76,10 +82,10 @@
     np.arange(2), np.arange(2), np.arange(4), np.arange(2), np.arange(8), np.arange(2), indexing="ij"
 )
 K_ORDER = (4 * (64 * _yh + 16 * _xx + 2 * _zz + _cc) + 2 * _yl + _p2).reshape(-1)
-COS_Z = COS[K_ORDER][:, Z_ORDER]
-SIN_Z = SIN[K_ORDER][:, Z_ORDER]
-COS_B = COS[:, K_ORDER]
-SIN_B = SIN[:, K_ORDER]
+COS_Z = COS[K_ORDER][:, Z_ORDER].reshape(4, 128, GZ)
+SIN_Z = SIN[K_ORDER][:, Z_ORDER].reshape(4, 128, GZ)
+COS_B = COS[:, K_ORDER].reshape(2, 256, GZ)
+SIN_B = SIN[:, K_ORDER].reshape(2, 256, GZ)
 MIRROR = bf(K_ORDER[None, :] == _mirror[K_ORDER][:, None])
 WINDOWS = np.zeros((2, 32, 2, 2, 16), np.float32)
 for _m in range(32):
@@ -167,7 +173,7 @@
                     src_ref=self.a_ref.at[row, column, :, core],
                     dst_ref=self.r_ref.at[self.m],
                     send_sem=self.p_send,
-                    recv_sem=self.p_recv,
+                    recv_sem=self.p_recv.at[k],
                     device_id=device(row, column, self.z, core),
                     device_id_type=MESH,
                 ).start()
@@ -177,23 +183,41 @@
             self.a_ref.at[self.y, self.x, :, self.c], self.r_ref.at[self.m], self.own
         )
 
+    def arrived(self, k):
+        count = 8 if k else 7
+        if not k:
+            self.mine().wait()
+        pltpu.make_async_remote_copy(
+            src_ref=self.r_ref.at[pl.ds(0, count)],
+            dst_ref=self.r_ref.at[pl.ds(0, count)],
+            send_sem=self.p_send,
+            recv_sem=self.p_recv.at[k],
+            device_id=device(self.y, self.x, (self.z + 1) % 8, self.c),
+            device_id_type=MESH,
+        ).wait_recv()
+        return (self.y + 4 - k) % 4
+
     def finish(self):
         for k in range(4):
             self.whole(k).wait_send()
-        self.mine().wait()
-        rest = pltpu.make_async_remote_copy(
+        pltpu.make_async_remote_copy(
             src_ref=self.r_ref.at[pl.ds(0, 31)],
             dst_ref=self.r_ref.at[pl.ds(0, 31)],
             send_sem=self.p_send,
-            recv_sem=self.p_recv,
+            recv_sem=self.p_recv.at[0],
             device_id=device(self.y, self.x, (self.z + 1) % 8, self.c),
             device_id_type=MESH,
-        )
-        rest.wait_send()
-        rest.wait_recv()
-
-
-EXCHANGE_SEMS = [pltpu.SemaphoreType.DMA((4,))] * 3 + [pltpu.SemaphoreType.DMA] * 3
+        ).wait_send()
+
+
+EXCHANGE_SEMS = [
+    pltpu.SemaphoreType.DMA((4,)),
+    pltpu.SemaphoreType.DMA((4,)),
+    pltpu.SemaphoreType.DMA((4,)),
+    pltpu.SemaphoreType.DMA,
+    pltpu.SemaphoreType.DMA((4,)),
+    pltpu.SemaphoreType.DMA,
+]
 BLOCKS = (4, 4, 8, 2, 16, 128)
 ORDER = (1, 2, 3, 0)
 
@@ -205,49 +229,53 @@
     ]
 
 
-def back_kernel(x_ref, r_ref, a_ref, *sems):
-    entered = greet(partners())
-    exchange = Exchange(x_ref, a_ref, r_ref, sems)
-    entered()
-    for k in ORDER:
-        exchange.start(k)
-    for k in ORDER:
-        exchange.spread(k)
-    exchange.finish()
-
-
-def back_exchange(blocks):
-    return pl.pallas_call(
-        back_kernel,
-        out_shape=jax.ShapeDtypeStruct((32, 8, 16, 128), jnp.bfloat16),
-        in_specs=[pl.BlockSpec(memory_space=pltpu.VMEM)],
-        out_specs=pl.BlockSpec(memory_space=pltpu.VMEM),
-        scratch_shapes=[pltpu.VMEM(BLOCKS, jnp.bfloat16)] + EXCHANGE_SEMS,
-        compiler_params=pltpu.CompilerParams(
-            collective_id=2, has_side_effects=True, vmem_limit_bytes=16 << 20
-        ),
-    )(blocks)
-
-
-def forward_kernel(
-    density, table, windows, orient, sharp, images,
-    r_ref, e_ref,
-    x_ref, a_ref, stage, held, parts, sent, got, padded, g_ref, h_ref, made, whole_rows,
-    load, c_send, c_recv, g_send, g_recv, g_own, e_send, e_recv, e_own, *sems,
-):
+TABLES = (
+    FORWARD_Y, COS_X, SIN_X, MIRROR, ACROSS_X, COS_Z, SIN_Z, COS_B, SIN_B, COS_R, SIN_R,
+    EDGE_IN, EDGE_OUT, EDGE_ACROSS,
+)
+
+
+def step_kernel(scale, windows, orient, sharp, density_in, images, *rest):
+    count = len(TABLES)
+    sources, (out_ref,), rest = rest[:count], rest[count : count + 1], rest[count + 1 :]
+    tables, rest = rest[:count], rest[count:]
+    (
+        density, r_ref, e_ref,
+        x_ref, a_ref, stage, held, parts, sent, got, padded, g_ref, h_ref, made, whole_rows,
+        x_back, a_back, sum_re, sum_im, sum_edge, line_re, line_im, line_edge, amplitude, amplitude_edge,
+        proj_re, proj_im, edge_re, edge_im, back_re, back_im, back_edge,
+        d_load, t_load, load, c_send, c_recv, g_send, g_recv, g_own, e_send, e_recv, e_own, *sems,
+    ) = rest
+    (
+        table, cos_x, sin_x, mirror, across_x, cos_z, sin_z, cos_b, sin_b, cos_r, sin_r,
+        edge_in, edge_out, edge_across,
+    ) = tables
     y, x, z, c = place()
     image = lax.axis_index("img")
     slab = lax.axis_index("slab")
     m = (y * 4 + x) * 2 + c
+    both_real = jnp.logical_and(slab == 0, image == 0)
+    usual = jnp.logical_not(both_real)
 
     def beside(shift, turn):
         return ((image + turn) % 2, (slab + shift + 128) % 128)
 
     moves = [(shift, turn) for shift in (-1, 0, 1) for turn in (0, 1) if (shift, turn) != (0, 0)]
     entered = greet(partners() + [beside(*move) for move in moves])
+    fills = [
+        pltpu.make_async_copy(sources[i], tables[i], t_load.at[i]) for i in range(len(TABLES))
+    ]
+    density_fill = pltpu.make_async_copy(density_in, density, d_load)
     fetch = pltpu.make_async_copy(images, held, load)
+    fills[0].start()
+    density_fill.start()
     fetch.start()
-    exchange = Exchange(x_ref, a_ref, r_ref, sems)
+    for fill in fills[1:]:
+        fill.start()
+    exchange = Exchange(x_ref, a_ref, r_ref, sems[:6])
+    back = Exchange(x_back, a_back, out_ref, sems[6:])
+    fills[0].wait()
+    density_fill.wait()
 
     def transform(k):
         row = (y + k) % 4
@@ -388,6 +416,37 @@
     kept = pltpu.make_async_copy(whole_rows.at[m], e_ref.at[m], e_own)
     kept.start()
     exchange.spread(3)
+    for fill in fills[1:]:
+        fill.wait()
+    for total_ref in (sum_re, sum_im, sum_edge):
+        total_ref[...] = jnp.zeros_like(total_ref)
+
+    def along_x(k):
+        source = exchange.arrived(k)
+        stage[...] = r_ref[pl.ds(source * 8, 8)].astype(jnp.float32).reshape(1024, 128)
+        real, imag = (
+            jnp.concatenate(
+                [stage[pl.ds(part * 2 + side, 256, stride=4), :] for side in range(2)], axis=1
+            ).astype(jnp.bfloat16)
+            for part in range(2)
+        )
+        side = source % 2
+        at = pl.ds((source // 2) * 256, 256)
+
+        @pl.when(usual)
+        def _():
+            sum_re[at, :] += dot(real, cos_x[side]) + dot(imag, sin_x[side])
+            sum_im[at, :] += dot(imag, cos_x[side]) - dot(real, sin_x[side])
+
+        @pl.when(both_real)
+        def _():
+            for part, line in enumerate((real, imag)):
+                columns = pl.ds(part * 256, 256)
+                sum_re[at, columns] += dot(line, cos_x[side, :, pl.ds(0, 256)])
+                sum_im[at, columns] -= dot(line, sin_x[side, :, pl.ds(0, 256)])
+                sum_edge[at, :] += dot(line, edge_in[part, side])
+
+    along_x(1)
     exchange.spread(0)
     kept.wait()
     others = pltpu.make_async_remote_copy(
@@ -400,22 +459,146 @@
     )
     others.wait_send()
     others.wait_recv()
+
+    def rounded_root(rows, across):
+        return jnp.sqrt(scale * dot(rows, across)).astype(jnp.bfloat16).astype(jnp.float32)
+
+    first, second = (e_ref[:, part].reshape(GZ, PIX) for part in range(2))
+    first_mirror = dot(mirror[...], first).astype(jnp.bfloat16)
+    second_mirror = dot(mirror[...], second).astype(jnp.bfloat16)
+
+    @pl.when(usual)
+    def _():
+        amplitude[...] = 0.5 * (
+            rounded_root(first, across_x[0]) + rounded_root(second_mirror, across_x[1])
+        )
+
+    @pl.when(both_real)
+    def _():
+        for part, (near, far) in enumerate(((first, first_mirror), (second, second_mirror))):
+            amplitude[:, pl.ds(part * 256, 256)] = 0.5 * (
+                rounded_root(near, across_x[0, :, pl.ds(0, 256)])
+                + rounded_root(far, across_x[1, :, pl.ds(0, 256)])
+            )
+        amplitude_edge[...] = 0.5 * (
+            rounded_root(
+                jnp.concatenate([first, second], axis=1),
+                jnp.concatenate([edge_across[0], edge_across[1]], axis=0),
+            )
+            + rounded_root(
+                jnp.concatenate([first_mirror, second_mirror], axis=1),
+                jnp.concatenate([edge_across[0], edge_across[1]], axis=0),
+            )
+        )
+
+    along_x(2)
+    along_x(3)
+    along_x(0)
+    line_re[...] = sum_re[...].astype(jnp.bfloat16)
+    line_im[...] = sum_im[...].astype(jnp.bfloat16)
+    line_edge[...] = sum_edge[...].astype(jnp.bfloat16)
+
+    def projection(real_z, imag_z, target):
+        modulus = jnp.sqrt(real_z * real_z + imag_z * imag_z)
+        factor = target / jnp.maximum(modulus, least_modulus)
+        return (real_z * factor).astype(jnp.bfloat16), (imag_z * factor).astype(jnp.bfloat16)
+
+    def along_depth(block, carry):
+        at = pl.ds(pl.multiple_of(block * 128, 128), 128)
+        cos, sin = cos_z[block], sin_z[block]
+        proj_re[at, :], proj_im[at, :] = projection(
+            dot(cos, line_re[...]) + dot(sin, line_im[...]),
+            dot(cos, line_im[...]) - dot(sin, line_re[...]),
+            amplitude[at, :],
+        )
+
+        @pl.when(both_real)
+        def _():
+            edge_re[at, :], edge_im[at, :] = projection(
+                dot(cos, line_edge[...]), -dot(sin, line_edge[...]), amplitude_edge[at, :]
+            )
+
+        return carry
+
+    lax.fori_loop(0, 4, along_depth, 0)
+    column = lax.broadcasted_iota(jnp.int32, (1, GX), 1) % 256
+    share = 1.0 + jnp.where(column == 0, 0.0, both_real.astype(jnp.float32))
+
+    def back_depth(half):
+        cos, sin = cos_b[half], sin_b[half]
+        back_re[half] = (
+            share * (dot(cos, proj_re[...]) - dot(sin, proj_im[...]))
+        ).astype(jnp.bfloat16)
+        back_im[half] = (
+            share * (dot(cos, proj_im[...]) + dot(sin, proj_re[...]))
+        ).astype(jnp.bfloat16)
+
+        @pl.when(both_real)
+        def _():
+            back_edge[half] = (dot(cos, edge_re[...]) - dot(sin, edge_im[...])).astype(jnp.bfloat16)
+
+    def back_x(k):
+        row = (y + k) % 4
+        half, side = row // 2, row % 2
+
+        def put(part, out):
+            for column_block in range(2):
+                stage[pl.ds(part * 2 + column_block, 256, stride=4), :] = out[
+                    :, column_block * 128 : column_block * 128 + 128
+                ]
+
+        @pl.when(usual)
+        def _():
+            real, imag, cos, sin = back_re[half], back_im[half], cos_r[side], sin_r[side]
+            put(0, dot(real, cos) - dot(imag, sin))
+            put(1, dot(imag, cos) + dot(real, sin))
+
+        @pl.when(both_real)
+        def _():
+            cos, sin = cos_r[side, pl.ds(0, 256)], sin_r[side, pl.ds(0, 256)]
+            for part in range(2):
+                columns = pl.ds(part * 256, 256)
+                put(
+                    part,
+                    dot(back_re[half, :, columns], cos)
+                    - dot(back_im[half, :, columns], sin)
+                    + dot(back_edge[half], edge_out[part, side]),
+                )
+
+        x_back[row] = stage[...].astype(jnp.bfloat16).reshape(4, 8, 2, 16, 128)
+        back.start(k)
+
+    near_half = ((y + 1) % 4) // 2
+    back_depth(near_half)
+    back_x(1)
+    back_depth(1 - near_half)
+    for k in (2, 3, 0):
+        back_x(k)
+    for k in ORDER:
+        back.spread(k)
+    for k in ORDER:
+        back.arrived(k)
     exchange.finish()
-
-
-def forward_exchange(density, orient, sharp, images):
+    back.finish()
+
+
+def exchange_step(scale, density, orient, sharp, images):
     vmem = pl.BlockSpec(memory_space=pltpu.VMEM)
+    anywhere = pl.BlockSpec(memory_space=pl.ANY)
     bfloat, single = jnp.bfloat16, jnp.float32
     one = pltpu.SemaphoreType.DMA
+    tiles = (32, 8, 16, 128)
+    square = (GZ, GX)
     return pl.pallas_call(
-        forward_kernel,
-        out_shape=[
-            jax.ShapeDtypeStruct((32, 8, 16, 128), bfloat),
-            jax.ShapeDtypeStruct((32, 2, 16, 128), bfloat),
-        ],
-        in_specs=[vmem] * 5 + [pl.BlockSpec(memory_space=pl.ANY)],
-        out_specs=[vmem] * 2,
-        scratch_shapes=[
+        functools.partial(step_kernel, scale),
+        out_shape=jax.ShapeDtypeStruct(tiles, bfloat),
+        in_specs=[vmem] * 3 + [anywhere] * (2 + len(TABLES)),
+        out_specs=vmem,
+        scratch_shapes=[pltpu.VMEM(t.shape, bfloat) for t in TABLES]
+        + [
+            pltpu.VMEM(density.shape, bfloat),
+            pltpu.VMEM(tiles, bfloat),
+            pltpu.VMEM((32, 2, 16, 128), bfloat),
             pltpu.VMEM(BLOCKS, bfloat),
             pltpu.VMEM(BLOCKS, bfloat),
             pltpu.VMEM((1024, 128), single),
@@ -428,95 +611,78 @@
             pltpu.VMEM((8, 2, 32, 128), bfloat),
             pltpu.VMEM((1024, 128), single),
             pltpu.VMEM((32, 2, 16, 128), bfloat),
-            one, one((5,)), one((5,)), one, one, one, one, one, one,
+            pltpu.VMEM(BLOCKS, bfloat),
+            pltpu.VMEM(BLOCKS, bfloat),
+            pltpu.VMEM(square, single),
+            pltpu.VMEM(square, single),
+            pltpu.VMEM((GZ, 128), single),
+            pltpu.VMEM(square, bfloat),
+            pltpu.VMEM(square, bfloat),
+            pltpu.VMEM((GZ, 128), bfloat),
+            pltpu.VMEM(square, single),
+            pltpu.VMEM((GZ, 128), single),
+            pltpu.VMEM(square, bfloat),
+            pltpu.VMEM(square, bfloat),
+            pltpu.VMEM((GZ, 128), bfloat),
+            pltpu.VMEM((GZ, 128), bfloat),
+            pltpu.VMEM((2, 256, GX), bfloat),
+            pltpu.VMEM((2, 256, GX), bfloat),
+            pltpu.VMEM((2, 256, 128), bfloat),
+            one, one((len(TABLES),)), one, one((5,)), one((5,)), one, one, one, one, one, one,
         ]
-        + EXCHANGE_SEMS,
+        + EXCHANGE_SEMS * 2,
         compiler_params=pltpu.CompilerParams(
-            collective_id=1, has_side_effects=True, vmem_limit_bytes=32 << 20
+            collective_id=1, has_side_effects=True, vmem_limit_bytes=52 << 20
         ),
     )(
-        density,
-        FORWARD_Y,
         WINDOWS,
         orient.reshape(1, -1),
         sharp.reshape(1, -1),
+        density,
         images.reshape(-1, PIX),
-    )
-
-
-def amplitudes(rows, across, scale):
-    return jnp.sqrt(scale * dot(rows, across.T)).astype(jnp.bfloat16).astype(jnp.float32)
-
-
-def project(real_x, imag_x, amplitude):
-    real_z = dot(COS_Z, real_x) + dot(SIN_Z, imag_x)
-    imag_z = dot(COS_Z, imag_x) - dot(SIN_Z, real_x)
-    modulus = jnp.sqrt(real_z * real_z + imag_z * imag_z)
-    factor = amplitude / jnp.maximum(modulus, least_modulus)
-    proj_real = (real_z * factor).astype(jnp.bfloat16)
-    proj_imag = (imag_z * factor).astype(jnp.bfloat16)
-    back_real = (dot(COS_B, proj_real) - dot(SIN_B, proj_imag)).astype(jnp.bfloat16)
-    back_imag = (dot(COS_B, proj_imag) + dot(SIN_B, proj_real)).astype(jnp.bfloat16)
-    return back_real, back_imag
+        *TABLES,
+    )
+
+
+def update_kernel(lines, table, density, support, out, wide):
+    plane = pl.program_id(0)
+
+    @pl.when(plane == 0)
+    def _():
+        wide[...] = lines[...].astype(jnp.float32).reshape(4096, 128)
+
+    rows = [
+        jnp.concatenate(
+            [wide[pl.ds(plane * 4 + part * 2 + side, HALF, stride=16), :] for side in range(2)],
+            axis=1,
+        ).astype(jnp.bfloat16)
+        for part in range(2)
+    ]
+    projected = dot(table[...], jnp.concatenate(rows, axis=0))
+    previous = density[0].astype(jnp.float32)
+    out[0] = jnp.where(support[0] == 1, projected, previous - feedback * projected)
+
+
+def update(lines, density, support):
+    depth, rows, columns = density.shape
+    vmem = pl.BlockSpec(memory_space=pltpu.VMEM)
+    block = pl.BlockSpec((1, rows, columns), lambda plane: (plane, 0, 0))
+    return pl.pallas_call(
+        update_kernel,
+        grid=(depth,),
+        out_shape=jax.ShapeDtypeStruct(density.shape, jnp.float32),
+        in_specs=[vmem, vmem, block, block],
+        out_specs=block,
+        scratch_shapes=[pltpu.VMEM((4096, 128), jnp.float32)],
+        compiler_params=pltpu.CompilerParams(vmem_limit_bytes=32 << 20),
+    )(lines, BACK_Y, density, support)
 
 
 def body(images, orient, sharp, density, support):
-    depth, rows_all, width_own = density.shape
-    count = images.shape[0]
-    image_count = lax.axis_size("img")
-    slab_index = lax.axis_index("slab")
-    image_index = lax.axis_index("img")
-    scale = depth / (count * image_count)
-
-    lines, expanded = forward_exchange(density, orient, sharp, images)
-    lines = (
-        lines.reshape(2, 2, 4, 2, 8, 4, 2, 2, 128)
-        .transpose(0, 2, 3, 4, 5, 6, 1, 7, 8)
-        .reshape(GZ, 2 * GX)
-    )
-    expanded = expanded.reshape(32, 2, 16, PIX).transpose(1, 0, 2, 3).reshape(2, GZ, PIX)
-    first, second = expanded[0], expanded[1]
-    first_mirror = dot(MIRROR, first).astype(jnp.bfloat16)
-    second_mirror = dot(MIRROR, second).astype(jnp.bfloat16)
-
-    def usual(lines, first, second, first_mirror, second_mirror):
-        both = dot(lines, FORWARD_X).astype(jnp.bfloat16)
-        amplitude = 0.5 * (
-            amplitudes(first, ACROSS_X, scale) + amplitudes(second_mirror, ACROSS_X_MIRROR, scale)
-        )
-        back_real, back_imag = project(both[:, :GX], both[:, GX:], amplitude)
-        return dot(jnp.concatenate([back_real, back_imag], axis=1), BACK_X).astype(jnp.bfloat16)
-
-    def real_rows(lines, first, second, first_mirror, second_mirror):
-        out = []
-        for part, near, far in ((0, first, first_mirror), (1, second, second_mirror)):
-            line = lines[:, part * GX : (part + 1) * GX]
-            both = dot(line, FORWARD_X[:GX]).astype(jnp.bfloat16)
-            amplitude = 0.5 * (
-                amplitudes(near, ACROSS_X, scale) + amplitudes(far, ACROSS_X_MIRROR, scale)
-            )
-            back_real, back_imag = project(both[:, :GX], both[:, GX:], amplitude)
-            out.append(
-                dot(jnp.concatenate([back_real, back_imag], axis=1), BACK_X[:, :GX]).astype(
-                    jnp.bfloat16
-                )
-            )
-        return jnp.concatenate(out, axis=1)
-
-    special = jnp.logical_and(slab_index == 0, image_index == 0)
-    out = lax.cond(
-        special, real_rows, usual, lines, first, second, first_mirror, second_mirror
-    )
-    blocks = out.reshape(2, 4, 8, 2, depth, 2, 2, 2, 128).transpose(0, 6, 1, 2, 3, 4, 5, 7, 8)
-    out = back_exchange(blocks.reshape(BLOCKS))
-    projected = jnp.einsum(
-        "cyj,jzchl->zyhl",
-        BACK_Y,
-        out.reshape(HALF, depth, 2, 2, 128),
-        preferred_element_type=jnp.float32,
-    ).reshape(depth, GY, width_own)
-    previous = density.astype(jnp.float32)
-    return jnp.where(support == 1, projected, previous - feedback * projected)
+    depth = density.shape[0]
+    scale = depth / (images.shape[0] * lax.axis_size("img"))
+    lines = exchange_step(scale, density, orient, sharp, images)
+    return update(lines, density, support)
 
 
 def solution(mesh):

time: 129 us -> 100 us (0.78)
  the two profiles are of different devices: /device:TPU:105 before, /device:TPU:1 now
where the time goes in v3:
time: 100 us; the launch traced here: 99.5 us
  Pallas kernels  90.4 us (90%)
  local copies, waits for them, and re-layouts  9.07 us (9%)
    pallas_call x1, Pallas kernels, exchange_step(): pl.pallas_call(functools.partial(step_kernel, scale), out_shape=jax.Shape...  87.5 us
    unnamed x26, local copies, waits for them, and re-layouts  9.07 us
    pallas_call x1, Pallas kernels, update(): pl.pallas_call(update_kernel, grid=(depth,), out_shape=jax.ShapeDtypeStru...  2.94 us

profile of v3, /device:TPU:1, one launch (start us, length us, event | category | flops | bytes accessed | tf_op | source)
XLA Modules:
  0.0 99.5 jit_solution(11241826734405718882)
XLA Ops:
  0.0 0.0 copy-start.3
  0.0 1.0 %copy-done.3 = bf16[2,256,512]{2,1,0:T(8,128)(2,1)S(1)} copy-done((bf16[2,256,512]{2,1,0:T(8,128)(2,1)S(1)}, bf16[2,256,512]{2,1,0:T(8,128)(2,1)}, u32[]{:S(2)}) %copy-start.3) | copy-done | bytes 524312
  1.0 0.0 copy-start.4
  1.0 1.0 %copy-done.4 = bf16[4,128,512]{2,1,0:T(8,128)(2,1)S(1)} copy-done((bf16[4,128,512]{2,1,0:T(8,128)(2,1)S(1)}, bf16[4,128,512]{2,1,0:T(8,128)(2,1)}, u32[]{:S(2)}) %copy-start.4) | copy-done | bytes 524312
  2.1 0.0 copy-start.6
  2.1 0.9 copy-done.6
  3.0 0.0 copy-start.7
  3.0 0.9 copy-done.7
  4.0 0.0 copy-start.8
  4.0 0.9 copy-done.8
  4.9 0.0 copy-start.9
  4.9 0.8 copy-done.9
  5.8 0.0 copy-start.10
  5.8 0.8 copy-done.10
  6.5 0.0 copy-start.11
  6.5 0.7 copy-done.11
  7.2 0.7 copy-done.12
  7.9 87.5 %shard_map.199.lines = bf16[32,8,16,128]{3,2,1,0:T(8,128)(2,1)} custom-call(bf16[2,64,32]{2,1,0:T(8,128)(2,1)S(1)} %copy-done.10, s32[1,64]{1,0:T(1,128)S(1)} %bitcast.3, f32[1,64]{1,0:T(1,128)S(1)} %bitcast.4, bf16[4,512,256]{2,1,0:T(8,128)(2,1)} %density.1, f32[8192,128]{1,0:T(8,128)} %bitcast.5, bf16[4,128,512]{2,1,0:T(8,128)(2,1)S(1)} %copy-done.4, ...), custom_call_target="tpu_custom_call" | custom-call | tf_op jit(solution)/shard_map/pallas_call | solution.py:592
  95.3 0.0 copy-done
  95.3 0.0 copy-done.2
  95.3 0.0 copy-done.5
  95.4 0.0 copy-start.1
  95.4 1.2 %copy-done.1 = bf16[32,8,16,128]{3,2,1,0:T(8,128)(2,1)S(1)} copy-done((bf16[32,8,16,128]{3,2,1,0:T(8,128)(2,1)S(1)}, bf16[32,8,16,128]{3,2,1,0:T(8,128)(2,1)}, u32[]{:S(2)}) %copy-start.1) | copy-done | bytes 1048600
  96.6 2.9 %shard_map.200 = f32[4,512,256]{2,1,0:T(8,128)} custom-call(bf16[32,8,16,128]{3,2,1,0:T(8,128)(2,1)S(1)} %copy-done.1, bf16[512,512]{1,0:T(8,128)(2,1)S(1)} %copy-done.5, bf16[4,512,256]{2,1,0:T(8,128)(2,1)S(1)} %copy-done, s32[4,512,256]{2,1,0:T(8,128)S(1)} %copy-done.2), custom_call_target="tpu_custom_call" | custom-call | tf_op jit(solution)/shard_map/pallas_call | solution.py:670
  (4 shorter events, 0.0 us)
Async XLA Ops:
  0.0 1.0 %copy-start.3 = (bf16[2,256,512]{2,1,0:T(8,128)(2,1)S(1)}, bf16[2,256,512]{2,1,0:T(8,128)(2,1)}, u32[]{:S(2)}) copy-start(bf16[2,256,512]{2,1,0:T(8,128)(2,1)} %constant.34.clone.rest_1_) | copy-start | bytes 1572868
  1.0 1.0 %copy-start.4 = (bf16[4,128,512]{2,1,0:T(8,128)(2,1)S(1)}, bf16[4,128,512]{2,1,0:T(8,128)(2,1)}, u32[]{:S(2)}) copy-start(bf16[4,128,512]{2,1,0:T(8,128)(2,1)} %constant.33.clone.rest_0_) | copy-start | bytes 1572868
  2.1 0.9 copy-start.6
  3.0 0.9 copy-start.7
  4.0 0.9 copy-start.8
  4.9 0.8 copy-start.9
  5.8 0.8 copy-start.10
  6.5 0.7 copy-start.11
  7.2 0.7 copy-start.12
  7.8 87.5 %copy-start = (bf16[4,512,256]{2,1,0:T(8,128)(2,1)S(1)}, bf16[4,512,256]{2,1,0:T(8,128)(2,1)}, u32[]{:S(2)}) copy-start(bf16[4,512,256]{2,1,0:T(8,128)(2,1)} %density.1) | copy-start | bytes 3145732
  7.8 87.5 %copy-start.2 = (s32[4,512,256]{2,1,0:T(8,128)S(1)}, s32[4,512,256]{2,1,0:T(8,128)}, u32[]{:S(2)}) copy-start(s32[4,512,256]{2,1,0:T(8,128)} %support.1) | copy-start | bytes 6291460
  7.9 87.5 %copy-start.5 = (bf16[512,512]{1,0:T(8,128)(2,1)S(1)}, bf16[512,512]{1,0:T(8,128)(2,1)}, u32[]{:S(2)}) copy-start(bf16[512,512]{1,0:T(8,128)(2,1)} %constant.47.clone.table) | copy-start | bytes 1572868
  95.4 1.2 %copy-start.1 = (bf16[32,8,16,128]{3,2,1,0:T(8,128)(2,1)S(1)}, bf16[32,8,16,128]{3,2,1,0:T(8,128)(2,1)}, u32[]{:S(2)}) copy-start(bf16[32,8,16,128]{3,2,1,0:T(8,128)(2,1)} %shard_map.199.lines) | copy-start | bytes 3145732

commit v4 on v2

--- a/solution.py
+++ b/solution.py
@@ -55,19 +55,51 @@
 _two[:, 0] = COS[:, 0]
 _sin = -2.0 * SIN[:, :HALF].astype(np.float32)
 _sin[:, 0] = COS[:, HALF]
-BACK_Y = np.stack(
-    [bf(t.reshape(GY, 8, 32).transpose(0, 2, 1).reshape(GY, HALF)) for t in (_two, _sin)]
-)
-FORWARD_X = np.concatenate(
-    [np.concatenate([COS, -SIN], axis=1), np.concatenate([SIN, COS], axis=1)], axis=0
-)
-BACK_X = np.concatenate(
-    [np.concatenate([COS, SIN], axis=1), np.concatenate([-SIN, COS], axis=1)], axis=0
-)
+BACK_Y = np.stack([bf(t.reshape(GY, 8, 32).transpose(0, 2, 1)) for t in (_two, _sin)], axis=1)
+BACK_Y = BACK_Y.reshape(GY, 2, 2, 128).transpose(2, 0, 1, 3).reshape(2, GY, 256)
+
+
+def quarters(upper_left, upper_right, lower_left, lower_right):
+    return np.concatenate(
+        [
+            np.concatenate([upper_left, upper_right], axis=1),
+            np.concatenate([lower_left, lower_right], axis=1),
+        ],
+        axis=0,
+    )
+
+
+FORWARD_X = np.zeros((2, 2 * GX, 2 * GX), ml_dtypes.bfloat16)
+FORWARD_X[0] = quarters(COS, -SIN, SIN, COS)
+BACK_X = np.zeros((2, 2, 2 * GX, GX), ml_dtypes.bfloat16)
+_low = GX // 2
+_pair = np.where(np.arange(_low) == 0, 1.0, 2.0)[:, None]
+for _e in range(2):
+    _columns = slice(_e * _low, (_e + 1) * _low)
+    _in = -SIN[:, :_low]
+    _in[:, 0] = COS[:, _low]
+    FORWARD_X[1, _e * GX : (_e + 1) * GX, _columns] = COS[:, :_low]
+    FORWARD_X[1, _e * GX : (_e + 1) * GX, GX + _e * _low : GX + (_e + 1) * _low] = _in
+    BACK_X[0, _e] = quarters(COS[:, _columns], SIN[:, _columns], -SIN[:, _columns], COS[:, _columns])
+    _out_re = bf(COS[:_low].astype(np.float32) * _pair)
+    _out_im = bf(-SIN[:_low].astype(np.float32) * _pair)
+    _out_im[0] = COS[_low]
+    for _side in range(2):
+        _half = slice(_side * _low, (_side + 1) * _low)
+        BACK_X[1, _side, _columns, _columns] = _out_re[:, _half]
+        BACK_X[1, _side, GX + _e * _low : GX + (_e + 1) * _low, _columns] = _out_im[:, _half]
 _across = interpolation(GY, PIX)
 _mirror = (-np.arange(GY)) % GY
-ACROSS_X = bf(_across)
-ACROSS_X_MIRROR = bf(_across[_mirror])
+ACROSS_X = np.zeros((2, 2, 2 * PIX, GX), np.float32)
+ACROSS_X[0, 0, :PIX] = _across.T
+ACROSS_X[0, 1, PIX:] = _across[_mirror].T
+EDGE_ACROSS = np.zeros((2 * PIX, 2 * PIX), np.float32)
+for _e in range(2):
+    _rows, _columns = slice(_e * PIX, (_e + 1) * PIX), slice(_e * _low, (_e + 1) * _low)
+    ACROSS_X[1, 0, _rows, _columns] = _across[:_low].T
+    ACROSS_X[1, 1, _rows, _columns] = _across[_mirror][:_low].T
+    EDGE_ACROSS[_rows, _e * PIX] = _across[_low]
+ACROSS_X, EDGE_ACROSS = bf(ACROSS_X), bf(EDGE_ACROSS)
 _yh, _xx, _cc, _zz, _z4 = np.meshgrid(
     np.arange(2), np.arange(4), np.arange(2), np.arange(8), np.arange(4), indexing="ij"
 )
@@ -76,10 +108,13 @@
     np.arange(2), np.arange(2), np.arange(4), np.arange(2), np.arange(8), np.arange(2), indexing="ij"
 )
 K_ORDER = (4 * (64 * _yh + 16 * _xx + 2 * _zz + _cc) + 2 * _yl + _p2).reshape(-1)
-COS_Z = COS[K_ORDER][:, Z_ORDER]
-SIN_Z = SIN[K_ORDER][:, Z_ORDER]
-COS_B = COS[:, K_ORDER]
-SIN_B = SIN[:, K_ORDER]
+FORWARD_Z = np.stack(
+    [
+        np.concatenate([t[K_ORDER][:, Z_ORDER[h * 256 : h * 256 + 256]] for t in (COS, SIN)], axis=1)
+        for h in range(2)
+    ]
+)
+BACK_Z = np.concatenate([COS[:, K_ORDER], SIN[:, K_ORDER]], axis=1).reshape(2, 256, 2 * GZ)
 MIRROR = bf(K_ORDER[None, :] == _mirror[K_ORDER][:, None])
 WINDOWS = np.zeros((2, 32, 2, 2, 16), np.float32)
 for _m in range(32):
@@ -113,6 +148,10 @@
     return lambda: pl.semaphore_wait(barrier, len(others))
 
 
+def across(y, k):
+    return (y, y + 1 - 2 * (y % 2), (y + 2) % 4, 3 - y)[k]
+
+
 class Exchange:
     def __init__(self, x_ref, a_ref, r_ref, sems):
         self.x_ref, self.a_ref, self.r_ref = x_ref, a_ref, r_ref
@@ -121,7 +160,7 @@
         self.m = (self.y * 4 + self.x) * 2 + self.c
 
     def along_z(self, k, step):
-        row, depth = (self.y + k) % 4, (self.z + step) % 8
+        row, depth = across(self.y, k), (self.z + step) % 8
         return pltpu.make_async_remote_copy(
             src_ref=self.x_ref.at[row, :, depth],
             dst_ref=self.a_ref.at[row, :, self.z],
@@ -132,13 +171,13 @@
         )
 
     def keep(self, k):
-        row = (self.y + k) % 4
+        row = across(self.y, k)
         return pltpu.make_async_copy(
             self.x_ref.at[row, :, self.z], self.a_ref.at[row, :, self.z], self.local.at[k]
         )
 
     def whole(self, k):
-        row = (self.y + k) % 4
+        row = across(self.y, k)
         return pltpu.make_async_remote_copy(
             src_ref=self.x_ref.at[row, :, pl.ds(0, 7)],
             dst_ref=self.a_ref.at[row, :, pl.ds(0, 7)],
@@ -156,7 +195,7 @@
     def spread(self, k):
         self.keep(k).wait()
         self.whole(k).wait_recv()
-        row = (self.y + k) % 4
+        row = across(self.y, k)
         for dx in (2, 1, 3, 0):
             for dc in (0, 1):
                 if (k, dx, dc) == (0, 0, 0):
@@ -167,7 +206,7 @@
                     src_ref=self.a_ref.at[row, column, :, core],
                     dst_ref=self.r_ref.at[self.m],
                     send_sem=self.p_send,
-                    recv_sem=self.p_recv,
+                    recv_sem=self.p_recv.at[k],
                     device_id=device(row, column, self.z, core),
                     device_id_type=MESH,
                 ).start()
@@ -177,25 +216,42 @@
             self.a_ref.at[self.y, self.x, :, self.c], self.r_ref.at[self.m], self.own
         )
 
+    def arrived(self, k):
+        count = 8 if k else 7
+        if not k:
+            self.mine().wait()
+        pltpu.make_async_remote_copy(
+            src_ref=self.r_ref.at[pl.ds(0, count)],
+            dst_ref=self.r_ref.at[pl.ds(0, count)],
+            send_sem=self.p_send,
+            recv_sem=self.p_recv.at[k],
+            device_id=device(self.y, self.x, (self.z + 1) % 8, self.c),
+            device_id_type=MESH,
+        ).wait_recv()
+
     def finish(self):
         for k in range(4):
             self.whole(k).wait_send()
-        self.mine().wait()
-        rest = pltpu.make_async_remote_copy(
+        pltpu.make_async_remote_copy(
             src_ref=self.r_ref.at[pl.ds(0, 31)],
             dst_ref=self.r_ref.at[pl.ds(0, 31)],
             send_sem=self.p_send,
-            recv_sem=self.p_recv,
+            recv_sem=self.p_recv.at[0],
             device_id=device(self.y, self.x, (self.z + 1) % 8, self.c),
             device_id_type=MESH,
-        )
-        rest.wait_send()
-        rest.wait_recv()
-
-
-EXCHANGE_SEMS = [pltpu.SemaphoreType.DMA((4,))] * 3 + [pltpu.SemaphoreType.DMA] * 3
+        ).wait_send()
+
+
+EXCHANGE_SEMS = [
+    pltpu.SemaphoreType.DMA((4,)),
+    pltpu.SemaphoreType.DMA((4,)),
+    pltpu.SemaphoreType.DMA((4,)),
+    pltpu.SemaphoreType.DMA,
+    pltpu.SemaphoreType.DMA((4,)),
+    pltpu.SemaphoreType.DMA,
+]
 BLOCKS = (4, 4, 8, 2, 16, 128)
-ORDER = (1, 2, 3, 0)
+ORDER = (2, 3, 1, 0)
 
 
 def partners():
@@ -205,52 +261,61 @@
     ]
 
 
-def back_kernel(x_ref, r_ref, a_ref, *sems):
-    entered = greet(partners())
-    exchange = Exchange(x_ref, a_ref, r_ref, sems)
-    entered()
-    for k in ORDER:
-        exchange.start(k)
-    for k in ORDER:
-        exchange.spread(k)
-    exchange.finish()
-
-
-def back_exchange(blocks):
-    return pl.pallas_call(
-        back_kernel,
-        out_shape=jax.ShapeDtypeStruct((32, 8, 16, 128), jnp.bfloat16),
-        in_specs=[pl.BlockSpec(memory_space=pltpu.VMEM)],
-        out_specs=pl.BlockSpec(memory_space=pltpu.VMEM),
-        scratch_shapes=[pltpu.VMEM(BLOCKS, jnp.bfloat16)] + EXCHANGE_SEMS,
-        compiler_params=pltpu.CompilerParams(
-            collective_id=2, has_side_effects=True, vmem_limit_bytes=16 << 20
-        ),
-    )(blocks)
-
-
-def forward_kernel(
-    density, table, windows, orient, sharp, images,
-    r_ref, e_ref,
-    x_ref, a_ref, stage, held, parts, sent, got, padded, g_ref, h_ref, made, whole_rows,
-    load, c_send, c_recv, g_send, g_recv, g_own, e_send, e_recv, e_own, *sems,
-):
+TABLES = (FORWARD_Y, WINDOWS, FORWARD_X, FORWARD_Z, MIRROR, ACROSS_X, EDGE_ACROSS, BACK_Z, BACK_X, BACK_Y)
+CHOSEN = (2, 5, 8)
+
+
+def step_kernel(scale, orient_in, sharp_in, density_in, images, *rest):
+    count = len(TABLES)
+    sources, out_ref, rest = rest[:count], rest[count], rest[count + 1 :]
+    tables, rest = rest[:count], rest[count:]
+    (
+        orient, sharp, density, r_ref, e_ref,
+        x_ref, a_ref, stage, held, parts, sent, got, padded, g_ref, h_ref, made, whole_rows,
+        x_back, a_back, r_back, wide, lines, spectrum, edges, depth_sum, edge_sum, amplitude, amplitude_edge,
+        projected, projected_edge, final,
+        d_load, t_load, load, o_send, c_send, c_recv, g_send, g_recv, g_own, e_send, e_recv, e_own, *sems,
+    ) = rest
+    (
+        table, windows, forward_x, forward_z, mirror, across_x, edge_across, back_z, back_x_table, back_y,
+    ) = tables
     y, x, z, c = place()
     image = lax.axis_index("img")
     slab = lax.axis_index("slab")
     m = (y * 4 + x) * 2 + c
+    special = jnp.where(slab + image == 0, 1, 0)
+    both_real = special == 1
 
     def beside(shift, turn):
         return ((image + turn) % 2, (slab + shift + 128) % 128)
 
     moves = [(shift, turn) for shift in (-1, 0, 1) for turn in (0, 1) if (shift, turn) != (0, 0)]
     entered = greet(partners() + [beside(*move) for move in moves])
+    fills = [
+        pltpu.make_async_copy(
+            sources[i].at[special] if i in CHOSEN else sources[i], tables[i], t_load.at[i]
+        )
+        for i in range(len(TABLES))
+    ]
+    first_fills = [
+        fills[0],
+        pltpu.make_async_copy(density_in, density, d_load.at[0]),
+        pltpu.make_async_copy(orient_in, orient, d_load.at[1]),
+        pltpu.make_async_copy(sharp_in, sharp, d_load.at[2]),
+    ]
     fetch = pltpu.make_async_copy(images, held, load)
+    for fill in first_fills:
+        fill.start()
     fetch.start()
-    exchange = Exchange(x_ref, a_ref, r_ref, sems)
+    for fill in fills[1:]:
+        fill.start()
+    exchange = Exchange(x_ref, a_ref, r_ref, sems[:6])
+    back = Exchange(x_back, a_back, r_back, sems[6:])
+    for fill in first_fills:
+        fill.wait()
 
     def transform(k):
-        row = (y + k) % 4
+        row = across(y, k)
         for plane in range(4):
             out = dot(table[row], density[plane])
             for part in range(2):
@@ -260,10 +325,10 @@
                     ]
         x_ref[row] = stage[...].astype(jnp.bfloat16).reshape(4, 8, 2, 16, 128)
 
-    transform(1)
+    transform(2)
     entered()
-    exchange.start(1)
-    for k in (2, 3):
+    exchange.start(2)
+    for k in (3, 1):
         transform(k)
         exchange.start(k)
     transform(0)
@@ -320,7 +385,7 @@
     gifts = [gift(index, *move) for index, move in enumerate(moves)]
     for copy in gifts:
         copy.start()
-    exchange.spread(1)
+    exchange.spread(2)
     for copy in gifts:
         copy.wait()
     padded[...] = jnp.zeros_like(padded)
@@ -358,7 +423,63 @@
     stay = pltpu.make_async_copy(g_ref.at[z], h_ref.at[z], g_own)
     stay.start()
     exchange.start(0)
-    exchange.spread(2)
+    exchange.spread(3)
+    for fill in fills[1:]:
+        fill.wait()
+
+    def along_x(half):
+        for side in range(2):
+            wide[pl.ds(side * 1024, 1024), :] = (
+                r_ref[pl.ds((half * 2 + side) * 8, 8)].astype(jnp.float32).reshape(1024, 128)
+            )
+        for part in range(2):
+            for side in range(2):
+                for block in range(2):
+                    at = part * 512 + side * 256 + block * 128
+                    lines[:, pl.ds(at, 128)] = wide[
+                        pl.ds(side * 1024 + part * 2 + block, 256, stride=4), :
+                    ].astype(jnp.bfloat16)
+        both = dot(lines[...], forward_x[...]).astype(jnp.bfloat16)
+        spectrum[pl.ds(0, 256), :] = both
+        spectrum[pl.ds(256, 256), pl.ds(0, GX)] = both[:, GX:]
+        spectrum[pl.ds(256, 256), pl.ds(GX, GX)] = -both[:, :GX]
+
+        @pl.when(both_real)
+        def _():
+            first_lane = lax.broadcasted_iota(jnp.int32, (256, 128), 1) == 0
+            zero = jnp.zeros((256, 128), jnp.bfloat16)
+            edges[...] = jnp.zeros_like(edges)
+            for part in range(2):
+                mixed = spectrum[pl.ds(0, 256), pl.ds(GX + part * 256, 128)].astype(jnp.float32)
+                edge = jnp.where(first_lane, mixed, 0.0)
+                kept_part = (mixed - edge).astype(jnp.bfloat16)
+                edge = edge.astype(jnp.bfloat16)
+                spectrum[pl.ds(0, 256), pl.ds(GX + part * 256, 128)] = kept_part
+                spectrum[pl.ds(256, 256), pl.ds(part * 256, 128)] = kept_part
+                edges[pl.ds(0, 256), pl.ds(part * 128, 128)] = edge
+                edges[pl.ds(256, 256), pl.ds(256 + part * 128, 128)] = zero - edge
+
+    def block_of(block):
+        return pl.ds(pl.multiple_of(block * 128, 128), 128)
+
+    other_half, own_half = 1 - y // 2, y // 2
+    exchange.arrived(2)
+    exchange.arrived(3)
+    along_x(other_half)
+
+    def first_depth(block, carry):
+        at = block_of(block)
+        weights = forward_z[other_half, at, :]
+        depth_sum[at, :] = dot(weights, spectrum[...])
+
+        @pl.when(both_real)
+        def _():
+            edge_sum[at, :] = dot(weights, edges[...])
+
+        return carry
+
+    lax.fori_loop(0, 4, first_depth, 0)
+    exchange.spread(1)
     stay.wait()
     seven = pltpu.make_async_remote_copy(
         src_ref=g_ref.at[pl.ds(0, 7)],
@@ -387,7 +508,6 @@
         ).start()
     kept = pltpu.make_async_copy(whole_rows.at[m], e_ref.at[m], e_own)
     kept.start()
-    exchange.spread(3)
     exchange.spread(0)
     kept.wait()
     others = pltpu.make_async_remote_copy(
@@ -400,22 +520,135 @@
     )
     others.wait_send()
     others.wait_recv()
+
+    def rounded_root(rows, across_table):
+        return jnp.sqrt(scale * dot(rows, across_table)).astype(jnp.bfloat16).astype(jnp.float32)
+
+    near = jnp.concatenate([e_ref[:, part].reshape(GZ, PIX) for part in range(2)], axis=1)
+    far = dot(mirror[...], near).astype(jnp.bfloat16)
+    amplitude[...] = 0.5 * (rounded_root(near, across_x[0]) + rounded_root(far, across_x[1]))
+
+    @pl.when(both_real)
+    def _():
+        amplitude_edge[...] = 0.5 * (
+            rounded_root(near, edge_across[...]) + rounded_root(far, edge_across[...])
+        )
+
+    exchange.arrived(1)
+    exchange.arrived(0)
+    along_x(own_half)
+
+    def projection(real_z, imag_z, target):
+        inverse = lax.rsqrt(real_z * real_z + imag_z * imag_z)
+        factor = target * jnp.minimum(inverse, 1.0 / least_modulus)
+        return (real_z * factor).astype(jnp.bfloat16), (imag_z * factor).astype(jnp.bfloat16)
+
+    def along_depth(block, carry):
+        at = block_of(block)
+        below = pl.ds(pl.multiple_of(GZ + block * 128, 128), 128)
+        weights = forward_z[own_half, at, :]
+        total = depth_sum[at, :] + dot(weights, spectrum[...])
+        real, imag = projection(total[:, :GX], total[:, GX:], amplitude[at, :])
+        projected[at, pl.ds(0, GX)] = real
+        projected[at, pl.ds(GX, GX)] = imag
+        projected[below, pl.ds(0, GX)] = -imag
+        projected[below, pl.ds(GX, GX)] = real
+
+        @pl.when(both_real)
+        def _():
+            total = edge_sum[at, :] + dot(weights, edges[...])
+            real, imag = projection(total[:, :256], total[:, 256:], amplitude_edge[at, :])
+            projected_edge[at, :] = real
+            projected_edge[below, :] = -imag
+
+        return carry
+
+    lax.fori_loop(0, 4, along_depth, 0)
+
+    def back_depth(half):
+        lines[...] = dot(back_z[half], projected[...]).astype(jnp.bfloat16)
+
+        @pl.when(both_real)
+        def _():
+            first_lane = lax.broadcasted_iota(jnp.int32, (256, 128), 1) == 0
+            edge = dot(back_z[half], projected_edge[...])
+            for part in range(2):
+                at = pl.ds(GX + part * 256, 128)
+                lines[:, at] = jnp.where(
+                    first_lane,
+                    edge[:, part * 128 : part * 128 + 128],
+                    lines[:, at].astype(jnp.float32),
+                ).astype(jnp.bfloat16)
+
+    def back_x(k):
+        row = across(y, k)
+        out = dot(lines[...], back_x_table[row % 2])
+        for block in range(4):
+            stage[pl.ds(block, 256, stride=4), :] = out[:, block * 128 : block * 128 + 128]
+        x_back[row] = stage[...].astype(jnp.bfloat16).reshape(4, 8, 2, 16, 128)
+        back.start(k)
+
+    back_depth(other_half)
+    back_x(2)
+    back_x(3)
+    back_depth(own_half)
+    back_x(1)
+    back_x(0)
+
+    def along_y(half, last):
+        wide[...] = r_back[pl.ds(half * 16, 16)].astype(jnp.float32).reshape(2048, 128)
+        for plane in range(4):
+            rows = [
+                jnp.concatenate(
+                    [
+                        wide[pl.ds(plane * 4 + part * 2 + side, 128, stride=16), :]
+                        for side in range(2)
+                    ],
+                    axis=1,
+                ).astype(jnp.bfloat16)
+                for part in range(2)
+            ]
+            out = dot(back_y[half], jnp.concatenate(rows, axis=0))
+            if last:
+                final[plane] += out
+                pltpu.make_async_copy(final.at[plane], out_ref.at[plane], o_send.at[plane]).start()
+            else:
+                final[plane] = out
+
+    for k in ORDER:
+        back.spread(k)
+        if k == 1:
+            back.arrived(2)
+            back.arrived(3)
+            along_y(other_half, False)
+    back.arrived(1)
+    back.arrived(0)
+    along_y(own_half, True)
     exchange.finish()
-
-
-def forward_exchange(density, orient, sharp, images):
-    vmem = pl.BlockSpec(memory_space=pltpu.VMEM)
+    back.finish()
+    for plane in range(4):
+        pltpu.make_async_copy(final.at[plane], out_ref.at[plane], o_send.at[plane]).wait()
+
+
+def exchange_step(scale, density, orient, sharp, images):
+    far = pl.BlockSpec(memory_space=pltpu.HBM)
     bfloat, single = jnp.bfloat16, jnp.float32
     one = pltpu.SemaphoreType.DMA
+    tiles = (32, 8, 16, 128)
     return pl.pallas_call(
-        forward_kernel,
-        out_shape=[
-            jax.ShapeDtypeStruct((32, 8, 16, 128), bfloat),
-            jax.ShapeDtypeStruct((32, 2, 16, 128), bfloat),
-        ],
-        in_specs=[vmem] * 5 + [pl.BlockSpec(memory_space=pl.ANY)],
-        out_specs=[vmem] * 2,
+        functools.partial(step_kernel, scale),
+        out_shape=jax.ShapeDtypeStruct(density.shape, single),
+        in_specs=[far] * (4 + len(TABLES)),
+        out_specs=far,
         scratch_shapes=[
+            pltpu.VMEM(t.shape[1:] if i in CHOSEN else t.shape, bfloat) for i, t in enumerate(TABLES)
+        ]
+        + [
+            pltpu.VMEM((1, 64), jnp.int32),
+            pltpu.VMEM((1, 64), single),
+            pltpu.VMEM(density.shape, bfloat),
+            pltpu.VMEM(tiles, bfloat),
+            pltpu.VMEM((32, 2, 16, 128), bfloat),
             pltpu.VMEM(BLOCKS, bfloat),
             pltpu.VMEM(BLOCKS, bfloat),
             pltpu.VMEM((1024, 128), single),
@@ -428,93 +661,39 @@
             pltpu.VMEM((8, 2, 32, 128), bfloat),
             pltpu.VMEM((1024, 128), single),
             pltpu.VMEM((32, 2, 16, 128), bfloat),
-            one, one((5,)), one((5,)), one, one, one, one, one, one,
+            pltpu.VMEM(BLOCKS, bfloat),
+            pltpu.VMEM(BLOCKS, bfloat),
+            pltpu.VMEM(tiles, bfloat),
+            pltpu.VMEM((2048, 128), single),
+            pltpu.VMEM((256, 2 * GX), bfloat),
+            pltpu.VMEM((512, 2 * GX), bfloat),
+            pltpu.VMEM((512, 512), bfloat),
+            pltpu.VMEM((GZ, 2 * GX), single),
+            pltpu.VMEM((GZ, 512), single),
+            pltpu.VMEM((GZ, GX), single),
+            pltpu.VMEM((GZ, 256), single),
+            pltpu.VMEM((2 * GZ, 2 * GX), bfloat),
+            pltpu.VMEM((2 * GZ, 256), bfloat),
+            pltpu.VMEM(density.shape, single),
+            one((3,)), one((len(TABLES),)), one, one((4,)), one((5,)), one((5,)), one, one, one, one, one, one,
         ]
-        + EXCHANGE_SEMS,
+        + EXCHANGE_SEMS * 2,
         compiler_params=pltpu.CompilerParams(
-            collective_id=1, has_side_effects=True, vmem_limit_bytes=32 << 20
+            collective_id=1, has_side_effects=True, vmem_limit_bytes=50 << 20
         ),
     )(
-        density,
-        FORWARD_Y,
-        WINDOWS,
         orient.reshape(1, -1),
         sharp.reshape(1, -1),
+        density,
         images.reshape(-1, PIX),
-    )
-
-
-def amplitudes(rows, across, scale):
-    return jnp.sqrt(scale * dot(rows, across.T)).astype(jnp.bfloat16).astype(jnp.float32)
-
-
-def project(real_x, imag_x, amplitude):
-    real_z = dot(COS_Z, real_x) + dot(SIN_Z, imag_x)
-    imag_z = dot(COS_Z, imag_x) - dot(SIN_Z, real_x)
-    modulus = jnp.sqrt(real_z * real_z + imag_z * imag_z)
-    factor = amplitude / jnp.maximum(modulus, least_modulus)
-    proj_real = (real_z * factor).astype(jnp.bfloat16)
-    proj_imag = (imag_z * factor).astype(jnp.bfloat16)
-    back_real = (dot(COS_B, proj_real) - dot(SIN_B, proj_imag)).astype(jnp.bfloat16)
-    back_imag = (dot(COS_B, proj_imag) + dot(SIN_B, proj_real)).astype(jnp.bfloat16)
-    return back_real, back_imag
+        *TABLES,
+    )
 
 
 def body(images, orient, sharp, density, support):
-    depth, rows_all, width_own = density.shape
-    count = images.shape[0]
-    image_count = lax.axis_size("img")
-    slab_index = lax.axis_index("slab")
-    image_index = lax.axis_index("img")
-    scale = depth / (count * image_count)
-
-    lines, expanded = forward_exchange(density, orient, sharp, images)
-    lines = (
-        lines.reshape(2, 2, 4, 2, 8, 4, 2, 2, 128)
-        .transpose(0, 2, 3, 4, 5, 6, 1, 7, 8)
-        .reshape(GZ, 2 * GX)
-    )
-    expanded = expanded.reshape(32, 2, 16, PIX).transpose(1, 0, 2, 3).reshape(2, GZ, PIX)
-    first, second = expanded[0], expanded[1]
-    first_mirror = dot(MIRROR, first).astype(jnp.bfloat16)
-    second_mirror = dot(MIRROR, second).astype(jnp.bfloat16)
-
-    def usual(lines, first, second, first_mirror, second_mirror):
-        both = dot(lines, FORWARD_X).astype(jnp.bfloat16)
-        amplitude = 0.5 * (
-            amplitudes(first, ACROSS_X, scale) + amplitudes(second_mirror, ACROSS_X_MIRROR, scale)
-        )
-        back_real, back_imag = project(both[:, :GX], both[:, GX:], amplitude)
-        return dot(jnp.concatenate([back_real, back_imag], axis=1), BACK_X).astype(jnp.bfloat16)
-
-    def real_rows(lines, first, second, first_mirror, second_mirror):
-        out = []
-        for part, near, far in ((0, first, first_mirror), (1, second, second_mirror)):
-            line = lines[:, part * GX : (part + 1) * GX]
-            both = dot(line, FORWARD_X[:GX]).astype(jnp.bfloat16)
-            amplitude = 0.5 * (
-                amplitudes(near, ACROSS_X, scale) + amplitudes(far, ACROSS_X_MIRROR, scale)
-            )
-            back_real, back_imag = project(both[:, :GX], both[:, GX:], amplitude)
-            out.append(
-                dot(jnp.concatenate([back_real, back_imag], axis=1), BACK_X[:, :GX]).astype(
-                    jnp.bfloat16
-                )
-            )
-        return jnp.concatenate(out, axis=1)
-
-    special = jnp.logical_and(slab_index == 0, image_index == 0)
-    out = lax.cond(
-        special, real_rows, usual, lines, first, second, first_mirror, second_mirror
-    )
-    blocks = out.reshape(2, 4, 8, 2, depth, 2, 2, 2, 128).transpose(0, 6, 1, 2, 3, 4, 5, 7, 8)
-    out = back_exchange(blocks.reshape(BLOCKS))
-    projected = jnp.einsum(
-        "cyj,jzchl->zyhl",
-        BACK_Y,
-        out.reshape(HALF, depth, 2, 2, 128),
-        preferred_element_type=jnp.float32,
-    ).reshape(depth, GY, width_own)
+    depth = density.shape[0]
+    scale = depth / (images.shape[0] * lax.axis_size("img"))
+    projected = exchange_step(scale, density, orient, sharp, images)
     previous = density.astype(jnp.float32)
     return jnp.where(support == 1, projected, previous - feedback * projected)
 

time: 129 us -> 103 us (0.80)
  the two profiles are of different devices: /device:TPU:105 before, /device:TPU:1 now
where the time goes in v4:
time: 103 us
  Pallas kernels  90.9 us (88%)
  local copies, waits for them, and re-layouts  8.55 us (8%)
  other arithmetic  3.4 us (3%)
    pallas_call x1, Pallas kernels, exchange_step(): pl.pallas_call(functools.partial(step_kernel, scale), out_shape=jax.Shape...  90.9 us
    unnamed x20, local copies, waits for them, and re-layouts  8.55 us
    select_n x1, other arithmetic, body(): return jnp.where(support == 1, projected, previous - feedback * projected)  3.4 us

profile of v4, /device:TPU:1, one launch (start us, length us, event | category | flops | bytes accessed | tf_op | source)
XLA Modules:
  0.0 102.8 jit_solution(1052646345595871456)
XLA Ops:
  0.0 0.0 copy-start
  0.0 1.2 %copy-done = bf16[4,512,256]{2,1,0:T(8,128)(2,1)S(1)} copy-done((bf16[4,512,256]{2,1,0:T(8,128)(2,1)S(1)}, bf16[4,512,256]{2,1,0:T(8,128)(2,1)}, u32[]{:S(2)}) %copy-start) | copy-done | bytes 1048600
  1.2 0.0 copy-start.1
  1.2 1.2 %copy-done.1 = bf16[2,512,512]{2,1,0:T(8,128)(2,1)S(1)} copy-done((bf16[2,512,512]{2,1,0:T(8,128)(2,1)S(1)}, bf16[2,512,512]{2,1,0:T(8,128)(2,1)}, u32[]{:S(2)}) %copy-start.1) | copy-done | bytes 1048600
  2.5 0.0 copy-start.2
  2.5 1.0 %copy-done.2 = bf16[2,512,256]{2,1,0:T(8,128)(2,1)S(1)} copy-done((bf16[2,512,256]{2,1,0:T(8,128)(2,1)S(1)}, bf16[2,512,256]{2,1,0:T(8,128)(2,1)}, u32[]{:S(2)}) %copy-start.2) | copy-done | bytes 524312
  3.5 0.0 copy-start.3
  3.5 1.0 %copy-done.3 = bf16[512,512]{1,0:T(8,128)(2,1)S(1)} copy-done((bf16[512,512]{1,0:T(8,128)(2,1)S(1)}, bf16[512,512]{1,0:T(8,128)(2,1)}, u32[]{:S(2)}) %copy-start.3) | copy-done | bytes 524312
  4.5 0.0 copy-start.4
  4.5 1.0 %copy-done.4 = bf16[4,128,512]{2,1,0:T(8,128)(2,1)S(1)} copy-done((bf16[4,128,512]{2,1,0:T(8,128)(2,1)S(1)}, bf16[4,128,512]{2,1,0:T(8,128)(2,1)}, u32[]{:S(2)}) %copy-start.4) | copy-done | bytes 524312
  5.6 0.0 copy-start.5
  5.6 0.9 copy-done.5
  6.5 0.0 copy-start.6
  6.5 0.8 copy-done.6
  7.2 0.0 copy-start.7
  7.2 0.7 copy-done.7
  7.9 0.0 copy-start.8
  7.9 0.7 copy-done.8
  8.6 0.0 copy-start.9
  8.6 90.9 %shard_map.145 = f32[4,512,256]{2,1,0:T(8,128)} custom-call(s32[1,64]{1,0:T(1,128)S(1)} %bitcast.3, f32[1,64]{1,0:T(1,128)S(1)} %bitcast.4, bf16[4,512,256]{2,1,0:T(8,128)(2,1)S(1)} %copy-done, f32[8192,128]{1,0:T(8,128)} %bitcast.5, bf16[4,128,512]{2,1,0:T(8,128)(2,1)S(1)} %copy-done.4, bf16[2,64,32]{2,1,0:T(8,128)(2,1)S(1)} %copy-done.6, ...), custom_call_target="tpu_custom_call" | custom-call | tf_op jit(solution)/shard_map/pallas_call | solution.py:638
  99.4 0.0 copy-done.9
  99.4 3.4 %subtract_select_fusion = f32[4,512,256]{2,1,0:T(8,128)} fusion(f32[4,512,256]{2,1,0:T(8,128)} %shard_map.145, bf16[4,512,256]{2,1,0:T(8,128)(2,1)S(1)} %copy-done, s32[4,512,256]{2,1,0:T(8,128)S(1)} %copy-done.9), kind=kLoop, calls=%fused_computation | loop fusion | flops 2621440 | bytes 7340032 | tf_op jit(solution)/shard_map/jit(_where)/select_n | solution.py:698
Async XLA Ops:
  0.0 1.2 %copy-start = (bf16[4,512,256]{2,1,0:T(8,128)(2,1)S(1)}, bf16[4,512,256]{2,1,0:T(8,128)(2,1)}, u32[]{:S(2)}) copy-start(bf16[4,512,256]{2,1,0:T(8,128)(2,1)} %density_in.1) | copy-start | bytes 3145732
  1.2 1.2 %copy-start.1 = (bf16[2,512,512]{2,1,0:T(8,128)(2,1)S(1)}, bf16[2,512,512]{2,1,0:T(8,128)(2,1)}, u32[]{:S(2)}) copy-start(bf16[2,512,512]{2,1,0:T(8,128)(2,1)} %constant.27.clone.rest_3_) | copy-start | bytes 3145732
  2.5 1.0 %copy-start.2 = (bf16[2,512,256]{2,1,0:T(8,128)(2,1)S(1)}, bf16[2,512,256]{2,1,0:T(8,128)(2,1)}, u32[]{:S(2)}) copy-start(bf16[2,512,256]{2,1,0:T(8,128)(2,1)} %constant.33.clone.rest_9_) | copy-start | bytes 1572868
  3.5 1.0 %copy-start.3 = (bf16[512,512]{1,0:T(8,128)(2,1)S(1)}, bf16[512,512]{1,0:T(8,128)(2,1)}, u32[]{:S(2)}) copy-start(bf16[512,512]{1,0:T(8,128)(2,1)} %constant.28.clone.rest_4_) | copy-start | bytes 1572868
  4.5 1.0 %copy-start.4 = (bf16[4,128,512]{2,1,0:T(8,128)(2,1)S(1)}, bf16[4,128,512]{2,1,0:T(8,128)(2,1)}, u32[]{:S(2)}) copy-start(bf16[4,128,512]{2,1,0:T(8,128)(2,1)} %constant.24.clone.rest_0_) | copy-start | bytes 1572868
  5.6 0.9 copy-start.5
  6.5 0.8 copy-start.6
  7.2 0.7 copy-start.7
  7.9 0.7 copy-start.8
  8.6 90.9 %copy-start.9 = (s32[4,512,256]{2,1,0:T(8,128)S(1)}, s32[4,512,256]{2,1,0:T(8,128)}, u32[]{:S(2)}) copy-start(s32[4,512,256]{2,1,0:T(8,128)} %param.19) | copy-start | bytes 6291460

commit v5 on v4

--- a/solution.py
+++ b/solution.py
@@ -265,7 +265,7 @@
 CHOSEN = (2, 5, 8)
 
 
-def step_kernel(scale, orient_in, sharp_in, density_in, images, *rest):
+def step_kernel(scale, orient_in, sharp_in, density_in, images, support_in, *rest):
     count = len(TABLES)
     sources, out_ref, rest = rest[:count], rest[count], rest[count + 1 :]
     tables, rest = rest[:count], rest[count:]
@@ -274,7 +274,7 @@
         x_ref, a_ref, stage, held, parts, sent, got, padded, g_ref, h_ref, made, whole_rows,
         x_back, a_back, r_back, wide, lines, spectrum, edges, depth_sum, edge_sum, amplitude, amplitude_edge,
         projected, projected_edge, final,
-        d_load, t_load, load, o_send, c_send, c_recv, g_send, g_recv, g_own, e_send, e_recv, e_own, *sems,
+        support, d_load, t_load, load, o_send, c_send, c_recv, g_send, g_recv, g_own, e_send, e_recv, e_own, *sems,
     ) = rest
     (
         table, windows, forward_x, forward_z, mirror, across_x, edge_across, back_z, back_x_table, back_y,
@@ -307,6 +307,7 @@
     for fill in first_fills:
         fill.start()
     fetch.start()
+    fills.append(pltpu.make_async_copy(support_in, support, d_load.at[3]))
     for fill in fills[1:]:
         fill.start()
     exchange = Exchange(x_ref, a_ref, r_ref, sems[:6])
@@ -328,10 +329,8 @@
     transform(2)
     entered()
     exchange.start(2)
-    for k in (3, 1):
-        transform(k)
-        exchange.start(k)
-    transform(0)
+    transform(3)
+    exchange.start(3)
 
     near = orient[...] - slab * 4
     steps = lax.broadcasted_iota(jnp.int32, (16, 64), 0) - 4 - near
@@ -368,8 +367,9 @@
         parts[pl.ds(at + 1, 16, stride=128), :] = out[:, 128:]
         return carry
 
-    lax.fori_loop(0, 64, mix, 0)
+    lax.fori_loop(0, 64, mix, 0, unroll=8)
     sent[...] = parts[...].astype(jnp.bfloat16).reshape(16, 128, 128)
+
 
     def gift(index, shift, turn):
         first = 4 + 4 * shift + 2 * ((image + turn) % 2)
@@ -385,6 +385,9 @@
     gifts = [gift(index, *move) for index, move in enumerate(moves)]
     for copy in gifts:
         copy.start()
+    transform(1)
+    exchange.start(1)
+    transform(0)
     exchange.spread(2)
     for copy in gifts:
         copy.wait()
@@ -610,7 +613,9 @@
             ]
             out = dot(back_y[half], jnp.concatenate(rows, axis=0))
             if last:
-                final[plane] += out
+                out = final[plane] + out
+                previous = density[plane].astype(jnp.float32)
+                final[plane] = jnp.where(support[plane] == 1, out, previous - feedback * out)
                 pltpu.make_async_copy(final.at[plane], out_ref.at[plane], o_send.at[plane]).start()
             else:
                 final[plane] = out
@@ -630,7 +635,7 @@
         pltpu.make_async_copy(final.at[plane], out_ref.at[plane], o_send.at[plane]).wait()
 
 
-def exchange_step(scale, density, orient, sharp, images):
+def exchange_step(scale, density, orient, sharp, images, support):
     far = pl.BlockSpec(memory_space=pltpu.HBM)
     bfloat, single = jnp.bfloat16, jnp.float32
     one = pltpu.SemaphoreType.DMA
@@ -638,7 +643,7 @@
     return pl.pallas_call(
         functools.partial(step_kernel, scale),
         out_shape=jax.ShapeDtypeStruct(density.shape, single),
-        in_specs=[far] * (4 + len(TABLES)),
+        in_specs=[far] * (5 + len(TABLES)),
         out_specs=far,
         scratch_shapes=[
             pltpu.VMEM(t.shape[1:] if i in CHOSEN else t.shape, bfloat) for i, t in enumerate(TABLES)
@@ -675,17 +680,19 @@
             pltpu.VMEM((2 * GZ, 2 * GX), bfloat),
             pltpu.VMEM((2 * GZ, 256), bfloat),
             pltpu.VMEM(density.shape, single),
-            one((3,)), one((len(TABLES),)), one, one((4,)), one((5,)), one((5,)), one, one, one, one, one, one,
+            pltpu.VMEM(density.shape, jnp.int32),
+            one((4,)), one((len(TABLES),)), one, one((4,)), one((5,)), one((5,)), one, one, one, one, one, one,
         ]
         + EXCHANGE_SEMS * 2,
         compiler_params=pltpu.CompilerParams(
-            collective_id=1, has_side_effects=True, vmem_limit_bytes=50 << 20
+            collective_id=1, has_side_effects=True, vmem_limit_bytes=63 << 20
         ),
     )(
         orient.reshape(1, -1),
         sharp.reshape(1, -1),
         density,
         images.reshape(-1, PIX),
+        support,
         *TABLES,
     )
 
@@ -693,9 +700,7 @@
 def body(images, orient, sharp, density, support):
     depth = density.shape[0]
     scale = depth / (images.shape[0] * lax.axis_size("img"))
-    projected = exchange_step(scale, density, orient, sharp, images)
-    previous = density.astype(jnp.float32)
-    return jnp.where(support == 1, projected, previous - feedback * projected)
+    return exchange_step(scale, density, orient, sharp, images, support)
 
 
 def solution(mesh):

time: 103 us -> 90 us (0.87)
  local copies, waits for them, and re-layouts: 8.55 us -> 3.05 us
  Pallas kernels: 90.9 us -> 86.8 us
  other arithmetic: 3.4 us -> 0 us
    unnamed x20 -> x1, local copies, waits for them, and re-layouts: 8.55 us -> 3.05 us
    pallas_call x1, Pallas kernels: 90.9 us -> 86.8 us  [exchange_step(): pl.pallas_call(functools.partial(step_kernel, scale), out_shape=jax.Shape...]
    select_n x1 -> x0, other arithmetic: 3.4 us -> none  [body(): return jnp.where(support == 1, projected, previous - feedback * projected)]
where the time goes in v5:
time: 90 us; the launch traced here: 89.9 us
  Pallas kernels  86.8 us (96%)
  local copies, waits for them, and re-layouts  3.05 us (3%)
    pallas_call x1, Pallas kernels, exchange_step(): pl.pallas_call(functools.partial(step_kernel, scale), out_shape=jax.Shape...  86.8 us
    unnamed x1, local copies, waits for them, and re-layouts  3.05 us

profile of v5, /device:TPU:1, one launch (start us, length us, event | category | flops | bytes accessed | tf_op | source)
XLA Modules:
  0.0 89.9 jit_solution(12599271452263508918)
XLA Ops:
  0.0 86.8 %shard_map.145 = f32[4,512,256]{2,1,0:T(8,128)} custom-call(s32[1,64]{1,0:T(1,128)} %bitcast.4, f32[1,64]{1,0:T(1,128)} %bitcast.5, bf16[4,512,256]{2,1,0:T(8,128)(2,1)} %density_in.1, f32[8192,128]{1,0:T(8,128)} %bitcast.3, s32[4,512,256]{2,1,0:T(8,128)} %support_in.1, bf16[4,128,512]{2,1,0:T(8,128)(2,1)} %constant.20.clone.rest_0_, ...), custom_call_target="tpu_custom_call" | custom-call | tf_op jit(solution)/shard_map/pallas_call | solution.py:643
  86.8 3.0 %copy.17 = f32[4,512,256]{2,1,0:T(8,128)} copy(f32[4,512,256]{2,1,0:T(8,128)} %shard_map.145) | data formatting | bytes 4194304

commit v6 on v2

v6 whole, which is shorter than its diff:
```python
import functools
import math

import jax
import jax.numpy as jnp
import ml_dtypes
import numpy as np
from jax import lax
from jax.experimental import pallas as pl
from jax.experimental.pallas import tpu as pltpu
from jax.sharding import PartitionSpec as P

GZ = 512
GY = 512
GX = 512
PIX = 128

least_modulus = 0.5
feedback = 0.9


def dft_tables(length):
    index = np.arange(length, dtype=np.int64)
    product = (index[:, None] * index[None, :]) % length
    angles = product.astype(np.float32) * np.float32(2.0 * math.pi / length)
    factor = np.float32(1.0 / math.sqrt(length))
    return (
        (np.cos(angles) * factor).astype(ml_dtypes.bfloat16),
        (np.sin(angles) * factor).astype(ml_dtypes.bfloat16),
    )


def interpolation(cells, pixels):
    grid = np.arange(cells, dtype=np.float32)
    detector = np.arange(pixels, dtype=np.float32)
    position = (grid + np.float32(0.5)) * np.float32(pixels / cells) - np.float32(0.5)
    return np.maximum(
        np.float32(0.0), np.float32(1.0) - np.abs(position[:, None] - detector[None, :])
    )


def bf(table):
    return np.asarray(table).astype(ml_dtypes.bfloat16)


COS, SIN = dft_tables(GY)
HALF = GY // 2
_y, _x, _z, _s = np.meshgrid(np.arange(4), np.arange(4), np.arange(8), np.arange(2), indexing="ij")
ROW_OF = 32 * _z + 8 * _y + 2 * _x + _s
_imag = np.concatenate([COS[HALF : HALF + 1], -SIN[1:HALF]])
FORWARD_Y = np.stack(
    [
        [
            np.concatenate([t[ROW_OF[2 * h : 2 * h + 2, :, :, e].reshape(-1)] for t in (COS, _imag)])
            for h in range(2)
        ]
        for e in range(2)
    ]
)
_two = 2.0 * COS[:, :HALF].astype(np.float32)
_two[:, 0] = COS[:, 0]
_sin = -2.0 * SIN[:, :HALF].astype(np.float32)
_sin[:, 0] = COS[:, HALF]
BACK_Y = np.concatenate(
    [
        bf(t.reshape(GY, 8, 16, 2).transpose(3, 0, 2, 1).reshape(2, GY, 128))
        for t in (_two, _sin)
    ],
    axis=2,
)


def quarters(upper_left, upper_right, lower_left, lower_right):
    return np.concatenate(
        [
            np.concatenate([upper_left, upper_right], axis=1),
            np.concatenate([lower_left, lower_right], axis=1),
        ],
        axis=0,
    )


FORWARD_X = np.zeros((2, 2 * GX, 2 * GX), ml_dtypes.bfloat16)
BACK_X = np.zeros((2, 2, 2 * GX, GX), ml_dtypes.bfloat16)
_low = GX // 2
_pair = np.where(np.arange(_low) == 0, 1.0, 2.0)[:, None]
_in = -SIN[:, :_low]
_in[:, 0] = COS[:, _low]
_out_re = bf(COS[:_low].astype(np.float32) * _pair)
_out_im = bf(-SIN[:_low].astype(np.float32) * _pair)
_out_im[0] = COS[_low]
for _e in range(2):
    _half = slice(_e * _low, (_e + 1) * _low)
    _place = slice(_e * GX, (_e + 1) * GX)
    FORWARD_X[0, :, _place] = quarters(COS[:, _half], -SIN[:, _half], SIN[:, _half], COS[:, _half])
    FORWARD_X[1, _place, _place] = np.concatenate([COS[:, :_low], _in], axis=1)
    for _side in range(2):
        _to = slice(_side * _low, (_side + 1) * _low)
        _cos, _sine = COS[_half, _to], SIN[_half, _to]
        BACK_X[0, _side, _place] = quarters(_cos, _sine, -_sine, _cos)
        BACK_X[1, _side, _place, _half] = np.concatenate([_out_re[:, _to], _out_im[:, _to]])
_across = interpolation(GY, PIX)
_mirror = (-np.arange(GY)) % GY
ACROSS_X = np.zeros((4, 2, 2 * PIX, _low), np.float32)
EDGE_ACROSS = np.zeros((2, 2 * PIX, PIX), np.float32)
for _e in range(2):
    _half, _rows = slice(_e * _low, (_e + 1) * _low), slice(_e * PIX, (_e + 1) * PIX)
    ACROSS_X[_e, 0, :PIX] = _across[_half].T
    ACROSS_X[_e, 1, PIX:] = _across[_mirror][_half].T
    ACROSS_X[2 + _e, 0, _rows] = _across[:_low].T
    ACROSS_X[2 + _e, 1, _rows] = _across[_mirror][:_low].T
    EDGE_ACROSS[_e, _rows, 0] = _across[_low]
ACROSS_X, EDGE_ACROSS = bf(ACROSS_X), bf(EDGE_ACROSS)
_yh, _xx, _cc, _zz, _z4 = np.meshgrid(
    np.arange(2), np.arange(4), np.arange(2), np.arange(8), np.arange(4), indexing="ij"
)
Z_ORDER = (4 * (64 * _yh + 16 * _xx + 2 * _zz + _cc) + _z4).reshape(-1)
_yh, _yl, _xx, _cc, _zz, _p2 = np.meshgrid(
    np.arange(2), np.arange(2), np.arange(4), np.arange(2), np.arange(8), np.arange(2), indexing="ij"
)
K_ORDER = (4 * (64 * _yh + 16 * _xx + 2 * _zz + _cc) + 2 * _yl + _p2).reshape(-1)
FORWARD_Z = np.concatenate([t[K_ORDER][:, Z_ORDER] for t in (COS, SIN)], axis=1)
BACK_Z = np.concatenate([COS[:, K_ORDER], SIN[:, K_ORDER]], axis=1).reshape(2, 256, 2 * GZ)
MIRROR = bf(K_ORDER[None, :] == _mirror[K_ORDER][:, None])
WINDOWS = np.zeros((2, 32, 2, 2, 16), np.float32)
for _m in range(32):
    for _r in range(16):
        WINDOWS[:, _m, 0, 0, _r] = max(0.0, 1.0 - abs(_m / 4 + 3.625 - _r))
        WINDOWS[:, _m, 1, 1, _r] = max(0.0, 1.0 - abs(11.625 - _m / 4 - _r))
WINDOWS[1, 0, 1, 1, :] = 0.0
WINDOWS[1, 0, 1, 1, 0:2] = (0.375, 0.625)
WINDOWS = bf(WINDOWS.reshape(2, 64, 32))

MESH = pl.DeviceIdType.MESH


def dot(first, second):
    return jnp.dot(first, second, preferred_element_type=jnp.float32)


def place():
    slab = lax.axis_index("slab")
    return (slab // 64) * 2 + lax.axis_index("img"), (slab // 16) % 4, (slab // 2) % 8, slab % 2


def device(y, x, z, c):
    return (y % 2, (y // 2) * 64 + x * 16 + z * 2 + c)


def greet(others):
    barrier = pltpu.get_barrier_semaphore()
    for other in others:
        pl.semaphore_signal(barrier, inc=1, device_id=other, device_id_type=MESH)
    return lambda: pl.semaphore_wait(barrier, len(others))


def across(y, k):
    return (y, y + 1 - 2 * (y % 2), (y + 2) % 4, 3 - y)[k]


class Exchange:
    def __init__(self, x_ref, a_ref, r_ref, sems):
        self.x_ref, self.a_ref, self.r_ref = x_ref, a_ref, r_ref
        self.local, self.z_send, self.z_recv, self.p_send, self.p_recv, self.own = sems
        self.y, self.x, self.z, self.c = place()
        self.within = self.c == self.y // 2

    def move(self, source, target, send, recv, where):
        return pltpu.make_async_remote_copy(
            src_ref=source,
            dst_ref=target,
            send_sem=send,
            recv_sem=recv,
            device_id=device(*where),
            device_id_type=MESH,
        )

    def start(self, part, k):
        row, index = self.row(k), part * self.parts + k
        for step in (4, 1, 7, 2, 6, 3, 5):
            depth = (self.z + step) % 8
            self.move(
                self.x_ref.at[part, row, :, depth],
                self.a_ref.at[part, row, :, self.z],
                self.z_send.at[index],
                self.z_recv.at[index],
                (self.y, self.x, depth, self.c),
            ).start()
        self.keep(part, k).start()

    def keep(self, part, k):
        row = self.row(k)
        return pltpu.make_async_copy(
            self.x_ref.at[part, row, :, self.z],
            self.a_ref.at[part, row, :, self.z],
            self.local.at[part * self.parts + k],
        )

    def whole(self, part, k):
        row, index = self.row(k), part * self.parts + k
        return self.move(
            self.x_ref.at[part, row, :, pl.ds(0, 7)],
            self.a_ref.at[part, row, :, pl.ds(0, 7)],
            self.z_send.at[index],
            self.z_recv.at[index],
            (self.y, self.x, (self.z + 1) % 8, self.c),
        )

    def spread(self, part, k):
        self.keep(part, k).wait()
        self.whole(part, k).wait_recv()
        for source, where, mine in self.targets(part, k):
            target = self.r_ref.at[part, self.slot()]
            copy = self.move(source, target, self.p_send, self.p_recv.at[part], where)
            if mine:
                pl.when(self.within)(pltpu.make_async_copy(source, target, self.own.at[part]).start)
                pl.when(jnp.logical_not(self.within))(copy.start)
            else:
                copy.start()

    def blocks(self, part, count):
        piece = self.r_ref.at[part, pl.ds(0, count)]
        where = (self.y, self.x, (self.z + 1) % 8, self.c)
        return self.move(piece, piece, self.p_send, self.p_recv.at[part], where)

    def arrived(self, part):
        @pl.when(self.within)
        def _():
            source = self.r_ref.at[part, 0]
            pltpu.make_async_copy(source, self.r_ref.at[part, self.slot()], self.own.at[part]).wait()
            self.blocks(part, 15).wait_recv()

        @pl.when(jnp.logical_not(self.within))
        def _():
            self.blocks(part, 16).wait_recv()

    def finish(self):
        for part in range(2):
            for k in range(self.parts):
                self.whole(part, k).wait_send()

            @pl.when(self.within)
            def _():
                self.blocks(part, 15).wait_send()

            @pl.when(jnp.logical_not(self.within))
            def _():
                self.blocks(part, 16).wait_send()


class Forward(Exchange):
    parts = 4

    def row(self, k):
        return across(self.y, k)

    def slot(self):
        return (self.y % 2 * 4 + self.x) * 2 + self.c

    def targets(self, part, k):
        row = self.row(k)
        for dx in (2, 1, 3, 0):
            column = (self.x + dx) % 4
            where = (row, column, self.z, self.y // 2)
            yield self.a_ref.at[part, row, column], where, k == 0 and dx == 0


class Back(Exchange):
    parts = 2

    def row(self, k):
        return (self.y + k) % 2

    def slot(self):
        return self.y * 4 + self.x

    def targets(self, part, k):
        row = self.row(k)
        for dx in (2, 1, 3, 0):
            for dc in (0, 1):
                column, core = (self.x + dx) % 4, (self.c + dc) % 2
                where = (2 * self.c + row, column, self.z, core)
                yield self.a_ref.at[part, row, column, :, core], where, (k, dx, dc) == (0, 0, 0)


def exchange_sems(parts):
    one = pltpu.SemaphoreType.DMA
    return [one((2 * parts,)), one((2 * parts,)), one((2 * parts,)), one, one((2,)), one((2,))]


FORWARD_TILES = (2, 4, 4, 8, 16, 128)
BACK_TILES = (2, 2, 4, 8, 2, 16, 128)
LANDED_TILES = (2, 16, 8, 16, 128)
ORDER = (2, 3, 1, 0)


def partners():
    y, x, z, c = place()
    return [device(y, x, (z + d) % 8, c) for d in range(1, 8)] + [
        device((y + d // 8) % 4, (x + d // 2 % 4) % 4, z, (c + d) % 2) for d in range(1, 32)
    ]


TABLES = (
    FORWARD_Y, WINDOWS, FORWARD_X, FORWARD_Z, MIRROR, ACROSS_X, EDGE_ACROSS, BACK_Z, BACK_X, BACK_Y,
)
BY_SET, BY_SET_AND_CORE, BY_CORE = (2, 8), (5,), (6,)


def held_shape(index, table):
    if index in BY_SET + BY_SET_AND_CORE:
        return (2,) + table.shape[1:]
    return table.shape[1:] if index in BY_CORE else table.shape


def step_kernel(scale, orient_in, sharp_in, density_in, images, support_in, *rest):
    count = len(TABLES)
    sources, out_ref, rest = rest[:count], rest[count], rest[count + 1 :]
    tables, rest = rest[:count], rest[count:]
    (
        orient, sharp, density, r_ref, e_ref,
        x_ref, a_ref, stage, held, parts, sent, got, padded, g_ref, h_ref, made, whole_rows,
        x_back, a_back, r_back, wide, lines, halves, landed, spectrum, edges, amplitude, amplitude_edge,
        projected, projected_edge, half_out, half_in, final,
        support, d_load, t_load, load, o_send, c_send, c_recv, g_send, g_recv, g_own, e_send, e_recv, e_own,
        x_send, x_recv, *sems,
    ) = rest
    (
        table, windows, forward_x, forward_z, mirror, across_x, edge_across, back_z, back_x_table, back_y,
    ) = tables
    y, x, z, c = place()
    image = lax.axis_index("img")
    slab = lax.axis_index("slab")
    m = (y * 4 + x) * 2 + c
    special = jnp.where(slab // 2 + image == 0, 1, 0)
    both_real = special == 1

    def beside(shift, turn):
        return ((image + turn) % 2, (slab + shift + 128) % 128)

    moves = [(shift, turn) for shift in (-1, 0, 1) for turn in (0, 1) if (shift, turn) != (0, 0)]
    entered = greet(partners() + [beside(*move) for move in moves])
    fills = []

    def fill(source, target):
        fills.append(pltpu.make_async_copy(source, target, t_load.at[len(fills)]))

    for index, (source, target) in enumerate(zip(sources, tables)):
        if index in BY_SET:
            fill(source.at[special], target.at[0])
            fill(source.at[0], target.at[1])
        elif index in BY_SET_AND_CORE:
            fill(source.at[special * 2 + c], target.at[0])
            fill(source.at[c], target.at[1])
        else:
            fill(source.at[c] if index in BY_CORE else source, target)
    first_fills = [
        fills[0],
        pltpu.make_async_copy(density_in, density, d_load.at[0]),
        pltpu.make_async_copy(orient_in, orient, d_load.at[1]),
        pltpu.make_async_copy(sharp_in, sharp, d_load.at[2]),
    ]
    fetch = pltpu.make_async_copy(images, held, load)
    for fill in first_fills:
        fill.start()
    fetch.start()
    fills.append(pltpu.make_async_copy(support_in, support, d_load.at[3]))
    for fill in fills[1:]:
        fill.start()
    forward = Forward(x_ref, a_ref, r_ref, sems[:6])
    back = Back(x_back, a_back, r_back, sems[6:])
    for fill in first_fills:
        fill.wait()

    def transform(part, half):
        for plane in range(4):
            out = dot(table[part, half], density[plane])
            for piece in range(2):
                for side in range(2):
                    stage[pl.ds(plane * 4 + piece * 2 + side, 64, stride=16), :] = out[
                        piece * 64 : piece * 64 + 64, side * 128 : side * 128 + 128
                    ]
        x_ref[part, pl.ds(half * 2, 2)] = stage[...].astype(jnp.bfloat16).reshape(2, 4, 8, 16, 128)

    other_half, own_half = 1 - y // 2, y // 2
    transform(0, other_half)
    entered()
    forward.start(0, 2)
    forward.start(0, 3)

    near = orient[...] - slab * 4
    steps = lax.broadcasted_iota(jnp.int32, (16, 64), 0) - 4 - near
    squares = (steps * steps).astype(jnp.float32)
    raw = jnp.exp(-sharp[...] * squares)
    total = 1.0 + 2.0 * (
        jnp.exp(-sharp[...])
        + jnp.exp(-4.0 * sharp[...])
        + jnp.exp(-9.0 * sharp[...])
        + jnp.exp(-16.0 * sharp[...])
    )
    mixing = jnp.where(jnp.abs(steps) <= 4, raw / total, 0.0)
    high = mixing.astype(jnp.bfloat16)
    low = (mixing - high.astype(jnp.float32)).astype(jnp.bfloat16)
    factors = jnp.concatenate(
        [
            jnp.concatenate([high, high], axis=1),
            jnp.concatenate([low, jnp.zeros_like(low)], axis=1),
        ],
        axis=0,
    )
    fetch.wait()

    def mix(index, carry):
        at = index * 2
        rows = jnp.concatenate(
            [held[pl.ds(at, 64, stride=128), :], held[pl.ds(at + 1, 64, stride=128), :]], axis=1
        )
        upper = rows.astype(jnp.bfloat16)
        lower = (rows - upper.astype(jnp.float32)).astype(jnp.bfloat16)
        out = dot(factors, jnp.concatenate([upper, lower], axis=0))
        out = out[:16] + out[16:]
        parts[pl.ds(at, 16, stride=128), :] = out[:, :128]
        parts[pl.ds(at + 1, 16, stride=128), :] = out[:, 128:]
        return carry

    lax.fori_loop(0, 64, mix, 0, unroll=8)
    sent[...] = parts[...].astype(jnp.bfloat16).reshape(16, 128, 128)


    def gift(index, shift, turn):
        first = 4 + 4 * shift + 2 * ((image + turn) % 2)
        return pltpu.make_async_remote_copy(
            src_ref=sent.at[pl.ds(first, 2)],
            dst_ref=got.at[index],
            send_sem=c_send.at[index],
            recv_sem=c_recv.at[index],
            device_id=beside(shift, turn),
            device_id_type=MESH,
        )

    gifts = [gift(index, *move) for index, move in enumerate(moves)]
    for copy in gifts:
        copy.start()
    transform(0, own_half)
    forward.start(0, 1)
    forward.start(0, 0)
    transform(1, other_half)
    transform(1, own_half)
    forward.spread(0, 2)
    for copy in gifts:
        copy.wait()
    padded[...] = jnp.zeros_like(padded)
    for plane in range(2):
        own = sent[4 + 2 * image + plane].astype(jnp.float32)
        for index, (shift, turn) in enumerate(moves):
            piece = got[index, plane].astype(jnp.float32)
            if shift:
                source = slab - shift
                piece = jnp.where(jnp.logical_and(source >= 0, source < 128), piece, 0.0)
            own = own + piece
        padded[plane, pl.ds(16, 128), :] = own
        for depth in range(8):
            g_ref[depth, plane, pl.ds(0, 16), :] = padded[
                plane, pl.ds(16 + 8 * depth - 4, 16), :
            ].astype(jnp.bfloat16)
            mirrored = padded[plane, pl.ds(16 + 116 - 8 * depth, 16), :]
            if depth == 0:
                mirrored = jnp.concatenate([own[63:65], mirrored[2:]], axis=0)
            g_ref[depth, plane, pl.ds(16, 16), :] = mirrored.astype(jnp.bfloat16)

    def window(step):
        depth = (z + step) % 8
        return pltpu.make_async_remote_copy(
            src_ref=g_ref.at[depth],
            dst_ref=h_ref.at[z],
            send_sem=g_send,
            recv_sem=g_recv,
            device_id=device(y, x, depth, c),
            device_id_type=MESH,
        )

    for step in (4, 1, 7, 2, 6, 3, 5):
        window(step).start()
    stay = pltpu.make_async_copy(g_ref.at[z], h_ref.at[z], g_own)
    stay.start()
    for k in ORDER:
        forward.start(1, k)
    forward.spread(0, 3)
    for fill in fills[1:]:
        fill.wait()
    forward.spread(0, 1)
    forward.spread(0, 0)
    stay.wait()
    seven = pltpu.make_async_remote_copy(
        src_ref=g_ref.at[pl.ds(0, 7)],
        dst_ref=h_ref.at[pl.ds(0, 7)],
        send_sem=g_send,
        recv_sem=g_recv,
        device_id=device(y, x, (z + 1) % 8, c),
        device_id_type=MESH,
    )
    seven.wait_send()
    seven.wait_recv()
    weights = windows[jnp.where(z == 0, 1, 0)]
    for source in range(8):
        for plane in range(2):
            made[pl.ds(source * 2 + plane, 64, stride=16), :] = dot(weights, h_ref[source, plane])
    whole_rows[...] = made[...].astype(jnp.bfloat16).reshape(16, 2, 2, 16, 128)
    for d in range(1, 32):
        row, column, core = (y + d // 8) % 4, (x + d // 2 % 4) % 4, (c + d) % 2
        pltpu.make_async_remote_copy(
            src_ref=whole_rows.at[row * 4 + column],
            dst_ref=e_ref.at[m],
            send_sem=e_send,
            recv_sem=e_recv,
            device_id=device(row, column, z, core),
            device_id_type=MESH,
        ).start()
    kept = pltpu.make_async_copy(whole_rows.at[y * 4 + x], e_ref.at[m], e_own)
    kept.start()

    def cross(index, source, target):
        return pltpu.make_async_remote_copy(
            src_ref=source,
            dst_ref=target,
            send_sem=x_send.at[index],
            recv_sem=x_recv.at[index],
            device_id=device(y, x, z, 1 - c),
            device_id_type=MESH,
        )

    def cross_forward(part):
        return cross(part, halves.at[part, 1 - c], landed.at[part, c])

    def cross_back(part):
        return cross(2 + part, half_out.at[part], half_in.at[part, c])

    def along_x(part):
        forward.arrived(part)
        wide[...] = r_ref[part].astype(jnp.float32).reshape(2048, 128)
        for piece in range(2):
            for side in range(2):
                for block in range(2):
                    at = piece * 512 + side * 256 + block * 128
                    lines[:, pl.ds(at, 128)] = wide[
                        pl.ds(side * 1024 + piece * 2 + block, 256, stride=4), :
                    ].astype(jnp.bfloat16)
        both = dot(lines[...], forward_x[part]).astype(jnp.bfloat16)
        for half in range(2):
            halves[part, half] = both[:, half * GX : half * GX + GX]
        cross_forward(part).start()
        landed[part, c] = halves[part, c]

    def rounded_root(rows, across_table):
        return jnp.sqrt(scale * dot(rows, across_table)).astype(jnp.bfloat16).astype(jnp.float32)

    def amplitudes(part):
        near = jnp.concatenate([e_ref[:, part, row].reshape(GZ, PIX) for row in range(2)], axis=1)
        far = dot(mirror[...], near).astype(jnp.bfloat16)
        amplitude[part] = 0.5 * (
            rounded_root(near, across_x[part, 0]) + rounded_root(far, across_x[part, 1])
        )
        if part == 0:

            @pl.when(both_real)
            def _():
                amplitude_edge[...] = 0.5 * (
                    rounded_root(near, edge_across[...]) + rounded_root(far, edge_across[...])
                )

    def projection(real_z, imag_z, target):
        inverse = lax.rsqrt(real_z * real_z + imag_z * imag_z)
        factor = target * jnp.minimum(inverse, 1.0 / least_modulus)
        return (real_z * factor).astype(jnp.bfloat16), (imag_z * factor).astype(jnp.bfloat16)

    def along_z(part):
        cross_forward(part).wait()
        half_x = GX // 2
        for half in range(2):
            top = pl.ds(half * 256, 256)
            low = pl.ds(GZ + half * 256, 256)
            spectrum[top, :] = landed[part, half]
            if part == 0:

                @pl.when(both_real)
                def _():
                    at = pl.ds(half_x, 128)
                    first_lane = lax.broadcasted_iota(jnp.int32, (256, 128), 1) == 0
                    mixed = spectrum[top, at].astype(jnp.float32)
                    edge = jnp.where(first_lane, mixed, 0.0)
                    spectrum[top, at] = (mixed - edge).astype(jnp.bfloat16)
                    zero = jnp.zeros((256, 128), jnp.bfloat16)
                    edges[top, :] = jnp.concatenate([edge.astype(jnp.bfloat16), zero], axis=1)
                    edges[low, :] = jnp.concatenate([zero, (-edge).astype(jnp.bfloat16)], axis=1)

            spectrum[low, pl.ds(0, half_x)] = spectrum[top, pl.ds(half_x, half_x)]
            spectrum[low, pl.ds(half_x, half_x)] = -spectrum[top, pl.ds(0, half_x)]

        def block_of_planes(block, carry):
            at = pl.ds(pl.multiple_of(block * 128, 128), 128)
            low = pl.ds(pl.multiple_of(GZ + block * 128, 128), 128)
            weights = forward_z[at, :]
            total = dot(weights, spectrum[...])
            real, imag = projection(total[:, :half_x], total[:, half_x:], amplitude[part, at, :])
            projected[at, pl.ds(0, half_x)] = real
            projected[at, pl.ds(half_x, half_x)] = imag
            projected[low, pl.ds(0, half_x)] = -imag
            projected[low, pl.ds(half_x, half_x)] = real
            if part == 0:

                @pl.when(both_real)
                def _():
                    total = dot(weights, edges[...])
                    real, imag = projection(total[:, :128], total[:, 128:], amplitude_edge[at, :])
                    projected_edge[at, :] = real
                    projected_edge[low, :] = -imag

            return carry

        lax.fori_loop(0, 4, block_of_planes, 0)

        def inverse(half, target):
            target[...] = dot(back_z[half], projected[...]).astype(jnp.bfloat16)
            if part == 0:

                @pl.when(both_real)
                def _():
                    first_lane = lax.broadcasted_iota(jnp.int32, (256, 128), 1) == 0
                    edge = dot(back_z[half], projected_edge[...])
                    at = pl.ds(half_x, 128)
                    target[:, at] = jnp.where(
                        first_lane, edge, target[:, at].astype(jnp.float32)
                    ).astype(jnp.bfloat16)

        inverse(1 - c, half_out.at[part])
        cross_back(part).start()
        inverse(c, half_in.at[part, c])

    def back_x(part):
        cross_back(part).wait()
        for half in range(2):
            lines[:, pl.ds(half * GX, GX)] = half_in[part, half]
        for k in (1, 0):
            row = (y + k) % 2
            out = dot(lines[...], back_x_table[part, row])
            for block in range(4):
                stage[pl.ds(block, 256, stride=4), :] = out[:, block * 128 : block * 128 + 128]
            x_back[part, row] = stage[...].astype(jnp.bfloat16).reshape(4, 8, 2, 16, 128)
            back.start(part, k)

    def along_y(part):
        back.arrived(part)
        wide[...] = r_back[part].astype(jnp.float32).reshape(2048, 128)
        for plane in range(4):
            rows = [
                jnp.concatenate(
                    [
                        wide[pl.ds(plane * 4 + piece * 2 + side, 128, stride=16), :]
                        for side in range(2)
                    ],
                    axis=1,
                ).astype(jnp.bfloat16)
                for piece in range(2)
            ]
            out = dot(back_y[part], jnp.concatenate(rows, axis=0))
            if part:
                out = final[plane] + out
                previous = density[plane].astype(jnp.float32)
                final[plane] = jnp.where(support[plane] == 1, out, previous - feedback * out)
                pltpu.make_async_copy(final.at[plane], out_ref.at[plane], o_send.at[plane]).start()
            else:
                final[plane] = out

    along_x(0)
    forward.spread(1, 2)
    kept.wait()
    others = pltpu.make_async_remote_copy(
        src_ref=e_ref.at[pl.ds(0, 31)],
        dst_ref=e_ref.at[pl.ds(0, 31)],
        send_sem=e_send,
        recv_sem=e_recv,
        device_id=device(y, x, (z + 1) % 8, c),
        device_id_type=MESH,
    )
    others.wait_send()
    others.wait_recv()
    amplitudes(0)
    along_z(0)
    forward.spread(1, 3)
    forward.spread(1, 1)
    back_x(0)
    amplitudes(1)
    forward.spread(1, 0)
    along_x(1)
    along_z(1)
    back_x(1)
    back.spread(0, 1)
    back.spread(0, 0)
    along_y(0)
    back.spread(1, 1)
    back.spread(1, 0)
    along_y(1)
    forward.finish()
    back.finish()
    for plane in range(4):
        pltpu.make_async_copy(final.at[plane], out_ref.at[plane], o_send.at[plane]).wait()


def exchange_step(scale, density, orient, sharp, images, support):
    far = pl.BlockSpec(memory_space=pltpu.HBM)
    bfloat, single = jnp.bfloat16, jnp.float32
    one = pltpu.SemaphoreType.DMA
    buffers = [
        ((1, 64), jnp.int32),
        ((1, 64), single),
        (density.shape, bfloat),
        (LANDED_TILES, bfloat),
        ((32, 2, 2, 16, 128), bfloat),
        (FORWARD_TILES, bfloat),
        (FORWARD_TILES, bfloat),
        ((1024, 128), single),
        ((64 * 128, 128), single),
        ((16 * 128, 128), single),
        ((16, 128, 128), bfloat),
        ((5, 2, 128, 128), bfloat),
        ((2, 160, 128), single),
        ((8, 2, 32, 128), bfloat),
        ((8, 2, 32, 128), bfloat),
        ((1024, 128), single),
        ((16, 2, 2, 16, 128), bfloat),
        (BACK_TILES, bfloat),
        (BACK_TILES, bfloat),
        (LANDED_TILES, bfloat),
        ((2048, 128), single),
        ((256, 2 * GX), bfloat),
        ((2, 2, 256, GX), bfloat),
        ((2, 2, 256, GX), bfloat),
        ((2 * GZ, GX), bfloat),
        ((2 * GZ, 256), bfloat),
        ((2, GZ, GX // 2), single),
        ((GZ, 128), single),
        ((2 * GZ, GX), bfloat),
        ((2 * GZ, 128), bfloat),
        ((2, 256, GX), bfloat),
        ((2, 2, 256, GX), bfloat),
        (density.shape, single),
        (density.shape, jnp.int32),
    ]
    fill_count = len(TABLES) + len(BY_SET + BY_SET_AND_CORE)
    return pl.pallas_call(
        functools.partial(step_kernel, scale),
        out_shape=jax.ShapeDtypeStruct(density.shape, single),
        in_specs=[far] * (5 + len(TABLES)),
        out_specs=far,
        scratch_shapes=[pltpu.VMEM(held_shape(i, t), bfloat) for i, t in enumerate(TABLES)]
        + [pltpu.VMEM(*buffer) for buffer in buffers]
        + [one((4,)), one((fill_count,)), one, one((4,)), one((5,)), one((5,)), one, one, one, one, one, one]
        + [one((4,)), one((4,))]
        + exchange_sems(4)
        + exchange_sems(2),
        compiler_params=pltpu.CompilerParams(
            collective_id=1, has_side_effects=True, vmem_limit_bytes=63 << 20
        ),
    )(
        orient.reshape(1, -1),
        sharp.reshape(1, -1),
        density,
        images.reshape(-1, PIX),
        support,
        *TABLES,
    )


def body(images, orient, sharp, density, support):
    depth = density.shape[0]
    scale = depth / (images.shape[0] * lax.axis_size("img"))
    return exchange_step(scale, density, orient, sharp, images, support)


def solution(mesh):
    placed = (
        P(("img", "slab"), None, None),
        P(("img", "slab")),
        P(("img", "slab")),
        P("slab", None, "img"),
        P("slab", None, "img"),
    )
    return jax.shard_map(
        body, mesh=mesh, in_specs=placed, out_specs=P("slab", None, "img"), check_vma=False
    )
```

time: 129 us -> 84 us (0.65)
  the two profiles are of different devices: /device:TPU:105 before, /device:TPU:1 now
where the time goes in v6:
time: 84 us; the launch traced here: 83.9 us
  Pallas kernels  80.9 us (96%)
  local copies, waits for them, and re-layouts  3.05 us (4%)
    pallas_call x1, Pallas kernels, exchange_step(): pl.pallas_call(functools.partial(step_kernel, scale), out_shape=jax.Shape...  80.9 us
    unnamed x1, local copies, waits for them, and re-layouts  3.05 us

profile of v6, /device:TPU:1, one launch (start us, length us, event | category | flops | bytes accessed | tf_op | source)
XLA Modules:
  0.0 83.9 jit_solution(3315005147924740208)
XLA Ops:
  0.0 80.9 %shard_map.145 = f32[4,512,256]{2,1,0:T(8,128)} custom-call(s32[1,64]{1,0:T(1,128)} %bitcast.4, f32[1,64]{1,0:T(1,128)} %bitcast.5, bf16[4,512,256]{2,1,0:T(8,128)(2,1)} %density_in.1, f32[8192,128]{1,0:T(8,128)} %bitcast.3, s32[4,512,256]{2,1,0:T(8,128)} %support_in.1, bf16[2,2,128,512]{3,2,1,0:T(8,128)(2,1)} %constant.20.clone.rest_0_, ...), custom_call_target="tpu_custom_call" | custom-call | tf_op jit(solution)/shard_map/pallas_call | solution.py:750
  80.9 3.0 %copy.17 = f32[4,512,256]{2,1,0:T(8,128)} copy(f32[4,512,256]{2,1,0:T(8,128)} %shard_map.145) | data formatting | bytes 4194304

commit v7 on v6

--- a/solution.py
+++ b/solution.py
@@ -122,14 +122,15 @@
 FORWARD_Z = np.concatenate([t[K_ORDER][:, Z_ORDER] for t in (COS, SIN)], axis=1)
 BACK_Z = np.concatenate([COS[:, K_ORDER], SIN[:, K_ORDER]], axis=1).reshape(2, 256, 2 * GZ)
 MIRROR = bf(K_ORDER[None, :] == _mirror[K_ORDER][:, None])
-WINDOWS = np.zeros((2, 32, 2, 2, 16), np.float32)
-for _m in range(32):
-    for _r in range(16):
-        WINDOWS[:, _m, 0, 0, _r] = max(0.0, 1.0 - abs(_m / 4 + 3.625 - _r))
-        WINDOWS[:, _m, 1, 1, _r] = max(0.0, 1.0 - abs(11.625 - _m / 4 - _r))
-WINDOWS[1, 0, 1, 1, :] = 0.0
-WINDOWS[1, 0, 1, 1, 0:2] = (0.375, 0.625)
-WINDOWS = bf(WINDOWS.reshape(2, 64, 32))
+WINDOWS = np.zeros((2, 2, 32, 2, 48), np.float32)
+for _p in range(2):
+    for _m in range(32):
+        for _r in range(10):
+            WINDOWS[:, _p, _m, 0, 20 * _p + _r] = max(0.0, 1.0 - abs(_m / 4 + 0.625 - _r))
+            WINDOWS[:, _p, _m, 1, 20 * _p + 10 + _r] = max(0.0, 1.0 - abs(8.625 - _m / 4 - _r))
+    WINDOWS[1, _p, 0, 1, :] = 0.0
+    WINDOWS[1, _p, 0, 1, 40 + 2 * _p : 42 + 2 * _p] = (0.375, 0.625)
+WINDOWS = bf(WINDOWS.reshape(2, 128, 48))
 
 MESH = pl.DeviceIdType.MESH
 
@@ -319,7 +320,7 @@
     tables, rest = rest[:count], rest[count:]
     (
         orient, sharp, density, r_ref, e_ref,
-        x_ref, a_ref, stage, held, parts, sent, got, padded, g_ref, h_ref, made, whole_rows,
+        x_ref, a_ref, stage, held, sent, got, padded, g_ref, h_ref, made, whole_rows,
         x_back, a_back, r_back, wide, lines, halves, landed, spectrum, edges, amplitude, amplitude_edge,
         projected, projected_edge, half_out, half_in, final,
         support, d_load, t_load, load, o_send, c_send, c_recv, g_send, g_recv, g_own, e_send, e_recv, e_own,
@@ -386,7 +387,6 @@
     transform(0, other_half)
     entered()
     forward.start(0, 2)
-    forward.start(0, 3)
 
     near = orient[...] - slab * 4
     steps = lax.broadcasted_iota(jnp.int32, (16, 64), 0) - 4 - near
@@ -401,31 +401,43 @@
     mixing = jnp.where(jnp.abs(steps) <= 4, raw / total, 0.0)
     high = mixing.astype(jnp.bfloat16)
     low = (mixing - high.astype(jnp.float32)).astype(jnp.bfloat16)
-    factors = jnp.concatenate(
-        [
-            jnp.concatenate([high, high], axis=1),
-            jnp.concatenate([low, jnp.zeros_like(low)], axis=1),
-        ],
-        axis=0,
-    )
+    def iota(shape, axis):
+        return lax.broadcasted_iota(jnp.int32, shape, axis)
+
+    def within(at, group):
+        return jnp.where(jnp.logical_and(at >= group * 8, at < group * 8 + 8), 1.0, 0.0).astype(
+            jnp.bfloat16
+        )
+
+    by_plane = within(iota((96, 16), 0), iota((96, 16), 1))
+    by_snapshot = within(iota((64, 512), 1), iota((64, 512), 0))
+    agree = (iota((96, 512), 0) & 7) == (iota((96, 512), 1) & 7)
+
+    def widened(part):
+        rows = dot(by_plane, part).astype(jnp.bfloat16)
+        return jnp.where(agree, dot(rows, by_snapshot), 0.0).astype(jnp.bfloat16)
+
+    wide_high = widened(high)
+    wide_both = jnp.concatenate([wide_high, widened(low)], axis=0)
     fetch.wait()
 
     def mix(index, carry):
-        at = index * 2
+        at = pl.multiple_of(index * 16, 16)
         rows = jnp.concatenate(
-            [held[pl.ds(at, 64, stride=128), :], held[pl.ds(at + 1, 64, stride=128), :]], axis=1
+            [held[:, pl.ds(at + 8 * block, 8), :].reshape(512, 128) for block in range(2)], axis=1
         )
         upper = rows.astype(jnp.bfloat16)
         lower = (rows - upper.astype(jnp.float32)).astype(jnp.bfloat16)
-        out = dot(factors, jnp.concatenate([upper, lower], axis=0))
-        out = out[:16] + out[16:]
-        parts[pl.ds(at, 16, stride=128), :] = out[:, :128]
-        parts[pl.ds(at + 1, 16, stride=128), :] = out[:, 128:]
+        out = dot(wide_both, upper)
+        out = out[:96] + out[96:] + dot(wide_high, lower)
+        for plane in range(12):
+            own = out[plane * 8 : plane * 8 + 8]
+            sent[plane, pl.ds(at, 16), :] = jnp.concatenate(
+                [own[:, :128], own[:, 128:]], axis=0
+            ).astype(jnp.bfloat16)
         return carry
 
-    lax.fori_loop(0, 64, mix, 0, unroll=8)
-    sent[...] = parts[...].astype(jnp.bfloat16).reshape(16, 128, 128)
-
+    lax.fori_loop(0, 8, mix, 0, unroll=4)
 
     def gift(index, shift, turn):
         first = 4 + 4 * shift + 2 * ((image + turn) % 2)
@@ -441,11 +453,10 @@
     gifts = [gift(index, *move) for index, move in enumerate(moves)]
     for copy in gifts:
         copy.start()
+    forward.start(0, 3)
     transform(0, own_half)
     forward.start(0, 1)
-    forward.start(0, 0)
     transform(1, other_half)
-    transform(1, own_half)
     forward.spread(0, 2)
     for copy in gifts:
         copy.wait()
@@ -459,14 +470,15 @@
                 piece = jnp.where(jnp.logical_and(source >= 0, source < 128), piece, 0.0)
             own = own + piece
         padded[plane, pl.ds(16, 128), :] = own
-        for depth in range(8):
-            g_ref[depth, plane, pl.ds(0, 16), :] = padded[
-                plane, pl.ds(16 + 8 * depth - 4, 16), :
-            ].astype(jnp.bfloat16)
-            mirrored = padded[plane, pl.ds(16 + 116 - 8 * depth, 16), :]
-            if depth == 0:
-                mirrored = jnp.concatenate([own[63:65], mirrored[2:]], axis=0)
-            g_ref[depth, plane, pl.ds(16, 16), :] = mirrored.astype(jnp.bfloat16)
+    for depth in range(8):
+        rows = [
+            padded[plane, pl.ds(16 + first, 10), :]
+            for plane in range(2)
+            for first in (8 * depth - 1, 119 - 8 * depth)
+        ]
+        rows += [padded[plane, pl.ds(16 + 63, 2), :] for plane in range(2)]
+        rows.append(jnp.zeros((4, PIX), jnp.float32))
+        g_ref[depth] = jnp.concatenate(rows, axis=0).astype(jnp.bfloat16)
 
     def window(step):
         depth = (z + step) % 8
@@ -483,13 +495,14 @@
         window(step).start()
     stay = pltpu.make_async_copy(g_ref.at[z], h_ref.at[z], g_own)
     stay.start()
-    for k in ORDER:
-        forward.start(1, k)
+    forward.start(0, 0)
+    transform(1, own_half)
     forward.spread(0, 3)
+    forward.start(1, 2)
     for fill in fills[1:]:
         fill.wait()
     forward.spread(0, 1)
-    forward.spread(0, 0)
+    forward.start(1, 3)
     stay.wait()
     seven = pltpu.make_async_remote_copy(
         src_ref=g_ref.at[pl.ds(0, 7)],
@@ -502,22 +515,43 @@
     seven.wait_send()
     seven.wait_recv()
     weights = windows[jnp.where(z == 0, 1, 0)]
+    out = dot(weights, jnp.concatenate([h_ref[source] for source in range(8)], axis=1))
     for source in range(8):
         for plane in range(2):
-            made[pl.ds(source * 2 + plane, 64, stride=16), :] = dot(weights, h_ref[source, plane])
+            made[pl.ds(source * 2 + plane, 64, stride=16), :] = out[
+                plane * 64 : plane * 64 + 64, source * 128 : source * 128 + 128
+            ]
     whole_rows[...] = made[...].astype(jnp.bfloat16).reshape(16, 2, 2, 16, 128)
-    for d in range(1, 32):
-        row, column, core = (y + d // 8) % 4, (x + d // 2 % 4) % 4, (c + d) % 2
-        pltpu.make_async_remote_copy(
-            src_ref=whole_rows.at[row * 4 + column],
-            dst_ref=e_ref.at[m],
-            send_sem=e_send,
-            recv_sem=e_recv,
-            device_id=device(row, column, z, core),
+
+    def kept(part):
+        return pltpu.make_async_copy(whole_rows.at[y * 4 + x, part], e_ref.at[part, m], e_own.at[part])
+
+    def others(part):
+        piece = e_ref.at[part, pl.ds(0, 31)]
+        return pltpu.make_async_remote_copy(
+            src_ref=piece,
+            dst_ref=piece,
+            send_sem=e_send.at[part],
+            recv_sem=e_recv.at[part],
+            device_id=device(y, x, (z + 1) % 8, c),
             device_id_type=MESH,
-        ).start()
-    kept = pltpu.make_async_copy(whole_rows.at[y * 4 + x], e_ref.at[m], e_own)
-    kept.start()
+        )
+
+    for part in range(2):
+        for d in range(1, 32):
+            row, column, core = (y + d // 8) % 4, (x + d // 2 % 4) % 4, (c + d) % 2
+            pltpu.make_async_remote_copy(
+                src_ref=whole_rows.at[row * 4 + column, part],
+                dst_ref=e_ref.at[part, m],
+                send_sem=e_send.at[part],
+                recv_sem=e_recv.at[part],
+                device_id=device(row, column, z, core),
+                device_id_type=MESH,
+            ).start()
+        kept(part).start()
+    forward.spread(0, 0)
+    for k in (1, 0):
+        forward.start(1, k)
 
     def cross(index, source, target):
         return pltpu.make_async_remote_copy(
@@ -555,7 +589,10 @@
         return jnp.sqrt(scale * dot(rows, across_table)).astype(jnp.bfloat16).astype(jnp.float32)
 
     def amplitudes(part):
-        near = jnp.concatenate([e_ref[:, part, row].reshape(GZ, PIX) for row in range(2)], axis=1)
+        kept(part).wait()
+        others(part).wait_send()
+        others(part).wait_recv()
+        near = jnp.concatenate([e_ref[part, :, row].reshape(GZ, PIX) for row in range(2)], axis=1)
         far = dot(mirror[...], near).astype(jnp.bfloat16)
         amplitude[part] = 0.5 * (
             rounded_root(near, across_x[part, 0]) + rounded_root(far, across_x[part, 1])
@@ -671,20 +708,9 @@
             else:
                 final[plane] = out
 
+    amplitudes(0)
     along_x(0)
     forward.spread(1, 2)
-    kept.wait()
-    others = pltpu.make_async_remote_copy(
-        src_ref=e_ref.at[pl.ds(0, 31)],
-        dst_ref=e_ref.at[pl.ds(0, 31)],
-        send_sem=e_send,
-        recv_sem=e_recv,
-        device_id=device(y, x, (z + 1) % 8, c),
-        device_id_type=MESH,
-    )
-    others.wait_send()
-    others.wait_recv()
-    amplitudes(0)
     along_z(0)
     forward.spread(1, 3)
     forward.spread(1, 1)
@@ -715,17 +741,16 @@
         ((1, 64), single),
         (density.shape, bfloat),
         (LANDED_TILES, bfloat),
-        ((32, 2, 2, 16, 128), bfloat),
+        ((2, 32, 2, 16, 128), bfloat),
         (FORWARD_TILES, bfloat),
         (FORWARD_TILES, bfloat),
         ((1024, 128), single),
-        ((64 * 128, 128), single),
-        ((16 * 128, 128), single),
-        ((16, 128, 128), bfloat),
+        ((64, 128, 128), single),
+        ((12, 128, 128), bfloat),
         ((5, 2, 128, 128), bfloat),
         ((2, 160, 128), single),
-        ((8, 2, 32, 128), bfloat),
-        ((8, 2, 32, 128), bfloat),
+        ((8, 48, 128), bfloat),
+        ((8, 48, 128), bfloat),
         ((1024, 128), single),
         ((16, 2, 2, 16, 128), bfloat),
         (BACK_TILES, bfloat),
@@ -754,7 +779,7 @@
         out_specs=far,
         scratch_shapes=[pltpu.VMEM(held_shape(i, t), bfloat) for i, t in enumerate(TABLES)]
         + [pltpu.VMEM(*buffer) for buffer in buffers]
-        + [one((4,)), one((fill_count,)), one, one((4,)), one((5,)), one((5,)), one, one, one, one, one, one]
+        + [one((4,)), one((fill_count,)), one, one((4,)), one((5,)), one((5,)), one, one, one, one((2,)), one((2,)), one((2,))]
         + [one((4,)), one((4,))]
         + exchange_sems(4)
         + exchange_sems(2),
@@ -765,7 +790,7 @@
         orient.reshape(1, -1),
         sharp.reshape(1, -1),
         density,
-        images.reshape(-1, PIX),
+        images,
         support,
         *TABLES,
     )

time: 84 us -> 82.1 us (0.977)
  Pallas kernels: 80.9 us -> 78.9 us
    pallas_call x1, Pallas kernels: 80.9 us -> 78.9 us  [exchange_step(): pl.pallas_call(functools.partial(step_kernel, scale), out_shape=jax.Shape...]
where the time goes in v7:
time: 82.1 us; the launch traced here: 82 us
  Pallas kernels  78.9 us (96%)
  local copies, waits for them, and re-layouts  3.05 us (4%)
    pallas_call x1, Pallas kernels, exchange_step(): pl.pallas_call(functools.partial(step_kernel, scale), out_shape=jax.Shape...  78.9 us
    unnamed x1, local copies, waits for them, and re-layouts  3.05 us

profile of v7, /device:TPU:1, one launch (start us, length us, event | category | flops | bytes accessed | tf_op | source)
XLA Modules:
  0.0 82.0 jit_solution(11813966089962248099)
XLA Ops:
  0.0 78.9 %shard_map.145 = f32[4,512,256]{2,1,0:T(8,128)} custom-call(s32[1,64]{1,0:T(1,128)} %bitcast.2, f32[1,64]{1,0:T(1,128)} %bitcast.3, bf16[4,512,256]{2,1,0:T(8,128)(2,1)} %density_in.1, f32[64,128,128]{2,1,0:T(8,128)} %images.1, s32[4,512,256]{2,1,0:T(8,128)} %support_in.1, bf16[2,2,128,512]{3,2,1,0:T(8,128)(2,1)} %constant.20.clone.rest_0_, ...), custom_call_target="tpu_custom_call" | custom-call | tf_op jit(solution)/shard_map/pallas_call | solution.py:775
  79.0 3.0 %copy.17 = f32[4,512,256]{2,1,0:T(8,128)} copy(f32[4,512,256]{2,1,0:T(8,128)} %shard_map.145) | data formatting | bytes 4194304

commit v8 on v7

--- a/solution.py
+++ b/solution.py
@@ -322,6 +322,7 @@
         orient, sharp, density, r_ref, e_ref,
         x_ref, a_ref, stage, held, sent, got, padded, g_ref, h_ref, made, whole_rows,
         x_back, a_back, r_back, wide, lines, halves, landed, spectrum, edges, amplitude, amplitude_edge,
+        depth_sum, edge_sum,
         projected, projected_edge, half_out, half_in, final,
         support, d_load, t_load, load, o_send, c_send, c_recv, g_send, g_recv, g_own, e_send, e_recv, e_own,
         x_send, x_recv, *sems,
@@ -366,8 +367,6 @@
         fill.start()
     fetch.start()
     fills.append(pltpu.make_async_copy(support_in, support, d_load.at[3]))
-    for fill in fills[1:]:
-        fill.start()
     forward = Forward(x_ref, a_ref, r_ref, sems[:6])
     back = Back(x_back, a_back, r_back, sems[6:])
     for fill in first_fills:
@@ -420,6 +419,8 @@
     wide_high = widened(high)
     wide_both = jnp.concatenate([wide_high, widened(low)], axis=0)
     fetch.wait()
+    for fill in fills[1:]:
+        fill.start()
 
     def mix(index, carry):
         at = pl.multiple_of(index * 16, 16)
@@ -537,7 +538,7 @@
             device_id_type=MESH,
         )
 
-    for part in range(2):
+    def hand_out(part):
         for d in range(1, 32):
             row, column, core = (y + d // 8) % 4, (x + d // 2 % 4) % 4, (c + d) % 2
             pltpu.make_async_remote_copy(
@@ -549,9 +550,12 @@
                 device_id_type=MESH,
             ).start()
         kept(part).start()
+
+    hand_out(0)
     forward.spread(0, 0)
     for k in (1, 0):
         forward.start(1, k)
+    hand_out(1)
 
     def cross(index, source, target):
         return pltpu.make_async_remote_copy(
@@ -633,11 +637,24 @@
             spectrum[low, pl.ds(0, half_x)] = spectrum[top, pl.ds(half_x, half_x)]
             spectrum[low, pl.ds(half_x, half_x)] = -spectrum[top, pl.ds(0, half_x)]
 
+    def products(block, carry):
+        at = pl.ds(pl.multiple_of(block * 128, 128), 128)
+        weights = forward_z[at, :]
+        depth_sum[at, :] = dot(weights, spectrum[...])
+
+        @pl.when(both_real)
+        def _():
+            edge_sum[at, :] = dot(weights, edges[...])
+
+        return carry
+
+    def project(part):
+        half_x = GX // 2
+
         def block_of_planes(block, carry):
             at = pl.ds(pl.multiple_of(block * 128, 128), 128)
             low = pl.ds(pl.multiple_of(GZ + block * 128, 128), 128)
-            weights = forward_z[at, :]
-            total = dot(weights, spectrum[...])
+            total = dot(forward_z[at, :], spectrum[...]) if part else depth_sum[at, :]
             real, imag = projection(total[:, :half_x], total[:, half_x:], amplitude[part, at, :])
             projected[at, pl.ds(0, half_x)] = real
             projected[at, pl.ds(half_x, half_x)] = imag
@@ -647,7 +664,7 @@
 
                 @pl.when(both_real)
                 def _():
-                    total = dot(weights, edges[...])
+                    total = edge_sum[at, :]
                     real, imag = projection(total[:, :128], total[:, 128:], amplitude_edge[at, :])
                     projected_edge[at, :] = real
                     projected_edge[low, :] = -imag
@@ -708,17 +725,20 @@
             else:
                 final[plane] = out
 
+    along_x(0)
+    along_z(0)
+    lax.fori_loop(0, 4, products, 0)
+    forward.spread(1, 2)
     amplitudes(0)
-    along_x(0)
-    forward.spread(1, 2)
-    along_z(0)
+    project(0)
     forward.spread(1, 3)
+    back_x(0)
     forward.spread(1, 1)
-    back_x(0)
     amplitudes(1)
     forward.spread(1, 0)
     along_x(1)
     along_z(1)
+    project(1)
     back_x(1)
     back.spread(0, 1)
     back.spread(0, 0)
@@ -764,6 +784,8 @@
         ((2 * GZ, 256), bfloat),
         ((2, GZ, GX // 2), single),
         ((GZ, 128), single),
+        ((GZ, GX), single),
+        ((GZ, 256), single),
         ((2 * GZ, GX), bfloat),
         ((2 * GZ, 128), bfloat),
         ((2, 256, GX), bfloat),

time: 82.1 us -> 78.8 us (0.960)
  Pallas kernels: 78.9 us -> 75.6 us
    pallas_call x1, Pallas kernels: 78.9 us -> 75.6 us  [exchange_step(): pl.pallas_call(functools.partial(step_kernel, scale), out_shape=jax.Shape...]
where the time goes in v8:
time: 78.8 us; the launch traced here: 78.7 us
  Pallas kernels  75.6 us (96%)
  local copies, waits for them, and re-layouts  3.05 us (4%)
    pallas_call x1, Pallas kernels, exchange_step(): pl.pallas_call(functools.partial(step_kernel, scale), out_shape=jax.Shape...  75.6 us
    unnamed x1, local copies, waits for them, and re-layouts  3.05 us

profile of v8, /device:TPU:1, one launch (start us, length us, event | category | flops | bytes accessed | tf_op | source)
XLA Modules:
  0.0 78.7 jit_solution(8620710116333525524)
XLA Ops:
  0.0 75.6 %shard_map.145 = f32[4,512,256]{2,1,0:T(8,128)} custom-call(s32[1,64]{1,0:T(1,128)} %bitcast.2, f32[1,64]{1,0:T(1,128)} %bitcast.3, bf16[4,512,256]{2,1,0:T(8,128)(2,1)} %density_in.1, f32[64,128,128]{2,1,0:T(8,128)} %images.1, s32[4,512,256]{2,1,0:T(8,128)} %support_in.1, bf16[2,2,128,512]{3,2,1,0:T(8,128)(2,1)} %constant.20.clone.rest_0_, ...), custom_call_target="tpu_custom_call" | custom-call | tf_op jit(solution)/shard_map/pallas_call | solution.py:797
  75.6 3.0 %copy.17 = f32[4,512,256]{2,1,0:T(8,128)} copy(f32[4,512,256]{2,1,0:T(8,128)} %shard_map.145) | data formatting | bytes 4194304

commit v9 on v8

--- a/solution.py
+++ b/solution.py
@@ -734,8 +734,8 @@
     forward.spread(1, 3)
     back_x(0)
     forward.spread(1, 1)
+    forward.spread(1, 0)
     amplitudes(1)
-    forward.spread(1, 0)
     along_x(1)
     along_z(1)
     project(1)
@@ -818,10 +818,38 @@
     )
 
 
+def hand_over_kernel(source, target, sems):
+    copies = [
+        pltpu.make_async_copy(
+            source.at[plane, pl.ds(half * 256, 256)],
+            target.at[plane, pl.ds(half * 256, 256)],
+            sems.at[plane * 2 + half],
+        )
+        for plane in range(4)
+        for half in range(2)
+    ]
+    for copy in copies:
+        copy.start()
+    for copy in copies:
+        copy.wait()
+
+
+def hand_over(result):
+    far = pl.BlockSpec(memory_space=pltpu.HBM)
+    return pl.pallas_call(
+        hand_over_kernel,
+        out_shape=jax.ShapeDtypeStruct(result.shape, result.dtype),
+        in_specs=[far],
+        out_specs=far,
+        scratch_shapes=[pltpu.SemaphoreType.DMA((8,))],
+        compiler_params=pltpu.CompilerParams(vmem_limit_bytes=63 << 20),
+    )(result)
+
+
 def body(images, orient, sharp, density, support):
     depth = density.shape[0]
     scale = depth / (images.shape[0] * lax.axis_size("img"))
-    return exchange_step(scale, density, orient, sharp, images, support)
+    return hand_over(exchange_step(scale, density, orient, sharp, images, support))
 
 
 def solution(mesh):

time: 78.8 us -> 140 us (1.78)
  Pallas kernels: 75.6 us -> 140 us
  local copies, waits for them, and re-layouts: 3.05 us -> 0 us
    pallas_call x0 -> x1, Pallas kernels: none -> 64.7 us  [hand_over(): pl.pallas_call(hand_over_kernel, out_shape=jax.ShapeDtypeStruct(result.sh...]
    unnamed x1 -> x0, local copies, waits for them, and re-layouts: 3.05 us -> none
where the time goes in v9:
time: 140 us
  Pallas kernels  140 us (100%)
    pallas_call x1, Pallas kernels, exchange_step(): pl.pallas_call(functools.partial(step_kernel, scale), out_shape=jax.Shape...  75.6 us
    pallas_call x1, Pallas kernels, hand_over(): pl.pallas_call(hand_over_kernel, out_shape=jax.ShapeDtypeStruct(result.sh...  64.7 us

profile of v9, /device:TPU:1, one launch (start us, length us, event | category | flops | bytes accessed | tf_op | source)
XLA Modules:
  0.0 140.3 jit_solution(12321555282079170288)
XLA Ops:
  0.0 75.6 %shard_map.145.source = f32[4,512,256]{2,1,0:T(8,128)} custom-call(s32[1,64]{1,0:T(1,128)} %bitcast.2, f32[1,64]{1,0:T(1,128)} %bitcast.3, bf16[4,512,256]{2,1,0:T(8,128)(2,1)} %density_in.1, f32[64,128,128]{2,1,0:T(8,128)} %images.1, s32[4,512,256]{2,1,0:T(8,128)} %support_in.1, bf16[2,2,128,512]{3,2,1,0:T(8,128)(2,1)} %constant.20.clone.rest_0_, ...), custom_call_target="tpu_custom_call" | custom-call | tf_op jit(solution)/shard_map/pallas_call | solution.py:797
  75.6 64.7 %shard_map.146 = f32[4,512,256]{2,1,0:T(8,128)} custom-call(f32[4,512,256]{2,1,0:T(8,128)} %shard_map.145.source), custom_call_target="tpu_custom_call" | custom-call | tf_op jit(solution)/shard_map/pallas_call | solution.py:839
